TPU v7x, 1024 devices: a whole 4x4x32 slice. The times are simulated.
1024 devices in a mesh: hid: 64 (over z, core), row: 16 (over x, y).
Axes of the slice: x: 4, y: 4, z: 32, core: 2. Of those that a mesh axis runs over, the one named last changes fastest.
Arguments:
- inputs: bfloat16 [512, 12288], P('hid', 'row'), may hold values from -6 to 6
- out_grad: bfloat16 [512, 12288], P('hid', 'row'), may hold values from -6 to 6
- pre_act: bfloat16 [512, 24576], P(None, 'hid'), may hold values from -8 to 8
- w_in: bfloat16 [12288, 24576], P('row', 'hid'), may hold values from -0.15625 to 0.15625
- w_out: bfloat16 [24576, 12288], P('hid', 'row'), may hold values from -0.15625 to 0.15625
- pattern_in: int32 [96, 192], P('row', 'hid'), may hold values from 0 to 1, as said below
- pattern_out: int32 [192, 96], P('hid', 'row'), may hold values from 0 to 1, as said below
Outputs:
- in_grad: bfloat16 [512, 12288], P('hid', 'row')
- w_in_grad: bfloat16 [12288, 24576], P('row', 'hid')
- w_out_grad: bfloat16 [24576, 12288], P('hid', 'row')
Inputs may be any that keep to these rules, and one draw needn't show every extreme that they name: `pattern_in`: 1 marks a nonzero block; among the blocks that one index of row and one index of hid hold together, at least one is marked. `pattern_out`: 1 marks a nonzero block; among the blocks that one index of hid and one index of row hold together, at least one is marked.
All inputs are finite; a program needn't handle non-finite values.
Results may differ from a plain program's by a relative error of at most 0.0049.
Values may be sent and summed in bfloat16 or wider, within the bound.
No kernel may reach another device: no remote copies, remote signals or barrier semaphores. Data moves between devices by JAX's collectives and lax.ppermute only.
A program may use at most 32 MiB of HBM per device.

v0:
```python
import math

import jax
import jax.numpy as jnp
from jax import lax
from jax.sharding import PartitionSpec as P

BLOCK = 128


def widen(pattern, block):
    rows, cols = pattern.shape
    wide = jnp.broadcast_to(
        pattern.astype(jnp.bfloat16)[:, None, :, None], (rows, block, cols, block)
    )
    return wide.reshape(rows * block, cols * block)


def gelu_parts(pre_act):
    values = pre_act.astype(jnp.float32)
    return jax.jvp(lambda v: jax.nn.gelu(v, approximate=True), (values,), (jnp.ones_like(values),))


def shards(inputs, out_grad, pre_act, w_in, w_out, pattern_in, pattern_out):
    mask_in = widen(pattern_in, BLOCK)
    mask_out = widen(pattern_out, BLOCK)
    w_in_eff = w_in * mask_in
    w_out_eff = w_out * mask_out
    value, slope = gelu_parts(pre_act)
    act = value.astype(jnp.bfloat16)
    token_count = pre_act.shape[0]
    panel = lax.all_gather(out_grad, "hid", axis=0, tiled=True)
    new_rows = lax.dot_general(
        panel, w_out_eff, (((1,), (1,)), ((), ())), preferred_element_type=jnp.float32
    )
    out_weight = lax.dot_general(
        act, panel, (((0,), (0,)), ((), ())), preferred_element_type=jnp.float32
    )
    partial_grad, out_weight = (new_rows, out_weight)
    summed_share = lax.psum_scatter(partial_grad, "row", scatter_dimension=0, tiled=True)
    share_rows = summed_share.shape[0]
    slope_share = lax.dynamic_slice_in_dim(slope, lax.axis_index("row") * share_rows, share_rows, 0)
    delta_share = (summed_share * slope_share).astype(jnp.bfloat16)
    delta = lax.all_gather(delta_share, "row", axis=0, tiled=True)
    delta_rows = delta
    in_grad = lax.psum_scatter(
        lax.dot_general(
            delta_rows, w_in_eff, (((1,), (1,)), ((), ())), preferred_element_type=jnp.float32
        ),
        "hid",
        scatter_dimension=0,
        tiled=True,
    ).astype(jnp.bfloat16)
    delta_rows = delta
    in_weight = lax.dot_general(
        lax.all_gather(inputs, "hid", axis=0, tiled=True),
        delta_rows,
        (((0,), (0,)), ((), ())),
        preferred_element_type=jnp.float32,
    )
    scale = 1.0 / math.sqrt(token_count)
    w_in_grad = (in_weight * scale * mask_in.astype(jnp.float32)).astype(jnp.bfloat16)
    w_out_grad = (out_weight * scale * mask_out.astype(jnp.float32)).astype(jnp.bfloat16)
    return (in_grad, w_in_grad, w_out_grad)


def solution(mesh):
    placed = (
        P("hid", "row"),
        P("hid", "row"),
        P(None, "hid"),
        P("row", "hid"),
        P("hid", "row"),
        P("row", "hid"),
        P("hid", "row"),
    )
    return jax.shard_map(
        shards,
        mesh=mesh,
        in_specs=placed,
        out_specs=(P("hid", "row"), P("row", "hid"), P("hid", "row")),
        check_vma=False,
    )
```

profile of v0, /device:TPU:1, one launch (start us, length us, event | category | flops | bytes accessed | tf_op | source)
XLA Modules:
  0.0 424.4 jit_solution(5705301586866991782)
XLA Ops:
  7.2 0.0 reduce-scatter.7.cloned.1.call-start
  7.2 72.7 %all_gather.9 = bf16[512,768]{1,0:T(8,128)(2,1)S(1)} all-gather(bf16[8,768]{1,0:T(8,128)(2,1)} %param.8), channel_id=1, replica_groups=mesh['hid'=64,'row'=16] {'hid'}, dimensions={0}, use_global_device_ids=true | all-gather | bytes 798720 | tf_op jit(solution)/shard_map/all_gather | solution.py:32
  79.9 0.7 convert_element_type.30
  80.6 0.2 broadcast_in_dim.4
  80.7 0.5 convolution_bitcast_fusion
  81.3 1.2 copy.23
  82.4 0.0 reduce-scatter.7.cloned.1.call-update
  82.5 0.0 reduce-scatter.5.cloned.1.call-start
  82.5 0.9 convert_element_type.31
  83.5 0.0 copy-done.3
  83.5 0.3 copy.21
  83.8 1.7 multiply_multiply_fusion
  85.4 95.3 %reduce-scatter.7.cloned.1.call-done = f32[32,384]{1,0:T(8,128)} async-done(((f32[512,384]{1,0:T(8,128)}), f32[32,384]{1,0:T(8,128)}) %reduce-scatter.7.cloned.1.call-update) | async-done | bytes 49168 | tf_op jit(solution)/shard_map/reduce_scatter | solution.py:40
  180.7 0.9 fusion.13
  181.6 17.2 %all_gather.10 = bf16[512,384]{1,0:T(8,128)(2,1)S(1)} all-gather(bf16[32,384]{1,0:T(8,128)(2,1)S(1)} %fusion.13), channel_id=1, replica_groups=mesh['hid'=64,'row'=16] {'row'}, dimensions={0}, use_global_device_ids=true | all-gather | bytes 417792 | tf_op jit(solution)/shard_map/all_gather | solution.py:44
  198.9 0.2 broadcast_in_dim.5
  199.0 0.6 copy-done.1
  199.6 1.7 fusion.9
  201.4 1.4 fusion.4
  202.8 68.5 %all_gather.11 = bf16[512,768]{1,0:T(8,128)(2,1)S(1)} all-gather(bf16[8,768]{1,0:T(8,128)(2,1)S(1)} %copy-done.5), channel_id=1, replica_groups=mesh['hid'=64,'row'=16] {'hid'}, dimensions={0}, use_global_device_ids=true | all-gather | bytes 798720 | tf_op jit(solution)/shard_map/all_gather | solution.py:56
  271.4 0.5 fusion.3
  271.9 1.1 copy.22
  273.0 143.2 %reduce-scatter.5.cloned.1.call-done = f32[8,768]{1,0:T(8,128)} async-done(((f32[512,768]{1,0:T(8,128)}), f32[8,768]{1,0:T(8,128)}) %reduce-scatter.5.cloned.1.call-update) | async-done | bytes 24592 | tf_op jit(solution)/shard_map/reduce_scatter | solution.py:46
  416.2 1.3 convert_element_type.34
  (14 shorter events, 0.1 us)
Async XLA Ops:
  7.2 73.6 %copy-start.4 = (bf16[384,768]{1,0:T(8,128)(2,1)S(1)}, bf16[384,768]{1,0:T(8,128)(2,1)}, u32[]{:S(2)}) copy-start(bf16[384,768]{1,0:T(8,128)(2,1)} %param.11) | copy-start | bytes 1769476
  7.2 173.5 %reduce-scatter.7.cloned.1.call-start = ((), (), s32[]{:S(2)}) async-start(), calls=%async_computation.3 | async-start | bytes 835584 | tf_op jit(solution)/shard_map/reduce_scatter | solution.py:40
  81.3 1.3 copy-start
  82.4 1.1 copy-start.3
  82.5 333.7 %reduce-scatter.5.cloned.1.call-start = ((), (), s32[]{:S(2)}) async-start(), calls=%async_computation.2 | async-start | bytes 1597440 | tf_op jit(solution)/shard_map/reduce_scatter | solution.py:46
  82.5 1.3 copy-start.6
  198.9 0.7 copy-start.1
  201.4 1.5 copy-start.5
  201.4 70.0 %copy-start.2 = (bf16[512,384]{1,0:T(8,128)(2,1)S(1)}, bf16[512,384]{1,0:T(8,128)(2,1)}, u32[]{:S(2)}) copy-start(bf16[512,384]{1,0:T(8,128)(2,1)} %copy-done.1) | copy-start | bytes 1179652
Sparse Core Ops, SparseCore 0:
  82.6 98.0 reduce-scatter.6
  201.5 214.6 reduce-scatter.4
where the time goes:
time: 426 us; the launch traced here: 424 us
  waiting for transfers between devices  239 us (56%)
  blocking collectives  158 us (37%)
  between operations  14.2 us (3%)
  other arithmetic  5.54 us (1%)
    reduce_scatter x1, waiting for transfers between devices, shards(): lax.psum_scatter(lax.dot_general(delta_rows, w_in_eff, (((1,), (1,)), (()...  143 us
    reduce_scatter x1, waiting for transfers between devices, shards(): lax.psum_scatter(partial_grad, 'row', scatter_dimension=0, tiled=True)  95.3 us
    all_gather x1, blocking collectives, shards(): panel = lax.all_gather(out_grad, 'hid', axis=0, tiled=True)  72.7 us
    all_gather x1, blocking collectives, shards(): lax.all_gather(inputs, 'hid', axis=0, tiled=True)  68.5 us
    all_gather x1, blocking collectives, shards(): delta = lax.all_gather(delta_share, 'row', axis=0, tiled=True)  17.2 us
  transfers between devices with their start and end apart: 2, of which 2 were waited for; matrix products, arithmetic and copies ran while one was open for 1% of the time, Pallas kernels for 0%

commit v1 on v0

v1 whole, which is shorter than its diff:
```python
import math

import jax
import jax.numpy as jnp
from jax import lax
from jax.sharding import PartitionSpec as P

BLOCK = 128
NEAR = 4


def widen(pattern, block):
    rows, cols = pattern.shape
    wide = jnp.broadcast_to(
        pattern.astype(jnp.bfloat16)[:, None, :, None], (rows, block, cols, block)
    )
    return wide.reshape(rows * block, cols * block)


def gelu_parts(pre_act):
    values = pre_act.astype(jnp.float32)
    return jax.jvp(lambda v: jax.nn.gelu(v, approximate=True), (values,), (jnp.ones_like(values),))


def groups(n_hid):
    far = n_hid // 2 // NEAR
    at = lambda k, n, c: 2 * (NEAR * k + n) + c
    return (
        [[at(k, n, c) for k in range(far)] for n in range(NEAR) for c in range(2)],
        [[at(k, n, c) for n in range(NEAR)] for k in range(far) for c in range(2)],
        [[at(k, n, c) for c in range(2)] for k in range(far) for n in range(NEAR)],
    )


def swap(x, axis, within=None):
    return lax.all_to_all(x, axis, 0, 0, tiled=True, axis_index_groups=within)


def spread(x, axis, count, within=None):
    many = jnp.broadcast_to(x[None], (count,) + x.shape).reshape((count * x.shape[0],) + x.shape[1:])
    return swap(many, axis, within)


def shards(n_hid, n_row, inputs, out_grad, pre_act, w_in, w_out, pattern_in, pattern_out):
    far_groups, near_groups, pairs = groups(n_hid)
    far = n_hid // 2 // NEAR
    tokens, width = pre_act.shape
    own = out_grad.shape[0]
    core = lax.axis_index("hid") % 2

    def gather(x):
        x = spread(x, "hid", far, far_groups)
        x = spread(x, "hid", NEAR, near_groups)
        return lax.all_gather(x, "hid", axis=0, tiled=True, axis_index_groups=pairs)

    mask_in = widen(pattern_in, BLOCK)
    mask_out = widen(pattern_out, BLOCK)
    w_in_eff = w_in * mask_in
    w_out_eff = w_out * mask_out
    ordered = pre_act.reshape(far, NEAR, 2, own, width).transpose(2, 1, 0, 3, 4).reshape(tokens, width)
    value, slope = gelu_parts(ordered)
    act = value.astype(jnp.bfloat16)

    panel = gather(out_grad)
    partial = lax.dot_general(
        panel, w_out_eff, (((1,), (1,)), ((), ())), preferred_element_type=jnp.float32
    )
    share = tokens // n_row
    summed = jnp.sum(swap(partial, "row").reshape(n_row, share, width), axis=0)
    slope_share = lax.dynamic_slice_in_dim(slope, lax.axis_index("row") * share, share, 0)
    delta = spread((summed * slope_share).astype(jnp.bfloat16), "row", n_row)

    back = lax.dot_general(
        delta, w_in_eff, (((1,), (1,)), ((), ())), preferred_element_type=jnp.float32
    )
    features = back.shape[1]
    back = back.reshape(2, tokens // 2, features)
    mine = lax.dynamic_index_in_dim(back, core, 0, keepdims=False)
    other = lax.dynamic_index_in_dim(back, 1 - core, 0, keepdims=False)
    got = lax.ppermute(other, "hid", [(i, i ^ 1) for i in range(n_hid)])
    back = (mine + got).astype(jnp.bfloat16)
    back = swap(back, "hid", near_groups).astype(jnp.float32)
    back = jnp.sum(back.reshape(NEAR, far * own, features), axis=0).astype(jnp.bfloat16)
    back = swap(back, "hid", far_groups).astype(jnp.float32)
    in_grad = jnp.sum(back.reshape(far, own, features), axis=0).astype(jnp.bfloat16)

    in_weight = lax.dot_general(
        gather(inputs), delta, (((0,), (0,)), ((), ())), preferred_element_type=jnp.float32
    )
    out_weight = lax.dot_general(
        act, panel, (((0,), (0,)), ((), ())), preferred_element_type=jnp.float32
    )
    scale = 1.0 / math.sqrt(tokens)
    w_in_grad = (in_weight * scale * mask_in.astype(jnp.float32)).astype(jnp.bfloat16)
    w_out_grad = (out_weight * scale * mask_out.astype(jnp.float32)).astype(jnp.bfloat16)
    return (in_grad, w_in_grad, w_out_grad)


def solution(mesh):
    placed = (
        P("hid", "row"),
        P("hid", "row"),
        P(None, "hid"),
        P("row", "hid"),
        P("hid", "row"),
        P("row", "hid"),
        P("hid", "row"),
    )
    return jax.shard_map(
        lambda *blocks: shards(mesh.shape["hid"], mesh.shape["row"], *blocks),
        mesh=mesh,
        in_specs=placed,
        out_specs=(P("hid", "row"), P("row", "hid"), P("hid", "row")),
        check_vma=False,
    )
```

time: 426 us -> 213 us (0.50)
  waiting for transfers between devices: 239 us -> 69.8 us
  blocking collectives: 158 us -> 77.1 us
  starting transfers between devices: 0.08 us -> 40 us
  between operations: 14.2 us -> 0.83 us
  local copies, waits for them, and re-layouts: 3.45 us -> 12.1 us
    reduce_scatter x2 -> x0, waiting for transfers between devices: 239 us -> none  [the longest x1 143 us: shards(): lax.psum_scatter(lax.dot_general(delta_rows, w_in_eff, (((1,), (1,)), (()...]
    all_gather x3 -> x2, blocking collectives: 158 us -> 12.2 us  [gather(): return lax.all_gather(x, 'hid', axis=0, tiled=True, axis_index_groups=pairs)]
    all_to_all x0 -> x6, waiting for transfers between devices: none -> 69.8 us  [swap(): return lax.all_to_all(x, axis, 0, 0, tiled=True, axis_index_groups=within)]
    all_to_all x0 -> x2, blocking collectives: none -> 65 us  [swap(): return lax.all_to_all(x, axis, 0, 0, tiled=True, axis_index_groups=within)]
    all_to_all x0 -> x6, starting transfers between devices: none -> 35 us  [swap(): return lax.all_to_all(x, axis, 0, 0, tiled=True, axis_index_groups=within)]
    ppermute x0 -> x1, starting transfers between devices: none -> 5.04 us  [shards(): got = lax.ppermute(other, 'hid', [(i, i ^ 1) for i in range(n_hid)])]
    broadcast_in_dim x0 -> x5, local copies, waits for them, and re-layouts: none -> 4.58 us  [spread(): jnp.broadcast_to(x[None], (count,) + x.shape)]
  transfers between devices with their start and end apart: 2 -> 7, of which waited for: 2 -> 6; matrix products, arithmetic and copies ran while one was open for 1% -> 5% of each run, Pallas kernels for 0% -> 0%
where the time goes in v1:
time: 213 us; the launch traced here: 211 us
  blocking collectives  77.1 us (36%)
  waiting for transfers between devices  69.8 us (33%)
  starting transfers between devices  40 us (19%)
  local copies, waits for them, and re-layouts  12.1 us (6%)
  other arithmetic  7.84 us (4%)
  matrix products  2.92 us (1%)
    all_to_all x6, waiting for transfers between devices, swap(): return lax.all_to_all(x, axis, 0, 0, tiled=True, axis_index_groups=within)  69.8 us
    all_to_all x2, blocking collectives, swap(): return lax.all_to_all(x, axis, 0, 0, tiled=True, axis_index_groups=within)  65 us
    all_to_all x6, starting transfers between devices, swap(): return lax.all_to_all(x, axis, 0, 0, tiled=True, axis_index_groups=within)  35 us
    all_gather x2, blocking collectives, gather(): return lax.all_gather(x, 'hid', axis=0, tiled=True, axis_index_groups=pairs)  12.2 us
    ppermute x1, starting transfers between devices, shards(): got = lax.ppermute(other, 'hid', [(i, i ^ 1) for i in range(n_hid)])  5.04 us
    unnamed x26, local copies, waits for them, and re-layouts  4.99 us
    broadcast_in_dim x5, local copies, waits for them, and re-layouts, spread(): jnp.broadcast_to(x[None], (count,) + x.shape)  4.58 us
  transfers between devices with their start and end apart: 7, of which 6 were waited for; matrix products, arithmetic and copies ran while one was open for 5% of the time, Pallas kernels for 0%

profile of v1, /device:TPU:1, one launch (start us, length us, event | category | flops | bytes accessed | tf_op | source)
XLA Modules:
  0.0 210.6 jit_solution(13654290589248892164)
XLA Ops:
  1.4 51.2 %all_to_all.63 = bf16[8,8,768]{2,1,0:T(8,128)(2,1)S(1)} all-to-all(bf16[8,8,768]{2,1,0:T(8,128)(2,1)S(1)} %broadcast_in_dim.19), channel_id=1, replica_groups={{0,128,256,384,512,640,768,896},{16,144,272,400,528,656,784,912},{32,16..., dimensions={0} | all-to-all | bytes 196608 | tf_op jit(solution)/shard_map/all_to_all | solution.py:36
  53.4 6.1 %all-to-all-start.1 = ((bf16[4,64,768]{2,1,0:T(8,128)(2,1)}), bf16[4,64,768]{2,1,0:T(8,128)(2,1)S(1)}, u32[]{:S(2)}, u32[]{:S(2)}) async-start(bf16[4,64,768]{2,1,0:T(8,128)(2,1)} %broadcast_in_dim.21), calls=%async_computation.1 | async-start | bytes 786432 | tf_op jit(solution)/shard_map/all_to_all | solution.py:36
  59.5 7.7 %all-to-all-done.1 = bf16[4,64,768]{2,1,0:T(8,128)(2,1)S(1)} async-done(((bf16[4,64,768]{2,1,0:T(8,128)(2,1)}), bf16[4,64,768]{2,1,0:T(8,128)(2,1)S(1)}, u32[]{:S(2)}, u32[]{:S(2)}) %all-to-all-start.1) | async-done | bytes 393248 | tf_op jit(solution)/shard_map/all_to_all | solution.py:36
  67.2 6.9 %all_gather.6 = bf16[512,768]{1,0:T(8,128)(2,1)S(1)} all-gather(bf16[256,768]{1,0:T(8,128)(2,1)S(1)} %bitcast.66), channel_id=1, replica_groups={{0,16},{32,48},{64,80},{96,112},{128,144},{160,176},{192,208},{224,240}..., dimensions={0}, use_global_device_ids=true | all-gather | bytes 1179648 | tf_op jit(solution)/shard_map/all_gather | solution.py:54
  76.8 6.9 %all-to-all-start.2 = ((f32[16,32,384]{2,1,0:T(8,128)}), f32[16,32,384]{2,1,0:T(8,128)S(1)}, u32[]{:S(2)}, u32[]{:S(2)}) async-start(f32[16,32,384]{2,1,0:T(8,128)} %bitcast.3), calls=%async_computation.2 | async-start | bytes 1572864 | tf_op jit(solution)/shard_map/all_to_all | solution.py:36
  83.9 1.6 multiply_multiply_fusion
  85.5 10.9 %all-to-all-done.2 = f32[16,32,384]{2,1,0:T(8,128)S(1)} async-done(((f32[16,32,384]{2,1,0:T(8,128)}), f32[16,32,384]{2,1,0:T(8,128)S(1)}, u32[]{:S(2)}, u32[]{:S(2)}) %all-to-all-start.2) | async-done | bytes 786464 | tf_op jit(solution)/shard_map/all_to_all | solution.py:36
  98.2 4.3 %all-to-all-start.3 = ((bf16[16,32,384]{2,1,0:T(8,128)(2,1)}), bf16[16,32,384]{2,1,0:T(8,128)(2,1)S(1)}, u32[]{:S(2)}, u32[]{:S(2)}) async-start(bf16[16,32,384]{2,1,0:T(8,128)(2,1)} %broadcast_in_dim.22), calls=%async_computation.3 | async-start | bytes 786432 | tf_op jit(solution)/shard_map/all_to_all | solution.py:36
  102.5 2.1 %copy.24 = bf16[768,384]{0,1:T(8,128)(2,1)} copy(bf16[768,384]{1,0:T(8,128)(2,1)} %param.10) | data formatting | bytes 1179648 | tf_op args[3]
  104.6 5.8 %all-to-all-done.3 = bf16[16,32,384]{2,1,0:T(8,128)(2,1)S(1)} async-done(((bf16[16,32,384]{2,1,0:T(8,128)(2,1)}), bf16[16,32,384]{2,1,0:T(8,128)(2,1)S(1)}, u32[]{:S(2)}, u32[]{:S(2)}) %all-to-all-start.3) | async-done | bytes 393248 | tf_op jit(solution)/shard_map/all_to_all | solution.py:36
  113.1 5.0 %collective-permute-start = (f32[256,768]{1,0:T(8,128)}, f32[256,768]{1,0:T(8,128)}, u32[]{:S(2)}, u32[]{:S(2)}) collective-permute-start(f32[256,768]{1,0:T(8,128)} %dynamic-slice_bitcast_fusion), channel_id=1, source_target_pairs={{0,16},{16,0},{32,48},{48,32},{64,80},{80,64},{96,112},{112,96},{1... | collective-permute-start | bytes 2359304 | tf_op jit(solution)/shard_map/ppermute | solution.py:80
  118.8 4.5 %all-to-all-start.6 = ((bf16[8,8,768]{2,1,0:T(8,128)(2,1)}), bf16[8,8,768]{2,1,0:T(8,128)(2,1)}, u32[]{:S(2)}, u32[]{:S(2)}) async-start(bf16[8,8,768]{2,1,0:T(8,128)(2,1)} %broadcast_in_dim.24), calls=%async_computation.6 | async-start | bytes 196608 | tf_op jit(solution)/shard_map/all_to_all | solution.py:36
  123.2 2.0 fusion.9
  125.2 23.2 %all-to-all-done.6 = bf16[8,8,768]{2,1,0:T(8,128)(2,1)} async-done(((bf16[8,8,768]{2,1,0:T(8,128)(2,1)}), bf16[8,8,768]{2,1,0:T(8,128)(2,1)}, u32[]{:S(2)}, u32[]{:S(2)}) %all-to-all-start.6) | async-done | bytes 98336 | tf_op jit(solution)/shard_map/all_to_all | solution.py:36
  148.4 13.7 %all_to_all.64 = bf16[4,64,768]{2,1,0:T(8,128)(2,1)} all-to-all(bf16[4,64,768]{2,1,0:T(8,128)(2,1)} %bitcast.67), channel_id=1, replica_groups={{0,32,64,96},{16,48,80,112},{128,160,192,224},{144,176,208,240},{256,28..., dimensions={0} | all-to-all | bytes 786432 | tf_op jit(solution)/shard_map/all_to_all | solution.py:36
  162.2 1.7 broadcast_in_dim.26
  163.8 4.2 %all-to-all-start.7 = ((bf16[4,64,768]{2,1,0:T(8,128)(2,1)}), bf16[4,64,768]{2,1,0:T(8,128)(2,1)}, u32[]{:S(2)}, u32[]{:S(2)}) async-start(bf16[4,64,768]{2,1,0:T(8,128)(2,1)} %broadcast_in_dim.26), calls=%async_computation.7 | async-start | bytes 786432 | tf_op jit(solution)/shard_map/all_to_all | solution.py:36
  168.1 1.7 reduce_sum.34
  169.8 6.1 %all-to-all-done.7 = bf16[4,64,768]{2,1,0:T(8,128)(2,1)} async-done(((bf16[4,64,768]{2,1,0:T(8,128)(2,1)}), bf16[4,64,768]{2,1,0:T(8,128)(2,1)}, u32[]{:S(2)}, u32[]{:S(2)}) %all-to-all-start.7) | async-done | bytes 393248 | tf_op jit(solution)/shard_map/all_to_all | solution.py:36
  175.9 9.0 %all-to-all-start.5 = ((bf16[8,8,768]{2,1,0:T(8,128)(2,1)}), bf16[8,8,768]{2,1,0:T(8,128)(2,1)}, u32[]{:S(2)}, u32[]{:S(2)}) async-start(bf16[8,8,768]{2,1,0:T(8,128)(2,1)} %bitcast.68), calls=%async_computation.5 | async-start | bytes 196608 | tf_op jit(solution)/shard_map/all_to_all | solution.py:36
  184.9 5.3 %all_gather.7 = bf16[512,768]{1,0:T(8,128)(2,1)S(1)} all-gather(bf16[256,768]{1,0:T(8,128)(2,1)} %bitcast.15), channel_id=1, replica_groups={{0,16},{32,48},{64,80},{96,112},{128,144},{160,176},{192,208},{224,240}..., dimensions={0}, use_global_device_ids=true | all-gather | bytes 1179648 | tf_op jit(solution)/shard_map/all_gather | solution.py:54
  190.2 1.3 fusion.4
  193.1 16.0 %all-to-all-done.5 = bf16[8,8,768]{2,1,0:T(8,128)(2,1)} async-done(((bf16[8,8,768]{2,1,0:T(8,128)(2,1)}), bf16[8,8,768]{2,1,0:T(8,128)(2,1)}, u32[]{:S(2)}, u32[]{:S(2)}) %all-to-all-start.5) | async-done | bytes 98336 | tf_op jit(solution)/shard_map/all_to_all | solution.py:36
  209.1 1.5 reduce_sum.35
  (43 shorter events, 10.9 us)
Async XLA Ops:
  0.6 58.8 %copy-start.10 = (s32[3,6]{1,0:T(4,128)S(1)}, s32[3,6]{1,0:T(4,128)}, u32[]{:S(2)}) copy-start(s32[3,6]{1,0:T(4,128)} %param.13) | copy-start | bytes 220
  53.4 13.8 %all-to-all-start.1 = ((bf16[4,64,768]{2,1,0:T(8,128)(2,1)}), bf16[4,64,768]{2,1,0:T(8,128)(2,1)S(1)}, u32[]{:S(2)}, u32[]{:S(2)}) async-start(bf16[4,64,768]{2,1,0:T(8,128)(2,1)} %broadcast_in_dim.21), calls=%async_computation.1 | async-start | bytes 786432 | tf_op jit(solution)/shard_map/all_to_all | solution.py:36
  59.5 15.7 %copy-start.7 = (bf16[384,768]{1,0:T(8,128)(2,1)S(1)}, bf16[384,768]{1,0:T(8,128)(2,1)}, u32[]{:S(2)}) copy-start(bf16[384,768]{1,0:T(8,128)(2,1)} %param.11) | copy-start | bytes 1769476
  74.3 0.9 copy-start
  76.8 6.9 %copy-start.8 = (bf16[512,384]{1,0:T(8,128)(2,1)S(1)}, bf16[512,384]{1,0:T(8,128)(2,1)}, u32[]{:S(2)}) copy-start(bf16[512,384]{1,0:T(8,128)(2,1)} %param.9) | copy-start | bytes 1179652
  76.8 19.6 %all-to-all-start.2 = ((f32[16,32,384]{2,1,0:T(8,128)}), f32[16,32,384]{2,1,0:T(8,128)S(1)}, u32[]{:S(2)}, u32[]{:S(2)}) async-start(f32[16,32,384]{2,1,0:T(8,128)} %bitcast.3), calls=%async_computation.2 | async-start | bytes 1572864 | tf_op jit(solution)/shard_map/all_to_all | solution.py:36
  85.5 12.7 %copy-start.2 = (f32[512,384]{1,0:T(8,128)}, f32[512,384]{1,0:T(8,128)S(1)}, u32[]{:S(2)}) copy-start(f32[512,384]{1,0:T(8,128)S(1)} %get-tuple-element.18) | copy-start | bytes 2359300
  85.5 17.0 %copy-start.11 = (s32[6,3]{0,1:T(4,128)S(1)}, s32[6,3]{0,1:T(4,128)}, u32[]{:S(2)}) copy-start(s32[6,3]{0,1:T(4,128)} %param.12) | copy-start | bytes 220
  98.2 12.3 %all-to-all-start.3 = ((bf16[16,32,384]{2,1,0:T(8,128)(2,1)}), bf16[16,32,384]{2,1,0:T(8,128)(2,1)S(1)}, u32[]{:S(2)}, u32[]{:S(2)}) async-start(bf16[16,32,384]{2,1,0:T(8,128)(2,1)} %broadcast_in_dim.22), calls=%async_computation.3 | async-start | bytes 786432 | tf_op jit(solution)/shard_map/all_to_all | solution.py:36
  110.4 1.1 copy-start.6
  110.6 1.5 copy-start.4
  112.1 6.0 %copy-start.9 = (bf16[8,768]{1,0:T(8,128)(2,1)S(1)}, bf16[8,768]{1,0:T(8,128)(2,1)}, u32[]{:S(2)}) copy-start(bf16[8,768]{1,0:T(8,128)(2,1)} %param.7) | copy-start | bytes 36868
  113.1 10.2 %collective-permute-start = (f32[256,768]{1,0:T(8,128)}, f32[256,768]{1,0:T(8,128)}, u32[]{:S(2)}, u32[]{:S(2)}) collective-permute-start(f32[256,768]{1,0:T(8,128)} %dynamic-slice_bitcast_fusion), channel_id=1, source_target_pairs={{0,16},{16,0},{32,48},{48,32},{64,80},{80,64},{96,112},{112,96},{1... | collective-permute-start | bytes 2359304 | tf_op jit(solution)/shard_map/ppermute | solution.py:80
  118.8 29.7 %all-to-all-start.6 = ((bf16[8,8,768]{2,1,0:T(8,128)(2,1)}), bf16[8,8,768]{2,1,0:T(8,128)(2,1)}, u32[]{:S(2)}, u32[]{:S(2)}) async-start(bf16[8,8,768]{2,1,0:T(8,128)(2,1)} %broadcast_in_dim.24), calls=%async_computation.6 | async-start | bytes 196608 | tf_op jit(solution)/shard_map/all_to_all | solution.py:36
  163.8 26.4 %copy-start.1 = (bf16[3,128,6,128]{3,2,1,0:T(8,128)(2,1)S(1)}, bf16[3,128,6,128]{3,2,1,0:T(8,128)(2,1)}, u32[]{:S(2)}) copy-start(bf16[3,128,6,128]{3,2,1,0:T(8,128)(2,1)} %copy-done) | copy-start | bytes 1769476
  163.8 26.4 %copy-start.3 = (f32[512,384]{1,0:T(8,128)S(1)}, f32[512,384]{1,0:T(8,128)}, u32[]{:S(2)}) copy-start(f32[512,384]{1,0:T(8,128)} %copy-done.2) | copy-start | bytes 2359300
  163.8 12.0 %all-to-all-start.7 = ((bf16[4,64,768]{2,1,0:T(8,128)(2,1)}), bf16[4,64,768]{2,1,0:T(8,128)(2,1)}, u32[]{:S(2)}, u32[]{:S(2)}) async-start(bf16[4,64,768]{2,1,0:T(8,128)(2,1)} %broadcast_in_dim.26), calls=%async_computation.7 | async-start | bytes 786432 | tf_op jit(solution)/shard_map/all_to_all | solution.py:36
  175.9 33.2 %all-to-all-start.5 = ((bf16[8,8,768]{2,1,0:T(8,128)(2,1)}), bf16[8,8,768]{2,1,0:T(8,128)(2,1)}, u32[]{:S(2)}, u32[]{:S(2)}) async-start(bf16[8,8,768]{2,1,0:T(8,128)(2,1)} %bitcast.68), calls=%async_computation.5 | async-start | bytes 196608 | tf_op jit(solution)/shard_map/all_to_all | solution.py:36
  190.2 1.3 copy-start.5

commit v2 on v1

v2 whole, which is shorter than its diff:
```python
import math

import jax
import jax.numpy as jnp
from jax import lax
from jax.experimental import pallas as pl
from jax.experimental.pallas import tpu as pltpu
from jax.sharding import PartitionSpec as P

BLOCK = 128
NEAR = 4
CONTRACT_LAST = (((1,), (1,)), ((), ()))
CONTRACT_FIRST = (((0,), (0,)), ((), ()))


def widen(pattern, block):
    rows, cols = pattern.shape
    wide = jnp.broadcast_to(
        pattern.astype(jnp.bfloat16)[:, None, :, None], (rows, block, cols, block)
    )
    return wide.reshape(rows * block, cols * block)


def gelu_parts(pre_act):
    values = pre_act.astype(jnp.float32)
    return jax.jvp(lambda v: jax.nn.gelu(v, approximate=True), (values,), (jnp.ones_like(values),))


def groups(n_hid):
    far = n_hid // 2 // NEAR
    at = lambda k, n, c: 2 * (NEAR * k + n) + c
    return (
        [[at(k, n, c) for k in range(far)] for n in range(NEAR) for c in range(2)],
        [[at(k, n, c) for n in range(NEAR)] for k in range(far) for c in range(2)],
    )


def swap(x, axis, within=None):
    return lax.all_to_all(x, axis, 0, 0, axis_index_groups=within, tiled=True)


def local(body, out_shape, flops, *args):
    size = sum(a.size * a.dtype.itemsize for a in (*args, out_shape))
    return pl.pallas_call(
        body,
        out_shape=out_shape,
        in_specs=[pl.BlockSpec(memory_space=pltpu.VMEM)] * len(args),
        out_specs=pl.BlockSpec(memory_space=pltpu.VMEM),
        compiler_params=pltpu.CompilerParams(vmem_limit_bytes=24 * 2**20),
        cost_estimate=pl.CostEstimate(flops=flops, bytes_accessed=size, transcendentals=0),
    )(*args)


def act_grad_body(rows_ref, own_ref, got_ref, out_ref):
    width, features = own_ref.shape
    rows = rows_ref[:, :features]
    out_ref[:, :width] = lax.dot_general(
        rows, own_ref[...], CONTRACT_LAST, preferred_element_type=jnp.float32
    )
    out_ref[:, width:] = lax.dot_general(
        rows, got_ref[...], CONTRACT_LAST, preferred_element_type=jnp.float32
    )


def delta_body(parts_ref, slope_ref, out_ref):
    total = parts_ref[0]
    for part in range(1, parts_ref.shape[0]):
        total = total + parts_ref[part]
    delta = (total * slope_ref[...]).astype(out_ref.dtype)
    for copy in range(out_ref.shape[0]):
        out_ref[copy] = delta


def in_grad_body(delta_ref, own_ref, got_ref, out_ref):
    width = own_ref.shape[1]
    total = lax.dot_general(
        delta_ref[:, :width], own_ref[...], CONTRACT_LAST, preferred_element_type=jnp.float32
    )
    total = total + lax.dot_general(
        delta_ref[:, width:], got_ref[...], CONTRACT_LAST, preferred_element_type=jnp.float32
    )
    out_ref[...] = total.astype(out_ref.dtype)


def sum_body(parts_ref, out_ref):
    total = parts_ref[0].astype(jnp.float32)
    for part in range(1, parts_ref.shape[0]):
        total = total + parts_ref[part].astype(jnp.float32)
    out_ref[...] = total.astype(out_ref.dtype)


def over_tokens(left, right):
    return lax.dot_general(left, right, CONTRACT_FIRST, preferred_element_type=jnp.float32)


def w_in_grad_body(scale, rows_ref, rows_got_ref, delta_ref, delta_got_ref, mask_ref, out_ref):
    features = out_ref.shape[0]
    grad = over_tokens(rows_ref[:, features:], delta_ref[...])
    grad = grad + over_tokens(rows_got_ref[:, features:], delta_got_ref[...])
    out_ref[...] = (grad * scale * mask_ref[...].astype(jnp.float32)).astype(out_ref.dtype)


def w_out_grad_body(scale, act_ref, act_other_ref, rows_ref, rows_got_ref, mask_ref, out_ref):
    features = out_ref.shape[1]
    grad = over_tokens(act_ref[...], rows_ref[:, :features])
    grad = grad + over_tokens(act_other_ref[...], rows_got_ref[:, :features])
    out_ref[...] = (grad * scale * mask_ref[...].astype(jnp.float32)).astype(out_ref.dtype)


def shards(n_hid, n_row, inputs, out_grad, pre_act, w_in, w_out, pattern_in, pattern_out):
    far_groups, near_groups = groups(n_hid)
    far = n_hid // 2 // NEAR
    tokens, width = pre_act.shape
    own, features = out_grad.shape
    half = tokens // 2
    share = half // n_row
    runs = share // own
    core = lax.axis_index("hid") % 2
    row = lax.axis_index("row")
    struct = jax.ShapeDtypeStruct

    other = 1 - core

    def partner(x):
        return lax.ppermute(x, "hid", [(i, i ^ 1) for i in range(n_hid)])

    mask_in = widen(pattern_in, BLOCK)
    mask_out = widen(pattern_out, BLOCK)
    w_in_eff = w_in * mask_in
    w_out_eff = w_out * mask_out
    w_in_got = partner(w_in_eff)
    w_out_got = partner(w_out_eff)
    placed = pre_act.reshape(far, NEAR, 2, own, width)
    first = (row % (far // runs)) * runs
    mine = lax.dynamic_slice_in_dim(placed, first, runs, 0)
    mine = lax.dynamic_index_in_dim(mine, row // (far // runs), 1, keepdims=False)
    pre_own = lax.dynamic_index_in_dim(mine, core, 1, keepdims=False).reshape(share, width)
    pre_other = lax.dynamic_index_in_dim(mine, other, 1, keepdims=False).reshape(share, width)
    _, slope = gelu_parts(jnp.concatenate([pre_own, partner(pre_other)], axis=1))

    both = jnp.concatenate([out_grad, inputs], axis=1)
    rows = swap(jnp.broadcast_to(both[None], (far, own, 2 * features)), "hid", far_groups)
    rows, w_out_got, w_in_got, slope, w_in_eff, w_out_eff = lax.optimization_barrier(
        (rows, w_out_got, w_in_got, slope, w_in_eff, w_out_eff)
    )
    rows = rows.reshape(1, far * own, 2 * features)
    rows = swap(jnp.broadcast_to(rows, (NEAR, far * own, 2 * features)), "hid", near_groups)
    rows = rows.reshape(half, 2 * features)

    partial = local(
        act_grad_body,
        struct((half, 2 * width), jnp.float32),
        4 * half * features * width,
        rows,
        w_out_eff,
        w_out_got,
    )
    parts = swap(partial.reshape(n_row, share, 2 * width), "row")
    copies = local(
        delta_body,
        struct((n_row, share, 2 * width), jnp.bfloat16),
        n_row * share * width,
        parts,
        slope,
    )
    delta = swap(copies, "row").reshape(half, 2 * width)

    back = local(
        in_grad_body,
        struct((half, features), jnp.bfloat16),
        4 * half * features * width,
        delta,
        w_in_eff,
        w_in_got,
    )
    back = swap(back.reshape(NEAR, far * own, features), "hid", near_groups)
    back = local(sum_body, struct((far * own, features), jnp.bfloat16), back.size, back)
    back = swap(back.reshape(far, own, features), "hid", far_groups)
    in_grad = local(sum_body, struct((own, features), jnp.bfloat16), back.size, back)

    scale = 1.0 / math.sqrt(tokens)
    rows_got = partner(rows)
    w_in_grad = local(
        lambda *refs: w_in_grad_body(scale, *refs),
        struct((features, width), jnp.bfloat16),
        2 * tokens * features * width,
        rows,
        rows_got,
        delta[:, :width],
        partner(delta[:, width:]),
        mask_in,
    )
    value, _ = gelu_parts(placed.transpose(2, 1, 0, 3, 4).reshape(2, half, width))
    act = value.astype(jnp.bfloat16)
    w_out_grad = local(
        lambda *refs: w_out_grad_body(scale, *refs),
        struct((width, features), jnp.bfloat16),
        2 * tokens * features * width,
        lax.dynamic_index_in_dim(act, core, 0, keepdims=False),
        lax.dynamic_index_in_dim(act, other, 0, keepdims=False),
        rows,
        rows_got,
        mask_out,
    )
    return (in_grad, w_in_grad, w_out_grad)


def solution(mesh):
    placed = (
        P("hid", "row"),
        P("hid", "row"),
        P(None, "hid"),
        P("row", "hid"),
        P("hid", "row"),
        P("row", "hid"),
        P("hid", "row"),
    )
    return jax.shard_map(
        lambda *blocks: shards(mesh.shape["hid"], mesh.shape["row"], *blocks),
        mesh=mesh,
        in_specs=placed,
        out_specs=(P("hid", "row"), P("row", "hid"), P("hid", "row")),
        check_vma=False,
    )
```

time: 213 us -> 167 us (0.78)
  the two profiles are of different devices: /device:TPU:1 before, /device:TPU:32 now
where the time goes in v2:
time: 167 us
  blocking collectives  54 us (32%)
  starting transfers between devices  48.8 us (29%)
  waiting for transfers between devices  47.3 us (28%)
  local copies, waits for them, and re-layouts  7.05 us (4%)
  Pallas kernels  5.5 us (3%)
  other arithmetic  2.94 us (2%)
    all_to_all x3, blocking collectives, swap(): return lax.all_to_all(x, axis, 0, 0, axis_index_groups=within, tiled=True)  54 us
    all_to_all x3, waiting for transfers between devices, swap(): return lax.all_to_all(x, axis, 0, 0, axis_index_groups=within, tiled=True)  46.1 us
    all_to_all x3, starting transfers between devices, swap(): return lax.all_to_all(x, axis, 0, 0, axis_index_groups=within, tiled=True)  38.7 us
    ppermute x5, starting transfers between devices, partner(): return lax.ppermute(x, 'hid', [(i, i ^ 1) for i in range(n_hid)])  10.1 us
    pallas_call x7, Pallas kernels, local(): pl.pallas_call(body, out_shape=out_shape, in_specs=[pl.BlockSpec(memory_s...  5.5 us
    unnamed x23, local copies, waits for them, and re-layouts  3.87 us
  transfers between devices with their start and end apart: 8, of which 4 were waited for; matrix products, arithmetic and copies ran while one was open for 2% of the time, Pallas kernels for 2%

profile of v2, /device:TPU:32, one launch (start us, length us, event | category | flops | bytes accessed | tf_op | source)
XLA Modules:
  0.0 166.5 jit_solution(2246581895490312505)
XLA Ops:
  2.0 27.6 %all-to-all-start = ((bf16[8,8,1536]{2,1,0:T(8,128)(2,1)}), bf16[8,8,1536]{2,1,0:T(8,128)(2,1)}, u32[]{:S(2)}, u32[]{:S(2)}) async-start(bf16[8,8,1536]{2,1,0:T(8,128)(2,1)} %broadcast_in_dim.10), calls=%async_computation | async-start | bytes 393216 | tf_op jit(solution)/shard_map/all_to_all | solution.py:39
  29.9 1.9 %collective-permute-start = (bf16[384,768]{1,0:T(8,128)(2,1)S(1)}, bf16[384,768]{1,0:T(8,128)(2,1)S(1)}, u32[]{:S(2)}, u32[]{:S(2)}) collective-permute-start(bf16[384,768]{1,0:T(8,128)(2,1)S(1)} %get-tuple-element.10.own_ref), channel_id=1, source_target_pairs={{0,16},{16,0},{32,48},{48,32},{64,80},{80,64},{96,112},{112,96},{1... | collective-permute-start | bytes 1769480 | tf_op jit(solution)/shard_map/ppermute | solution.py:125
  32.5 0.7 copy-done.8
  33.4 2.4 %collective-permute-start.1 = (bf16[768,384]{1,0:T(8,128)(2,1)S(1)}, bf16[768,384]{1,0:T(8,128)(2,1)S(1)}, u32[]{:S(2)}, u32[]{:S(2)}) collective-permute-start(bf16[768,384]{1,0:T(8,128)(2,1)S(1)} %mul.62.own_ref), channel_id=1, source_target_pairs={{0,16},{16,0},{32,48},{48,32},{64,80},{80,64},{96,112},{112,96},{1... | collective-permute-start | bytes 1769480 | tf_op jit(solution)/shard_map/ppermute | solution.py:125
  35.8 0.7 dynamic-slice_bitcast_fusion.3
  36.6 1.9 %collective-permute-start.2 = (bf16[16,384]{1,0:T(8,128)(2,1)S(1)}, bf16[16,384]{1,0:T(8,128)(2,1)S(1)}, u32[]{:S(2)}, u32[]{:S(2)}) collective-permute-start(bf16[16,384]{1,0:T(8,128)(2,1)S(1)} %get-tuple-element.22), channel_id=1, source_target_pairs={{0,16},{16,0},{32,48},{48,32},{64,80},{80,64},{96,112},{112,96},{1... | collective-permute-start | bytes 36872 | tf_op jit(solution)/shard_map/ppermute | solution.py:125
  38.5 1.1 collective-permute-done.2
  40.3 0.8 copy-done.1
  41.1 0.8 copy-done.3
  41.9 22.9 %all-to-all-done = bf16[8,8,1536]{2,1,0:T(8,128)(2,1)} async-done(((bf16[8,8,1536]{2,1,0:T(8,128)(2,1)}), bf16[8,8,1536]{2,1,0:T(8,128)(2,1)}, u32[]{:S(2)}, u32[]{:S(2)}) %all-to-all-start) | async-done | bytes 196640 | tf_op jit(solution)/shard_map/all_to_all | solution.py:39
  64.8 1.0 broadcast_in_dim.14
  65.8 21.8 %all_to_all.30 = bf16[4,64,1536]{2,1,0:T(8,128)(2,1)S(1)} all-to-all(bf16[4,64,1536]{2,1,0:T(8,128)(2,1)S(1)} %broadcast_in_dim.14), channel_id=1, replica_groups={{0,32,64,96},{16,48,80,112},{128,160,192,224},{144,176,208,240},{256,28..., dimensions={0} | all-to-all | bytes 1572864 | tf_op jit(solution)/shard_map/all_to_all | solution.py:39
  88.2 19.5 %all_to_all.31.parts_ref = f32[16,16,768]{2,1,0:T(8,128)S(1)} all-to-all(f32[16,16,768]{2,1,0:T(8,128)S(1)} %bitcast.41), channel_id=1, replica_groups=mesh['hid'=64,'row'=16] {'row'}, dimensions={0} | all-to-all | bytes 1572864 | tf_op jit(solution)/shard_map/all_to_all | solution.py:39
  107.8 12.7 %all_to_all.32 = bf16[16,16,768]{2,1,0:T(8,128)(2,1)S(1)} all-to-all(bf16[16,16,768]{2,1,0:T(8,128)(2,1)S(1)} %shard_map.95), channel_id=1, replica_groups=mesh['hid'=64,'row'=16] {'row'}, dimensions={0} | all-to-all | bytes 786432 | tf_op jit(solution)/shard_map/all_to_all | solution.py:39
  121.8 5.6 %all-to-all-start.4 = ((bf16[4,64,768]{2,1,0:T(8,128)(2,1)}), bf16[4,64,768]{2,1,0:T(8,128)(2,1)S(1)}, u32[]{:S(2)}, u32[]{:S(2)}) async-start(bf16[4,64,768]{2,1,0:T(8,128)(2,1)} %bitcast.42), calls=%async_computation.4 | async-start | bytes 786432 | tf_op jit(solution)/shard_map/all_to_all | solution.py:39
  127.4 1.9 %collective-permute-start.3 = (bf16[256,1536]{1,0:T(8,128)(2,1)S(1)}, bf16[256,1536]{1,0:T(8,128)(2,1)S(1)}, u32[]{:S(2)}, u32[]{:S(2)}) collective-permute-start(bf16[256,1536]{1,0:T(8,128)(2,1)S(1)} %bitcast.36), channel_id=1, source_target_pairs={{0,16},{16,0},{32,48},{48,32},{64,80},{80,64},{96,112},{112,96},{1... | collective-permute-start | bytes 2359304 | tf_op jit(solution)/shard_map/ppermute | solution.py:125
  129.3 5.5 %all-to-all-done.4.parts_ref = bf16[4,64,768]{2,1,0:T(8,128)(2,1)S(1)} async-done(((bf16[4,64,768]{2,1,0:T(8,128)(2,1)}), bf16[4,64,768]{2,1,0:T(8,128)(2,1)S(1)}, u32[]{:S(2)}, u32[]{:S(2)}) %all-to-all-start.4) | async-done | bytes 393248 | tf_op jit(solution)/shard_map/all_to_all | solution.py:39
  135.5 5.5 %all-to-all-start.5 = ((bf16[8,8,768]{2,1,0:T(8,128)(2,1)}), bf16[8,8,768]{2,1,0:T(8,128)(2,1)}, u32[]{:S(2)}, u32[]{:S(2)}) async-start(bf16[8,8,768]{2,1,0:T(8,128)(2,1)} %bitcast.43), calls=%async_computation.5 | async-start | bytes 196608 | tf_op jit(solution)/shard_map/all_to_all | solution.py:39
  141.1 1.1 convert_bitcast_fusion
  142.2 1.9 %collective-permute-start.4 = (bf16[256,384]{1,0:T(8,128)(2,1)S(1)}, bf16[256,384]{1,0:T(8,128)(2,1)S(1)}, u32[]{:S(2)}, u32[]{:S(2)}) collective-permute-start(bf16[256,384]{1,0:T(8,128)(2,1)S(1)} %get-tuple-element.19), channel_id=1, source_target_pairs={{0,16},{16,0},{32,48},{48,32},{64,80},{80,64},{96,112},{112,96},{1... | collective-permute-start | bytes 589832 | tf_op jit(solution)/shard_map/ppermute | solution.py:125
  144.5 1.3 shard_map.100
  145.8 1.4 shard_map.99
  147.3 17.8 %all-to-all-done.5.parts_ref = bf16[8,8,768]{2,1,0:T(8,128)(2,1)} async-done(((bf16[8,8,768]{2,1,0:T(8,128)(2,1)}), bf16[8,8,768]{2,1,0:T(8,128)(2,1)}, u32[]{:S(2)}, u32[]{:S(2)}) %all-to-all-start.5) | async-done | bytes 98336 | tf_op jit(solution)/shard_map/all_to_all | solution.py:39
  165.0 1.5 shard_map.98
  (42 shorter events, 6.1 us)
Async XLA Ops:
  1.4 28.3 %copy-start.9 = (s32[3,6]{1,0:T(4,128)S(1)}, s32[3,6]{1,0:T(4,128)}, u32[]{:S(2)}) copy-start(s32[3,6]{1,0:T(4,128)} %param.13) | copy-start | bytes 220
  2.0 27.8 %copy-start.7 = (bf16[384,768]{1,0:T(8,128)(2,1)S(1)}, bf16[384,768]{1,0:T(8,128)(2,1)}, u32[]{:S(2)}) copy-start(bf16[384,768]{1,0:T(8,128)(2,1)} %param.11) | copy-start | bytes 1769476
  2.0 62.8 %all-to-all-start = ((bf16[8,8,1536]{2,1,0:T(8,128)(2,1)}), bf16[8,8,1536]{2,1,0:T(8,128)(2,1)}, u32[]{:S(2)}, u32[]{:S(2)}) async-start(bf16[8,8,1536]{2,1,0:T(8,128)(2,1)} %broadcast_in_dim.10), calls=%async_computation | async-start | bytes 393216 | tf_op jit(solution)/shard_map/all_to_all | solution.py:39
  29.8 2.0 %copy-start.10 = (s32[6,3]{0,1:T(4,128)S(1)}, s32[6,3]{0,1:T(4,128)}, u32[]{:S(2)}) copy-start(s32[6,3]{0,1:T(4,128)} %param.12) | copy-start | bytes 220
  29.9 10.4 %collective-permute-start = (bf16[384,768]{1,0:T(8,128)(2,1)S(1)}, bf16[384,768]{1,0:T(8,128)(2,1)S(1)}, u32[]{:S(2)}, u32[]{:S(2)}) collective-permute-start(bf16[384,768]{1,0:T(8,128)(2,1)S(1)} %get-tuple-element.10.own_ref), channel_id=1, source_target_pairs={{0,16},{16,0},{32,48},{48,32},{64,80},{80,64},{96,112},{112,96},{1... | collective-permute-start | bytes 1769480 | tf_op jit(solution)/shard_map/ppermute | solution.py:125
  32.1 1.1 copy-start.8
  33.4 7.7 %collective-permute-start.1 = (bf16[768,384]{1,0:T(8,128)(2,1)S(1)}, bf16[768,384]{1,0:T(8,128)(2,1)S(1)}, u32[]{:S(2)}, u32[]{:S(2)}) collective-permute-start(bf16[768,384]{1,0:T(8,128)(2,1)S(1)} %mul.62.own_ref), channel_id=1, source_target_pairs={{0,16},{16,0},{32,48},{48,32},{64,80},{80,64},{96,112},{112,96},{1... | collective-permute-start | bytes 1769480 | tf_op jit(solution)/shard_map/ppermute | solution.py:125
  36.6 3.1 %collective-permute-start.2 = (bf16[16,384]{1,0:T(8,128)(2,1)S(1)}, bf16[16,384]{1,0:T(8,128)(2,1)S(1)}, u32[]{:S(2)}, u32[]{:S(2)}) collective-permute-start(bf16[16,384]{1,0:T(8,128)(2,1)S(1)} %get-tuple-element.22), channel_id=1, source_target_pairs={{0,16},{16,0},{32,48},{48,32},{64,80},{80,64},{96,112},{112,96},{1... | collective-permute-start | bytes 36872 | tf_op jit(solution)/shard_map/ppermute | solution.py:125
  40.3 0.8 copy-start.1
  41.1 0.8 copy-start.3
  65.8 21.8 %copy-start.2 = (bf16[384,768]{1,0:T(8,128)(2,1)S(1)}, bf16[384,768]{1,0:T(8,128)(2,1)}, u32[]{:S(2)}) copy-start(bf16[384,768]{1,0:T(8,128)(2,1)} %copy-done.1) | copy-start | bytes 1769476
  88.2 19.5 %copy-start.6 = (f32[16,768]{1,0:T(8,128)S(1)}, f32[16,768]{1,0:T(8,128)}, u32[]{:S(2)}) copy-start(f32[16,768]{1,0:T(8,128)} %fusion.16.slope_ref) | copy-start | bytes 147460
  107.8 12.7 %copy-start.4 = (bf16[768,384]{1,0:T(8,128)(2,1)S(1)}, bf16[768,384]{1,0:T(8,128)(2,1)}, u32[]{:S(2)}) copy-start(bf16[768,384]{1,0:T(8,128)(2,1)} %copy-done.3) | copy-start | bytes 1769476
  121.1 0.7 copy-start
  121.8 13.0 %all-to-all-start.4 = ((bf16[4,64,768]{2,1,0:T(8,128)(2,1)}), bf16[4,64,768]{2,1,0:T(8,128)(2,1)S(1)}, u32[]{:S(2)}, u32[]{:S(2)}) async-start(bf16[4,64,768]{2,1,0:T(8,128)(2,1)} %bitcast.42), calls=%async_computation.4 | async-start | bytes 786432 | tf_op jit(solution)/shard_map/all_to_all | solution.py:39
  127.4 17.1 %collective-permute-start.3 = (bf16[256,1536]{1,0:T(8,128)(2,1)S(1)}, bf16[256,1536]{1,0:T(8,128)(2,1)S(1)}, u32[]{:S(2)}, u32[]{:S(2)}) collective-permute-start(bf16[256,1536]{1,0:T(8,128)(2,1)S(1)} %bitcast.36), channel_id=1, source_target_pairs={{0,16},{16,0},{32,48},{48,32},{64,80},{80,64},{96,112},{112,96},{1... | collective-permute-start | bytes 2359304 | tf_op jit(solution)/shard_map/ppermute | solution.py:125
  134.9 0.6 copy-start.5
  135.5 29.5 %all-to-all-start.5 = ((bf16[8,8,768]{2,1,0:T(8,128)(2,1)}), bf16[8,8,768]{2,1,0:T(8,128)(2,1)}, u32[]{:S(2)}, u32[]{:S(2)}) async-start(bf16[8,8,768]{2,1,0:T(8,128)(2,1)} %bitcast.43), calls=%async_computation.5 | async-start | bytes 196608 | tf_op jit(solution)/shard_map/all_to_all | solution.py:39
  142.2 3.6 %collective-permute-start.4 = (bf16[256,384]{1,0:T(8,128)(2,1)S(1)}, bf16[256,384]{1,0:T(8,128)(2,1)S(1)}, u32[]{:S(2)}, u32[]{:S(2)}) collective-permute-start(bf16[256,384]{1,0:T(8,128)(2,1)S(1)} %get-tuple-element.19), channel_id=1, source_target_pairs={{0,16},{16,0},{32,48},{48,32},{64,80},{80,64},{96,112},{112,96},{1... | collective-permute-start | bytes 589832 | tf_op jit(solution)/shard_map/ppermute | solution.py:125

commit v3 on v2

--- a/solution.py
+++ b/solution.py
@@ -52,8 +52,8 @@
 
 
 def act_grad_body(rows_ref, own_ref, got_ref, out_ref):
-    width, features = own_ref.shape
-    rows = rows_ref[:, :features]
+    width = own_ref.shape[0]
+    rows = rows_ref[...]
     out_ref[:, :width] = lax.dot_general(
         rows, own_ref[...], CONTRACT_LAST, preferred_element_type=jnp.float32
     )
@@ -93,21 +93,23 @@
     return lax.dot_general(left, right, CONTRACT_FIRST, preferred_element_type=jnp.float32)
 
 
-def w_in_grad_body(scale, rows_ref, rows_got_ref, delta_ref, delta_got_ref, mask_ref, out_ref):
-    features = out_ref.shape[0]
-    grad = over_tokens(rows_ref[:, features:], delta_ref[...])
-    grad = grad + over_tokens(rows_got_ref[:, features:], delta_got_ref[...])
+def w_in_grad_body(scale, panel_ref, delta_ref, mask_ref, out_ref):
+    grad = over_tokens(panel_ref[...].astype(jnp.bfloat16), delta_ref[...])
     out_ref[...] = (grad * scale * mask_ref[...].astype(jnp.float32)).astype(out_ref.dtype)
 
 
 def w_out_grad_body(scale, act_ref, act_other_ref, rows_ref, rows_got_ref, mask_ref, out_ref):
-    features = out_ref.shape[1]
-    grad = over_tokens(act_ref[...], rows_ref[:, :features])
-    grad = grad + over_tokens(act_other_ref[...], rows_got_ref[:, :features])
+    grad = over_tokens(act_ref[...], rows_ref[...])
+    grad = grad + over_tokens(act_other_ref[...], rows_got_ref[...])
     out_ref[...] = (grad * scale * mask_ref[...].astype(jnp.float32)).astype(out_ref.dtype)
 
 
-def shards(n_hid, n_row, inputs, out_grad, pre_act, w_in, w_out, pattern_in, pattern_out):
+def partner(x):
+    count = lax.axis_size("hid")
+    return lax.ppermute(x, "hid", [(i, i ^ 1) for i in range(count)])
+
+
+def chain(n_hid, n_row, out_grad, pre_act, w_in, w_out, pattern_in, pattern_out):
     far_groups, near_groups = groups(n_hid)
     far = n_hid // 2 // NEAR
     tokens, width = pre_act.shape
@@ -119,15 +121,8 @@
     row = lax.axis_index("row")
     struct = jax.ShapeDtypeStruct
 
-    other = 1 - core
-
-    def partner(x):
-        return lax.ppermute(x, "hid", [(i, i ^ 1) for i in range(n_hid)])
-
-    mask_in = widen(pattern_in, BLOCK)
-    mask_out = widen(pattern_out, BLOCK)
-    w_in_eff = w_in * mask_in
-    w_out_eff = w_out * mask_out
+    w_in_eff = w_in * widen(pattern_in, BLOCK)
+    w_out_eff = w_out * widen(pattern_out, BLOCK)
     w_in_got = partner(w_in_eff)
     w_out_got = partner(w_out_eff)
     placed = pre_act.reshape(far, NEAR, 2, own, width)
@@ -135,17 +130,16 @@
     mine = lax.dynamic_slice_in_dim(placed, first, runs, 0)
     mine = lax.dynamic_index_in_dim(mine, row // (far // runs), 1, keepdims=False)
     pre_own = lax.dynamic_index_in_dim(mine, core, 1, keepdims=False).reshape(share, width)
-    pre_other = lax.dynamic_index_in_dim(mine, other, 1, keepdims=False).reshape(share, width)
+    pre_other = lax.dynamic_index_in_dim(mine, 1 - core, 1, keepdims=False).reshape(share, width)
     _, slope = gelu_parts(jnp.concatenate([pre_own, partner(pre_other)], axis=1))
 
-    both = jnp.concatenate([out_grad, inputs], axis=1)
-    rows = swap(jnp.broadcast_to(both[None], (far, own, 2 * features)), "hid", far_groups)
+    rows = swap(jnp.broadcast_to(out_grad[None], (far, own, features)), "hid", far_groups)
     rows, w_out_got, w_in_got, slope, w_in_eff, w_out_eff = lax.optimization_barrier(
         (rows, w_out_got, w_in_got, slope, w_in_eff, w_out_eff)
     )
-    rows = rows.reshape(1, far * own, 2 * features)
-    rows = swap(jnp.broadcast_to(rows, (NEAR, far * own, 2 * features)), "hid", near_groups)
-    rows = rows.reshape(half, 2 * features)
+    rows = rows.reshape(1, far * own, features)
+    rows = swap(jnp.broadcast_to(rows, (NEAR, far * own, features)), "hid", near_groups)
+    rows = rows.reshape(half, features)
 
     partial = local(
         act_grad_body,
@@ -175,31 +169,64 @@
     )
     back = swap(back.reshape(NEAR, far * own, features), "hid", near_groups)
     back = local(sum_body, struct((far * own, features), jnp.bfloat16), back.size, back)
+    return back, delta, rows
+
+
+def shards(n_hid, n_row, inputs, out_grad, pre_act, w_in, w_out, pattern_in, pattern_out):
+    far_groups, _ = groups(n_hid)
+    far = n_hid // 2 // NEAR
+    tokens, width = pre_act.shape
+    own, features = out_grad.shape
+    half = tokens // 2
+    core = lax.axis_index("hid") % 2
+    struct = jax.ShapeDtypeStruct
+
+    mask_in = widen(pattern_in, BLOCK)
+    mask_out = widen(pattern_out, BLOCK)
+    in_panel = lax.all_gather(inputs.astype(jnp.float32), "hid", axis=0, tiled=True)
+    back, delta, rows = lax.cond(
+        pattern_in[0, 0] >= 0,
+        lambda *args: chain(n_hid, n_row, *args),
+        lambda *args: (
+            jnp.zeros((far * own, features), jnp.bfloat16),
+            jnp.zeros((half, 2 * width), jnp.bfloat16),
+            jnp.zeros((half, features), jnp.bfloat16),
+        ),
+        out_grad,
+        pre_act,
+        w_in,
+        w_out,
+        pattern_in,
+        pattern_out,
+    )
     back = swap(back.reshape(far, own, features), "hid", far_groups)
     in_grad = local(sum_body, struct((own, features), jnp.bfloat16), back.size, back)
 
     scale = 1.0 / math.sqrt(tokens)
-    rows_got = partner(rows)
+    delta_own, delta_got = delta[:, :width], partner(delta[:, width:])
+    by_core = lax.dynamic_slice_in_dim(
+        jnp.concatenate([delta_own, delta_got, delta_own], axis=0), core * half, tokens, 0
+    )
+    by_token = by_core.reshape(2, NEAR, far, own, width).transpose(2, 1, 0, 3, 4)
     w_in_grad = local(
         lambda *refs: w_in_grad_body(scale, *refs),
         struct((features, width), jnp.bfloat16),
         2 * tokens * features * width,
-        rows,
-        rows_got,
-        delta[:, :width],
-        partner(delta[:, width:]),
+        in_panel,
+        by_token.reshape(tokens, width),
         mask_in,
     )
-    value, _ = gelu_parts(placed.transpose(2, 1, 0, 3, 4).reshape(2, half, width))
-    act = value.astype(jnp.bfloat16)
+    value, _ = gelu_parts(pre_act)
+    act = value.astype(jnp.bfloat16).reshape(far, NEAR, 2, own, width)
+    act = act.transpose(2, 1, 0, 3, 4).reshape(2, half, width)
     w_out_grad = local(
         lambda *refs: w_out_grad_body(scale, *refs),
         struct((width, features), jnp.bfloat16),
         2 * tokens * features * width,
         lax.dynamic_index_in_dim(act, core, 0, keepdims=False),
-        lax.dynamic_index_in_dim(act, other, 0, keepdims=False),
+        lax.dynamic_index_in_dim(act, 1 - core, 0, keepdims=False),
         rows,
-        rows_got,
+        partner(rows),
         mask_out,
     )
     return (in_grad, w_in_grad, w_out_grad)

time: 167 us -> 174 us (1.042)
  the two profiles are of different devices: /device:TPU:32 before, /device:TPU:1 now
where the time goes in v3:
time: 174 us; the launch traced here: 172 us
  blocking collectives  59.3 us (34%)
  starting transfers between devices  54.2 us (31%)
  waiting for transfers between devices  23 us (13%)
  between operations  14.9 us (9%)
  local copies, waits for them, and re-layouts  7.98 us (5%)
  Pallas kernels  6.29 us (4%)
  other arithmetic  5.54 us (3%)
    all_to_all x4, blocking collectives, swap(): return lax.all_to_all(x, axis, 0, 0, axis_index_groups=within, tiled=True)  59.3 us
    all_to_all x2, starting transfers between devices, swap(): return lax.all_to_all(x, axis, 0, 0, axis_index_groups=within, tiled=True)  38.2 us
    all_to_all x2, waiting for transfers between devices, swap(): return lax.all_to_all(x, axis, 0, 0, axis_index_groups=within, tiled=True)  22.2 us
    ppermute x5, starting transfers between devices, partner(): return lax.ppermute(x, 'hid', [(i, i ^ 1) for i in range(count)])  16 us
    pallas_call x7, Pallas kernels, local(): pl.pallas_call(body, out_shape=out_shape, in_specs=[pl.BlockSpec(memory_s...  6.29 us
  transfers between devices with their start and end apart: 8, of which 3 were waited for; matrix products, arithmetic and copies ran while one was open for 6% of the time, Pallas kernels for 3%

profile of v3, /device:TPU:1, one launch (start us, length us, event | category | flops | bytes accessed | tf_op | source)
XLA Modules:
  0.0 171.5 jit_solution(9475684310675470790)
XLA Ops:
  7.2 1.3 convert_element_type.32
  8.5 1.2 slice.9
  10.4 115.2 %conditional.1 = (bf16[64,768]{1,0:T(8,128)(2,1)}, bf16[256,768]{1,0:T(8,128)(2,1)}, bf16[256,768]{1,0:T(8,128)(2,1)S(1)}) conditional(s32[]{:T(128)} %bitcast.8, () %tuple.17, (bf16[8,768]{1,0:T(8,128)(2,1)}, s32[3,6]{1,0:T(4,128)}, bf16[384,768]{1,0:T(8,128)(2,1)}, s32[6,3]{0,1:T(4,128)}, bf16[768,384]{1,0:T(8,128)(2,1)}, ...), branch_computations={%region_0.1_spmd, %region_1.2_spmd} | conditional | flops 605110336 | bytes 28349868 | solution.py:187
  10.4 1.4 broadcast_in_dim.0
  11.8 28.9 %all-to-all-start = ((bf16[8,8,768]{2,1,0:T(8,128)(2,1)}), bf16[8,8,768]{2,1,0:T(8,128)(2,1)S(1)}, u32[]{:S(2)}, u32[]{:S(2)}) async-start(bf16[8,8,768]{2,1,0:T(8,128)(2,1)} %broadcast_in_dim.0), calls=%async_computation | async-start | bytes 196608 | tf_op jit(solution)/shard_map/cond/branch_1_fun/all_to_all | solution.py:39
  41.5 1.1 bitcast_multiply_fusion.own_ref
  42.7 2.9 %collective-permute-start = (bf16[384,768]{1,0:T(8,128)(2,1)S(1)}, bf16[384,768]{1,0:T(8,128)(2,1)S(1)}, u32[]{:S(2)}, u32[]{:S(2)}) collective-permute-start(bf16[384,768]{1,0:T(8,128)(2,1)S(1)} %bitcast_multiply_fusion.own_ref), channel_id=1, source_target_pairs={{0,16},{16,0},{32,48},{48,32},{64,80},{80,64},{96,112},{112,96},{1... | collective-permute-start | bytes 1769480 | tf_op jit(solution)/shard_map/cond/branch_1_fun/ppermute | solution.py:109
  46.8 1.9 %collective-permute-start.1 = (bf16[768,384]{1,0:T(8,128)(2,1)S(1)}, bf16[768,384]{1,0:T(8,128)(2,1)S(1)}, u32[]{:S(2)}, u32[]{:S(2)}) collective-permute-start(bf16[768,384]{1,0:T(8,128)(2,1)S(1)} %mul.43.own_ref), channel_id=1, source_target_pairs={{0,16},{16,0},{32,48},{48,32},{64,80},{80,64},{96,112},{112,96},{1... | collective-permute-start | bytes 1769480 | tf_op jit(solution)/shard_map/cond/branch_1_fun/ppermute | solution.py:109
  49.5 2.4 %collective-permute-start.2 = (bf16[16,384]{1,0:T(8,128)(2,1)S(1)}, bf16[16,384]{1,0:T(8,128)(2,1)S(1)}, u32[]{:S(2)}, u32[]{:S(2)}) collective-permute-start(bf16[16,384]{1,0:T(8,128)(2,1)S(1)} %get-tuple-element.46), channel_id=1, source_target_pairs={{0,16},{16,0},{32,48},{48,32},{64,80},{80,64},{96,112},{112,96},{1... | collective-permute-start | bytes 36872 | tf_op jit(solution)/shard_map/cond/branch_1_fun/ppermute | solution.py:109
  52.8 10.5 %all-to-all-done = bf16[8,8,768]{2,1,0:T(8,128)(2,1)S(1)} async-done(((bf16[8,8,768]{2,1,0:T(8,128)(2,1)}), bf16[8,8,768]{2,1,0:T(8,128)(2,1)S(1)}, u32[]{:S(2)}, u32[]{:S(2)}) %all-to-all-start) | async-done | bytes 98336 | tf_op jit(solution)/shard_map/cond/branch_1_fun/all_to_all | solution.py:39
  63.3 15.3 %all_to_all.25 = bf16[4,64,768]{2,1,0:T(8,128)(2,1)S(1)} all-to-all(bf16[4,64,768]{2,1,0:T(8,128)(2,1)S(1)} %broadcast_in_dim.5), channel_id=1, replica_groups={{0,32,64,96},{16,48,80,112},{128,160,192,224},{144,176,208,240},{256,28..., dimensions={0} | all-to-all | bytes 786432 | tf_op jit(solution)/shard_map/cond/branch_1_fun/all_to_all | solution.py:39
  79.2 19.9 %all_to_all.26.parts_ref = f32[16,16,768]{2,1,0:T(8,128)S(1)} all-to-all(f32[16,16,768]{2,1,0:T(8,128)S(1)} %bitcast.51), channel_id=1, replica_groups=mesh['hid'=64,'row'=16] {'row'}, dimensions={0} | all-to-all | bytes 1572864 | tf_op jit(solution)/shard_map/cond/branch_1_fun/all_to_all | solution.py:39
  99.1 12.0 %all_to_all.27 = bf16[16,16,768]{2,1,0:T(8,128)(2,1)} all-to-all(bf16[16,16,768]{2,1,0:T(8,128)(2,1)S(1)} %branch_1_fun.5), channel_id=1, replica_groups=mesh['hid'=64,'row'=16] {'row'}, dimensions={0} | all-to-all | bytes 786432 | tf_op jit(solution)/shard_map/cond/branch_1_fun/all_to_all | solution.py:39
  111.1 1.6 branch_1_fun.6
  112.8 12.1 %all_to_all.28.parts_ref = bf16[4,64,768]{2,1,0:T(8,128)(2,1)S(1)} all-to-all(bf16[4,64,768]{2,1,0:T(8,128)(2,1)S(1)} %bitcast.54), channel_id=1, replica_groups={{0,32,64,96},{16,48,80,112},{128,160,192,224},{144,176,208,240},{256,28..., dimensions={0} | all-to-all | bytes 786432 | tf_op jit(solution)/shard_map/cond/branch_1_fun/all_to_all | solution.py:39
  125.6 9.3 %all-to-all-start.5 = ((bf16[8,8,768]{2,1,0:T(8,128)(2,1)}), bf16[8,8,768]{2,1,0:T(8,128)(2,1)S(1)}, u32[]{:S(2)}, u32[]{:S(2)}) async-start(bf16[8,8,768]{2,1,0:T(8,128)(2,1)} %bitcast.9), calls=%async_computation.5 | async-start | bytes 196608 | tf_op jit(solution)/shard_map/all_to_all | solution.py:39
  134.9 1.1 fusion.17
  135.9 6.9 %collective-permute-start.3 = (bf16[256,384]{1,0:T(8,128)(2,1)S(1)}, bf16[256,384]{1,0:T(8,128)(2,1)S(1)}, u32[]{:S(2)}, u32[]{:S(2)}) collective-permute-start(bf16[256,384]{1,0:T(8,128)(2,1)S(1)} %get-tuple-element.49), channel_id=1, source_target_pairs={{0,16},{16,0},{32,48},{48,32},{64,80},{80,64},{96,112},{112,96},{1... | collective-permute-start | bytes 589832 | tf_op jit(solution)/shard_map/ppermute | solution.py:109
  142.9 1.9 %collective-permute-start.4 = (bf16[256,768]{1,0:T(8,128)(2,1)S(1)}, bf16[256,768]{1,0:T(8,128)(2,1)S(1)}, u32[]{:S(2)}, u32[]{:S(2)}) collective-permute-start(bf16[256,768]{1,0:T(8,128)(2,1)S(1)} %get-tuple-element.32.refs_2_), channel_id=1, source_target_pairs={{0,16},{16,0},{32,48},{48,32},{64,80},{80,64},{96,112},{112,96},{1... | collective-permute-start | bytes 1179656 | tf_op jit(solution)/shard_map/ppermute | solution.py:109
  144.8 1.3 fusion.14
  148.2 1.3 shard_map.99
  149.5 11.7 %all-to-all-done.5.parts_ref = bf16[8,8,768]{2,1,0:T(8,128)(2,1)S(1)} async-done(((bf16[8,8,768]{2,1,0:T(8,128)(2,1)}), bf16[8,8,768]{2,1,0:T(8,128)(2,1)S(1)}, u32[]{:S(2)}, u32[]{:S(2)}) %all-to-all-start.5) | async-done | bytes 98336 | tf_op jit(solution)/shard_map/all_to_all | solution.py:39
  161.8 1.4 copy-done
  163.2 1.4 shard_map.98
  (46 shorter events, 7.6 us)
Async XLA Ops:
  7.2 154.7 %all-gather.2.cloned.1.call-start = ((), (), s32[]{:S(2)}) async-start(), calls=%async_computation.6 | async-start | bytes 1597440 | tf_op jit(solution)/shard_map/all_gather | solution.py:186
  10.4 35.1 %copy-start.5 = (s32[6,3]{0,1:T(4,128)S(1)}, s32[6,3]{0,1:T(4,128)}, u32[]{:S(2)}) copy-start(s32[6,3]{0,1:T(4,128)} %get-tuple-element.16) | copy-start | bytes 220 | tf_op jit(solution)/shard_map/cond
  11.8 51.5 %all-to-all-start = ((bf16[8,8,768]{2,1,0:T(8,128)(2,1)}), bf16[8,8,768]{2,1,0:T(8,128)(2,1)S(1)}, u32[]{:S(2)}, u32[]{:S(2)}) async-start(bf16[8,8,768]{2,1,0:T(8,128)(2,1)} %broadcast_in_dim.0), calls=%async_computation | async-start | bytes 196608 | tf_op jit(solution)/shard_map/cond/branch_1_fun/all_to_all | solution.py:39
  42.7 10.1 %collective-permute-start = (bf16[384,768]{1,0:T(8,128)(2,1)S(1)}, bf16[384,768]{1,0:T(8,128)(2,1)S(1)}, u32[]{:S(2)}, u32[]{:S(2)}) collective-permute-start(bf16[384,768]{1,0:T(8,128)(2,1)S(1)} %bitcast_multiply_fusion.own_ref), channel_id=1, source_target_pairs={{0,16},{16,0},{32,48},{48,32},{64,80},{80,64},{96,112},{112,96},{1... | collective-permute-start | bytes 1769480 | tf_op jit(solution)/shard_map/cond/branch_1_fun/ppermute | solution.py:109
  45.6 1.1 copy-start.3
  46.8 6.0 %collective-permute-start.1 = (bf16[768,384]{1,0:T(8,128)(2,1)S(1)}, bf16[768,384]{1,0:T(8,128)(2,1)S(1)}, u32[]{:S(2)}, u32[]{:S(2)}) collective-permute-start(bf16[768,384]{1,0:T(8,128)(2,1)S(1)} %mul.43.own_ref), channel_id=1, source_target_pairs={{0,16},{16,0},{32,48},{48,32},{64,80},{80,64},{96,112},{112,96},{1... | collective-permute-start | bytes 1769480 | tf_op jit(solution)/shard_map/cond/branch_1_fun/ppermute | solution.py:109
  49.5 3.2 %collective-permute-start.2 = (bf16[16,384]{1,0:T(8,128)(2,1)S(1)}, bf16[16,384]{1,0:T(8,128)(2,1)S(1)}, u32[]{:S(2)}, u32[]{:S(2)}) collective-permute-start(bf16[16,384]{1,0:T(8,128)(2,1)S(1)} %get-tuple-element.46), channel_id=1, source_target_pairs={{0,16},{16,0},{32,48},{48,32},{64,80},{80,64},{96,112},{112,96},{1... | collective-permute-start | bytes 36872 | tf_op jit(solution)/shard_map/cond/branch_1_fun/ppermute | solution.py:109
  78.6 20.5 %copy-start.1 = (bf16[4,64,768]{2,1,0:T(8,128)(2,1)}, bf16[4,64,768]{2,1,0:T(8,128)(2,1)S(1)}, u32[]{:S(2)}) copy-start(bf16[4,64,768]{2,1,0:T(8,128)(2,1)S(1)} %all_to_all.25) | copy-start | bytes 1179652 | tf_op jit(solution)/shard_map/cond
  111.1 14.4 %copy-start.2 = (bf16[4,64,768]{2,1,0:T(8,128)(2,1)S(1)}, bf16[4,64,768]{2,1,0:T(8,128)(2,1)}, u32[]{:S(2)}) copy-start(bf16[4,64,768]{2,1,0:T(8,128)(2,1)} %copy-done.1) | copy-start | bytes 1179652 | tf_op jit(solution)/shard_map/cond
  125.6 20.5 %copy-start.4 = (s32[6,3]{0,1:T(4,128)S(1)}, s32[6,3]{0,1:T(4,128)}, u32[]{:S(2)}) copy-start(s32[6,3]{0,1:T(4,128)} %param.14) | copy-start | bytes 220
  125.6 20.5 %copy-start.6 = (s32[3,6]{1,0:T(4,128)S(1)}, s32[3,6]{1,0:T(4,128)}, u32[]{:S(2)}) copy-start(s32[3,6]{1,0:T(4,128)} %param.15) | copy-start | bytes 220
  125.6 35.6 %all-to-all-start.5 = ((bf16[8,8,768]{2,1,0:T(8,128)(2,1)}), bf16[8,8,768]{2,1,0:T(8,128)(2,1)S(1)}, u32[]{:S(2)}, u32[]{:S(2)}) async-start(bf16[8,8,768]{2,1,0:T(8,128)(2,1)} %bitcast.9), calls=%async_computation.5 | async-start | bytes 196608 | tf_op jit(solution)/shard_map/all_to_all | solution.py:39
  135.9 11.2 %collective-permute-start.3 = (bf16[256,384]{1,0:T(8,128)(2,1)S(1)}, bf16[256,384]{1,0:T(8,128)(2,1)S(1)}, u32[]{:S(2)}, u32[]{:S(2)}) collective-permute-start(bf16[256,384]{1,0:T(8,128)(2,1)S(1)} %get-tuple-element.49), channel_id=1, source_target_pairs={{0,16},{16,0},{32,48},{48,32},{64,80},{80,64},{96,112},{112,96},{1... | collective-permute-start | bytes 589832 | tf_op jit(solution)/shard_map/ppermute | solution.py:109
  142.9 5.3 %collective-permute-start.4 = (bf16[256,768]{1,0:T(8,128)(2,1)S(1)}, bf16[256,768]{1,0:T(8,128)(2,1)S(1)}, u32[]{:S(2)}, u32[]{:S(2)}) collective-permute-start(bf16[256,768]{1,0:T(8,128)(2,1)S(1)} %get-tuple-element.32.refs_2_), channel_id=1, source_target_pairs={{0,16},{16,0},{32,48},{48,32},{64,80},{80,64},{96,112},{112,96},{1... | collective-permute-start | bytes 1179656 | tf_op jit(solution)/shard_map/ppermute | solution.py:109
  161.8 1.4 copy-start
Sparse Core Ops, SparseCore 0:
  10.7 147.6 all-gather.1

commit v4 on v2

--- a/solution.py
+++ b/solution.py
@@ -52,14 +52,28 @@
 
 
 def act_grad_body(rows_ref, own_ref, got_ref, out_ref):
-    width, features = own_ref.shape
-    rows = rows_ref[:, :features]
+    width = own_ref.shape[0]
+    rows = rows_ref[...]
     out_ref[:, :width] = lax.dot_general(
         rows, own_ref[...], CONTRACT_LAST, preferred_element_type=jnp.float32
     )
     out_ref[:, width:] = lax.dot_general(
         rows, got_ref[...], CONTRACT_LAST, preferred_element_type=jnp.float32
     )
+
+
+def spread_body(left_ref, right_ref, out_ref):
+    width = left_ref.shape[1]
+    for copy in range(out_ref.shape[0]):
+        out_ref[copy, :, :width] = left_ref[...]
+        out_ref[copy, :, width:] = right_ref[...]
+
+
+def place_body(spots_ref, *refs):
+    *blocks, out_ref = refs
+    for block, block_ref in enumerate(blocks):
+        count = block_ref.shape[0]
+        out_ref[pl.ds(pl.multiple_of(spots_ref[block] * count, count), count), :] = block_ref[...]
 
 
 def delta_body(parts_ref, slope_ref, out_ref):
@@ -94,16 +108,14 @@
 
 
 def w_in_grad_body(scale, rows_ref, rows_got_ref, delta_ref, delta_got_ref, mask_ref, out_ref):
-    features = out_ref.shape[0]
-    grad = over_tokens(rows_ref[:, features:], delta_ref[...])
-    grad = grad + over_tokens(rows_got_ref[:, features:], delta_got_ref[...])
+    grad = over_tokens(rows_ref[...], delta_ref[...])
+    grad = grad + over_tokens(rows_got_ref[...], delta_got_ref[...])
     out_ref[...] = (grad * scale * mask_ref[...].astype(jnp.float32)).astype(out_ref.dtype)
 
 
 def w_out_grad_body(scale, act_ref, act_other_ref, rows_ref, rows_got_ref, mask_ref, out_ref):
-    features = out_ref.shape[1]
-    grad = over_tokens(act_ref[...], rows_ref[:, :features])
-    grad = grad + over_tokens(act_other_ref[...], rows_got_ref[:, :features])
+    grad = over_tokens(act_ref[...], rows_ref[...])
+    grad = grad + over_tokens(act_other_ref[...], rows_got_ref[...])
     out_ref[...] = (grad * scale * mask_ref[...].astype(jnp.float32)).astype(out_ref.dtype)
 
 
@@ -138,15 +150,24 @@
     pre_other = lax.dynamic_index_in_dim(mine, other, 1, keepdims=False).reshape(share, width)
     _, slope = gelu_parts(jnp.concatenate([pre_own, partner(pre_other)], axis=1))
 
-    both = jnp.concatenate([out_grad, inputs], axis=1)
-    rows = swap(jnp.broadcast_to(both[None], (far, own, 2 * features)), "hid", far_groups)
+    both = local(spread_body, struct((far, own, 2 * features), jnp.bfloat16), 0, out_grad, inputs)
+    rows = swap(both, "hid", far_groups)
     rows, w_out_got, w_in_got, slope, w_in_eff, w_out_eff = lax.optimization_barrier(
         (rows, w_out_got, w_in_got, slope, w_in_eff, w_out_eff)
     )
-    rows = rows.reshape(1, far * own, 2 * features)
-    rows = swap(jnp.broadcast_to(rows, (NEAR, far * own, 2 * features)), "hid", near_groups)
-    rows = rows.reshape(half, 2 * features)
-
+    rows = rows.reshape(far * own, 2 * features)
+    in_block = rows[:, features:]
+    rows = jnp.broadcast_to(rows[None, :, :features], (NEAR, far * own, features))
+    rows = swap(rows, "hid", near_groups).reshape(half, features)
+
+    n = lax.axis_index("hid") // 2 % NEAR
+    spots = jnp.stack([(n + NEAR - step) % NEAR for step in range(NEAR)]).astype(jnp.int32)
+    in_blocks = [in_block]
+    for step in range(1, NEAR):
+        pairs = [
+            (i, i - 2 * (i // 2 % NEAR) + 2 * ((i // 2 + step) % NEAR)) for i in range(n_hid)
+        ]
+        in_blocks.append(lax.ppermute(in_block, "hid", pairs))
     partial = local(
         act_grad_body,
         struct((half, 2 * width), jnp.float32),
@@ -156,6 +177,7 @@
         w_out_got,
     )
     parts = swap(partial.reshape(n_row, share, 2 * width), "row")
+    parts, *in_blocks[1:3] = lax.optimization_barrier((parts, *in_blocks[1:3]))
     copies = local(
         delta_body,
         struct((n_row, share, 2 * width), jnp.bfloat16),
@@ -164,6 +186,19 @@
         slope,
     )
     delta = swap(copies, "row").reshape(half, 2 * width)
+    delta, *in_blocks[3:] = lax.optimization_barrier((delta, *in_blocks[3:]))
+
+    in_rows = pl.pallas_call(
+        place_body,
+        out_shape=struct((half, features), jnp.bfloat16),
+        in_specs=[pl.BlockSpec(memory_space=pltpu.SMEM)]
+        + [pl.BlockSpec(memory_space=pltpu.VMEM)] * NEAR,
+        out_specs=pl.BlockSpec(memory_space=pltpu.VMEM),
+        compiler_params=pltpu.CompilerParams(vmem_limit_bytes=24 * 2**20),
+        cost_estimate=pl.CostEstimate(
+            flops=0, bytes_accessed=4 * half * features, transcendentals=0
+        ),
+    )(spots, *in_blocks)
 
     back = local(
         in_grad_body,
@@ -179,13 +214,12 @@
     in_grad = local(sum_body, struct((own, features), jnp.bfloat16), back.size, back)
 
     scale = 1.0 / math.sqrt(tokens)
-    rows_got = partner(rows)
     w_in_grad = local(
         lambda *refs: w_in_grad_body(scale, *refs),
         struct((features, width), jnp.bfloat16),
         2 * tokens * features * width,
-        rows,
-        rows_got,
+        in_rows,
+        partner(in_rows),
         delta[:, :width],
         partner(delta[:, width:]),
         mask_in,
@@ -199,7 +233,7 @@
         lax.dynamic_index_in_dim(act, core, 0, keepdims=False),
         lax.dynamic_index_in_dim(act, other, 0, keepdims=False),
         rows,
-        rows_got,
+        partner(rows),
         mask_out,
     )
     return (in_grad, w_in_grad, w_out_grad)

time: 167 us -> 165 us (0.988)
  the two profiles are of different devices: /device:TPU:32 before, /device:TPU:4 now
where the time goes in v4:
time: 165 us; the launch traced here: 164 us
  starting transfers between devices  76.7 us (46%)
  waiting for transfers between devices  49.8 us (30%)
  blocking collectives  17.8 us (11%)
  Pallas kernels  9.95 us (6%)
  local copies, waits for them, and re-layouts  6.56 us (4%)
  other arithmetic  2.28 us (1%)
    all_to_all x5, starting transfers between devices, swap(): return lax.all_to_all(x, axis, 0, 0, axis_index_groups=within, tiled=True)  53.6 us
    all_to_all x5, waiting for transfers between devices, swap(): return lax.all_to_all(x, axis, 0, 0, axis_index_groups=within, tiled=True)  42.2 us
    all_to_all x1, blocking collectives, swap(): return lax.all_to_all(x, axis, 0, 0, axis_index_groups=within, tiled=True)  17.8 us
    ppermute x6, starting transfers between devices, partner(): return lax.ppermute(x, 'hid', [(i, i ^ 1) for i in range(n_hid)])  12.6 us
    ppermute x3, starting transfers between devices, shards(): in_blocks.append(lax.ppermute(in_block, 'hid', pairs))  10.5 us
    pallas_call x8, Pallas kernels, local(): pl.pallas_call(body, out_shape=out_shape, in_specs=[pl.BlockSpec(memory_s...  9.37 us
    ppermute x3, waiting for transfers between devices, shards(): in_blocks.append(lax.ppermute(in_block, 'hid', pairs))  6.49 us
    unnamed x31, local copies, waits for them, and re-layouts  4.35 us
  transfers between devices with their start and end apart: 14, of which 8 were waited for; matrix products, arithmetic and copies ran while one was open for 2% of the time, Pallas kernels for 2%

profile of v4, /device:TPU:4, one launch (start us, length us, event | category | flops | bytes accessed | tf_op | source)
XLA Modules:
  0.0 164.0 jit_solution(15317932430249283873)
XLA Ops:
  2.7 28.5 %all-to-all-start = ((bf16[8,8,1536]{2,1,0:T(8,128)(2,1)}), bf16[8,8,1536]{2,1,0:T(8,128)(2,1)S(1)}, u32[]{:S(2)}, u32[]{:S(2)}) async-start(bf16[8,8,1536]{2,1,0:T(8,128)(2,1)} %shard_map.94), calls=%async_computation | async-start | bytes 393216 | tf_op jit(solution)/shard_map/all_to_all | solution.py:39
  31.5 1.9 %collective-permute-start = (bf16[384,768]{1,0:T(8,128)(2,1)S(1)}, bf16[384,768]{1,0:T(8,128)(2,1)}, u32[]{:S(2)}, u32[]{:S(2)}) collective-permute-start(bf16[384,768]{1,0:T(8,128)(2,1)S(1)} %get-tuple-element.15.own_ref), channel_id=1, source_target_pairs={{0,16},{16,0},{32,48},{48,32},{64,80},{80,64},{96,112},{112,96},{1... | collective-permute-start | bytes 1769480 | tf_op jit(solution)/shard_map/ppermute | solution.py:137
  35.0 2.4 %collective-permute-start.1 = (bf16[768,384]{1,0:T(8,128)(2,1)S(1)}, bf16[768,384]{1,0:T(8,128)(2,1)S(1)}, u32[]{:S(2)}, u32[]{:S(2)}) collective-permute-start(bf16[768,384]{1,0:T(8,128)(2,1)S(1)} %mul.62.own_ref), channel_id=1, source_target_pairs={{0,16},{16,0},{32,48},{48,32},{64,80},{80,64},{96,112},{112,96},{1... | collective-permute-start | bytes 1769480 | tf_op jit(solution)/shard_map/ppermute | solution.py:137
  38.2 1.9 %collective-permute-start.2 = (bf16[16,384]{1,0:T(8,128)(2,1)S(1)}, bf16[16,384]{1,0:T(8,128)(2,1)S(1)}, u32[]{:S(2)}, u32[]{:S(2)}) collective-permute-start(bf16[16,384]{1,0:T(8,128)(2,1)S(1)} %get-tuple-element.32), channel_id=1, source_target_pairs={{0,16},{16,0},{32,48},{48,32},{64,80},{80,64},{96,112},{112,96},{1... | collective-permute-start | bytes 36872 | tf_op jit(solution)/shard_map/ppermute | solution.py:137
  41.9 20.7 %all-to-all-done = bf16[8,8,1536]{2,1,0:T(8,128)(2,1)S(1)} async-done(((bf16[8,8,1536]{2,1,0:T(8,128)(2,1)}), bf16[8,8,1536]{2,1,0:T(8,128)(2,1)S(1)}, u32[]{:S(2)}, u32[]{:S(2)}) %all-to-all-start) | async-done | bytes 196640 | tf_op jit(solution)/shard_map/all_to_all | solution.py:39
  63.3 17.8 %all_to_all.30 = bf16[4,64,768]{2,1,0:T(8,128)(2,1)S(1)} all-to-all(bf16[4,64,768]{2,1,0:T(8,128)(2,1)S(1)} %broadcast_in_dim.8), channel_id=1, replica_groups={{0,32,64,96},{16,48,80,112},{128,160,192,224},{144,176,208,240},{256,28..., dimensions={0} | all-to-all | bytes 786432 | tf_op jit(solution)/shard_map/all_to_all | solution.py:39
  81.0 2.5 %shard_map.95 = f32[256,768]{1,0:T(8,128)} custom-call(bf16[256,768]{1,0:T(8,128)(2,1)S(1)} %bitcast.39, bf16[384,768]{1,0:T(8,128)(2,1)S(1)} %get-tuple-element.15.own_ref, bf16[384,768]{1,0:T(8,128)(2,1)} %collective-permute-done.got_ref), custom_call_target="tpu_custom_call" | custom-call | flops 301989888 | bytes 2359296 | tf_op jit(solution)/shard_map/pallas_call | solution.py:44
  83.6 7.4 %all-to-all-start.2 = ((f32[16,16,768]{2,1,0:T(8,128)}), f32[16,16,768]{2,1,0:T(8,128)S(1)}, u32[]{:S(2)}, u32[]{:S(2)}) async-start(f32[16,16,768]{2,1,0:T(8,128)} %bitcast.5), calls=%async_computation.2 | async-start | bytes 1572864 | tf_op jit(solution)/shard_map/all_to_all | solution.py:39
  91.0 2.1 %collective-permute-start.3 = (bf16[64,768]{1,0:T(8,128)(2,1)}, bf16[64,768]{1,0:T(8,128)(2,1)S(1)}, u32[]{:S(2)}, u32[]{:S(2)}) collective-permute-start(bf16[64,768]{1,0:T(8,128)(2,1)} %get-tuple-element.33.refs_0_), channel_id=1, source_target_pairs={{0,32},{16,48},{32,64},{48,80},{64,96},{80,112},{96,0},{112,16},{1... | collective-permute-start | bytes 294920 | tf_op jit(solution)/shard_map/ppermute | solution.py:170
  93.1 3.7 %collective-permute-start.4 = (bf16[64,768]{1,0:T(8,128)(2,1)}, bf16[64,768]{1,0:T(8,128)(2,1)S(1)}, u32[]{:S(2)}, u32[]{:S(2)}) collective-permute-start(bf16[64,768]{1,0:T(8,128)(2,1)} %get-tuple-element.33.refs_0_), channel_id=1, source_target_pairs={{0,64},{16,80},{32,96},{48,112},{64,0},{80,16},{96,32},{112,48},{1... | collective-permute-start | bytes 294920 | tf_op jit(solution)/shard_map/ppermute | solution.py:170
  96.9 2.7 %collective-permute-done.3.refs_1_ = bf16[64,768]{1,0:T(8,128)(2,1)S(1)} collective-permute-done((bf16[64,768]{1,0:T(8,128)(2,1)}, bf16[64,768]{1,0:T(8,128)(2,1)S(1)}, u32[]{:S(2)}, u32[]{:S(2)}) %collective-permute-start.3) | collective-permute-done | bytes 98336 | tf_op jit(solution)/shard_map/ppermute | solution.py:170
  100.2 1.6 %collective-permute-done.4.refs_2_ = bf16[64,768]{1,0:T(8,128)(2,1)S(1)} collective-permute-done((bf16[64,768]{1,0:T(8,128)(2,1)}, bf16[64,768]{1,0:T(8,128)(2,1)S(1)}, u32[]{:S(2)}, u32[]{:S(2)}) %collective-permute-start.4) | collective-permute-done | bytes 98336 | tf_op jit(solution)/shard_map/ppermute | solution.py:170
  104.0 7.4 %all-to-all-start.3 = ((bf16[16,16,768]{2,1,0:T(8,128)(2,1)}), bf16[16,16,768]{2,1,0:T(8,128)(2,1)S(1)}, u32[]{:S(2)}, u32[]{:S(2)}) async-start(bf16[16,16,768]{2,1,0:T(8,128)(2,1)} %shard_map.96), calls=%async_computation.3 | async-start | bytes 786432 | tf_op jit(solution)/shard_map/all_to_all | solution.py:39
  111.4 4.6 %collective-permute-start.5 = (bf16[64,768]{1,0:T(8,128)(2,1)S(1)}, bf16[64,768]{1,0:T(8,128)(2,1)S(1)}, u32[]{:S(2)}, u32[]{:S(2)}) collective-permute-start(bf16[64,768]{1,0:T(8,128)(2,1)S(1)} %copy-done), channel_id=1, source_target_pairs={{0,96},{16,112},{32,0},{48,16},{64,32},{80,48},{96,64},{112,80},{1... | collective-permute-start | bytes 294920 | tf_op jit(solution)/shard_map/ppermute | solution.py:170
  116.0 2.2 %collective-permute-done.5.refs_3_ = bf16[64,768]{1,0:T(8,128)(2,1)S(1)} collective-permute-done((bf16[64,768]{1,0:T(8,128)(2,1)S(1)}, bf16[64,768]{1,0:T(8,128)(2,1)S(1)}, u32[]{:S(2)}, u32[]{:S(2)}) %collective-permute-start.5) | collective-permute-done | bytes 98336 | tf_op jit(solution)/shard_map/ppermute | solution.py:170
  118.5 1.3 shard_map.97
  119.8 5.2 %all-to-all-start.4 = ((bf16[4,64,768]{2,1,0:T(8,128)(2,1)}), bf16[4,64,768]{2,1,0:T(8,128)(2,1)S(1)}, u32[]{:S(2)}, u32[]{:S(2)}) async-start(bf16[4,64,768]{2,1,0:T(8,128)(2,1)} %bitcast.7), calls=%async_computation.4 | async-start | bytes 786432 | tf_op jit(solution)/shard_map/all_to_all | solution.py:39
  126.1 7.8 %all-to-all-done.4.parts_ref = bf16[4,64,768]{2,1,0:T(8,128)(2,1)S(1)} async-done(((bf16[4,64,768]{2,1,0:T(8,128)(2,1)}), bf16[4,64,768]{2,1,0:T(8,128)(2,1)S(1)}, u32[]{:S(2)}, u32[]{:S(2)}) %all-to-all-start.4) | async-done | bytes 393248 | tf_op jit(solution)/shard_map/all_to_all | solution.py:39
  134.6 5.1 %all-to-all-start.5 = ((bf16[8,8,768]{2,1,0:T(8,128)(2,1)}), bf16[8,8,768]{2,1,0:T(8,128)(2,1)S(1)}, u32[]{:S(2)}, u32[]{:S(2)}) async-start(bf16[8,8,768]{2,1,0:T(8,128)(2,1)} %bitcast.8), calls=%async_computation.5 | async-start | bytes 196608 | tf_op jit(solution)/shard_map/all_to_all | solution.py:39
  139.9 2.1 %collective-permute-start.8 = (bf16[256,768]{1,0:T(8,128)(2,1)S(1)}, bf16[256,768]{1,0:T(8,128)(2,1)S(1)}, u32[]{:S(2)}, u32[]{:S(2)}) collective-permute-start(bf16[256,768]{1,0:T(8,128)(2,1)S(1)} %bitcast.40), channel_id=1, source_target_pairs={{0,16},{16,0},{32,48},{48,32},{64,80},{80,64},{96,112},{112,96},{1... | collective-permute-start | bytes 1179656 | tf_op jit(solution)/shard_map/ppermute | solution.py:137
  142.6 2.4 %collective-permute-start.6 = (bf16[256,768]{1,0:T(8,128)(2,1)S(1)}, bf16[256,768]{1,0:T(8,128)(2,1)S(1)}, u32[]{:S(2)}, u32[]{:S(2)}) collective-permute-start(bf16[256,768]{1,0:T(8,128)(2,1)S(1)} %shard_map.100.refs_0_), channel_id=1, source_target_pairs={{0,16},{16,0},{32,48},{48,32},{64,80},{80,64},{96,112},{112,96},{1... | collective-permute-start | bytes 1179656 | tf_op jit(solution)/shard_map/ppermute | solution.py:137
  145.0 1.9 %collective-permute-start.7 = (bf16[256,384]{1,0:T(8,128)(2,1)S(1)}, bf16[256,384]{1,0:T(8,128)(2,1)S(1)}, u32[]{:S(2)}, u32[]{:S(2)}) collective-permute-start(bf16[256,384]{1,0:T(8,128)(2,1)S(1)} %get-tuple-element.29), channel_id=1, source_target_pairs={{0,16},{16,0},{32,48},{48,32},{64,80},{80,64},{96,112},{112,96},{1... | collective-permute-start | bytes 589832 | tf_op jit(solution)/shard_map/ppermute | solution.py:137
  148.6 1.4 shard_map.101
  150.0 13.4 %all-to-all-done.5.parts_ref = bf16[8,8,768]{2,1,0:T(8,128)(2,1)S(1)} async-done(((bf16[8,8,768]{2,1,0:T(8,128)(2,1)}), bf16[8,8,768]{2,1,0:T(8,128)(2,1)S(1)}, u32[]{:S(2)}, u32[]{:S(2)}) %all-to-all-start.5) | async-done | bytes 98336 | tf_op jit(solution)/shard_map/all_to_all | solution.py:39
  (62 shorter events, 14.9 us)
Async XLA Ops:
  2.0 29.2 %copy-start.13 = (s32[3,6]{1,0:T(4,128)S(1)}, s32[3,6]{1,0:T(4,128)}, u32[]{:S(2)}) copy-start(s32[3,6]{1,0:T(4,128)} %param.13) | copy-start | bytes 220
  2.7 28.7 %copy-start.11 = (bf16[384,768]{1,0:T(8,128)(2,1)S(1)}, bf16[384,768]{1,0:T(8,128)(2,1)}, u32[]{:S(2)}) copy-start(bf16[384,768]{1,0:T(8,128)(2,1)} %param.11) | copy-start | bytes 1769476
  2.7 59.9 %all-to-all-start = ((bf16[8,8,1536]{2,1,0:T(8,128)(2,1)}), bf16[8,8,1536]{2,1,0:T(8,128)(2,1)S(1)}, u32[]{:S(2)}, u32[]{:S(2)}) async-start(bf16[8,8,1536]{2,1,0:T(8,128)(2,1)} %shard_map.94), calls=%async_computation | async-start | bytes 393216 | tf_op jit(solution)/shard_map/all_to_all | solution.py:39
  31.4 2.0 %copy-start.14 = (s32[6,3]{0,1:T(4,128)S(1)}, s32[6,3]{0,1:T(4,128)}, u32[]{:S(2)}) copy-start(s32[6,3]{0,1:T(4,128)} %param.12) | copy-start | bytes 220
  31.5 10.4 %collective-permute-start = (bf16[384,768]{1,0:T(8,128)(2,1)S(1)}, bf16[384,768]{1,0:T(8,128)(2,1)}, u32[]{:S(2)}, u32[]{:S(2)}) collective-permute-start(bf16[384,768]{1,0:T(8,128)(2,1)S(1)} %get-tuple-element.15.own_ref), channel_id=1, source_target_pairs={{0,16},{16,0},{32,48},{48,32},{64,80},{80,64},{96,112},{112,96},{1... | collective-permute-start | bytes 1769480 | tf_op jit(solution)/shard_map/ppermute | solution.py:137
  33.7 1.1 copy-start.12
  35.0 6.9 %collective-permute-start.1 = (bf16[768,384]{1,0:T(8,128)(2,1)S(1)}, bf16[768,384]{1,0:T(8,128)(2,1)S(1)}, u32[]{:S(2)}, u32[]{:S(2)}) collective-permute-start(bf16[768,384]{1,0:T(8,128)(2,1)S(1)} %mul.62.own_ref), channel_id=1, source_target_pairs={{0,16},{16,0},{32,48},{48,32},{64,80},{80,64},{96,112},{112,96},{1... | collective-permute-start | bytes 1769480 | tf_op jit(solution)/shard_map/ppermute | solution.py:137
  38.2 3.1 %collective-permute-start.2 = (bf16[16,384]{1,0:T(8,128)(2,1)S(1)}, bf16[16,384]{1,0:T(8,128)(2,1)S(1)}, u32[]{:S(2)}, u32[]{:S(2)}) collective-permute-start(bf16[16,384]{1,0:T(8,128)(2,1)S(1)} %get-tuple-element.32), channel_id=1, source_target_pairs={{0,16},{16,0},{32,48},{48,32},{64,80},{80,64},{96,112},{112,96},{1... | collective-permute-start | bytes 36872 | tf_op jit(solution)/shard_map/ppermute | solution.py:137
  83.6 18.9 %all-to-all-start.2 = ((f32[16,16,768]{2,1,0:T(8,128)}), f32[16,16,768]{2,1,0:T(8,128)S(1)}, u32[]{:S(2)}, u32[]{:S(2)}) async-start(f32[16,16,768]{2,1,0:T(8,128)} %bitcast.5), calls=%async_computation.2 | async-start | bytes 1572864 | tf_op jit(solution)/shard_map/all_to_all | solution.py:39
  91.0 8.5 %collective-permute-start.3 = (bf16[64,768]{1,0:T(8,128)(2,1)}, bf16[64,768]{1,0:T(8,128)(2,1)S(1)}, u32[]{:S(2)}, u32[]{:S(2)}) collective-permute-start(bf16[64,768]{1,0:T(8,128)(2,1)} %get-tuple-element.33.refs_0_), channel_id=1, source_target_pairs={{0,32},{16,48},{32,64},{48,80},{64,96},{80,112},{96,0},{112,16},{1... | collective-permute-start | bytes 294920 | tf_op jit(solution)/shard_map/ppermute | solution.py:170
  93.1 8.7 %collective-permute-start.4 = (bf16[64,768]{1,0:T(8,128)(2,1)}, bf16[64,768]{1,0:T(8,128)(2,1)S(1)}, u32[]{:S(2)}, u32[]{:S(2)}) collective-permute-start(bf16[64,768]{1,0:T(8,128)(2,1)} %get-tuple-element.33.refs_0_), channel_id=1, source_target_pairs={{0,64},{16,80},{32,96},{48,112},{64,0},{80,16},{96,32},{112,48},{1... | collective-permute-start | bytes 294920 | tf_op jit(solution)/shard_map/ppermute | solution.py:170
  104.0 7.4 %copy-start = (bf16[64,768]{1,0:T(8,128)(2,1)S(1)}, bf16[64,768]{1,0:T(8,128)(2,1)}, u32[]{:S(2)}) copy-start(bf16[64,768]{1,0:T(8,128)(2,1)} %get-tuple-element.33.refs_0_) | copy-start | bytes 294916
  104.0 14.4 %all-to-all-start.3 = ((bf16[16,16,768]{2,1,0:T(8,128)(2,1)}), bf16[16,16,768]{2,1,0:T(8,128)(2,1)S(1)}, u32[]{:S(2)}, u32[]{:S(2)}) async-start(bf16[16,16,768]{2,1,0:T(8,128)(2,1)} %shard_map.96), calls=%async_computation.3 | async-start | bytes 786432 | tf_op jit(solution)/shard_map/all_to_all | solution.py:39
  111.4 6.8 %collective-permute-start.5 = (bf16[64,768]{1,0:T(8,128)(2,1)S(1)}, bf16[64,768]{1,0:T(8,128)(2,1)S(1)}, u32[]{:S(2)}, u32[]{:S(2)}) collective-permute-start(bf16[64,768]{1,0:T(8,128)(2,1)S(1)} %copy-done), channel_id=1, source_target_pairs={{0,96},{16,112},{32,0},{48,16},{64,32},{80,48},{96,64},{112,80},{1... | collective-permute-start | bytes 294920 | tf_op jit(solution)/shard_map/ppermute | solution.py:170
  118.2 1.6 copy-start.7
  119.8 14.1 %all-to-all-start.4 = ((bf16[4,64,768]{2,1,0:T(8,128)(2,1)}), bf16[4,64,768]{2,1,0:T(8,128)(2,1)S(1)}, u32[]{:S(2)}, u32[]{:S(2)}) async-start(bf16[4,64,768]{2,1,0:T(8,128)(2,1)} %bitcast.7), calls=%async_computation.4 | async-start | bytes 786432 | tf_op jit(solution)/shard_map/all_to_all | solution.py:39
  134.6 28.8 %all-to-all-start.5 = ((bf16[8,8,768]{2,1,0:T(8,128)(2,1)}), bf16[8,8,768]{2,1,0:T(8,128)(2,1)S(1)}, u32[]{:S(2)}, u32[]{:S(2)}) async-start(bf16[8,8,768]{2,1,0:T(8,128)(2,1)} %bitcast.8), calls=%async_computation.5 | async-start | bytes 196608 | tf_op jit(solution)/shard_map/all_to_all | solution.py:39
  139.8 2.2 %copy-start.1 = (bf16[64,768]{1,0:T(8,128)(2,1)S(1)}, bf16[64,768]{1,0:T(8,128)(2,1)}, u32[]{:S(2)}) copy-start(bf16[64,768]{1,0:T(8,128)(2,1)} %get-tuple-element.33.refs_0_) | copy-start | bytes 294916
  139.8 2.2 %copy-start.4 = (bf16[64,768]{1,0:T(8,128)(2,1)S(1)}, bf16[64,768]{1,0:T(8,128)(2,1)}, u32[]{:S(2)}) copy-start(bf16[64,768]{1,0:T(8,128)(2,1)} %copy-done.3) | copy-start | bytes 294916
  139.8 2.2 %copy-start.6 = (bf16[64,768]{1,0:T(8,128)(2,1)S(1)}, bf16[64,768]{1,0:T(8,128)(2,1)}, u32[]{:S(2)}) copy-start(bf16[64,768]{1,0:T(8,128)(2,1)} %copy-done.5) | copy-start | bytes 294916
  139.9 2.2 %copy-start.8 = (bf16[64,768]{1,0:T(8,128)(2,1)S(1)}, bf16[64,768]{1,0:T(8,128)(2,1)}, u32[]{:S(2)}) copy-start(bf16[64,768]{1,0:T(8,128)(2,1)} %copy-done.7) | copy-start | bytes 294916
  139.9 7.4 %collective-permute-start.8 = (bf16[256,768]{1,0:T(8,128)(2,1)S(1)}, bf16[256,768]{1,0:T(8,128)(2,1)S(1)}, u32[]{:S(2)}, u32[]{:S(2)}) collective-permute-start(bf16[256,768]{1,0:T(8,128)(2,1)S(1)} %bitcast.40), channel_id=1, source_target_pairs={{0,16},{16,0},{32,48},{48,32},{64,80},{80,64},{96,112},{112,96},{1... | collective-permute-start | bytes 1179656 | tf_op jit(solution)/shard_map/ppermute | solution.py:137
  142.6 6.0 %collective-permute-start.6 = (bf16[256,768]{1,0:T(8,128)(2,1)S(1)}, bf16[256,768]{1,0:T(8,128)(2,1)S(1)}, u32[]{:S(2)}, u32[]{:S(2)}) collective-permute-start(bf16[256,768]{1,0:T(8,128)(2,1)S(1)} %shard_map.100.refs_0_), channel_id=1, source_target_pairs={{0,16},{16,0},{32,48},{48,32},{64,80},{80,64},{96,112},{112,96},{1... | collective-permute-start | bytes 1179656 | tf_op jit(solution)/shard_map/ppermute | solution.py:137
  145.0 3.6 %collective-permute-start.7 = (bf16[256,384]{1,0:T(8,128)(2,1)S(1)}, bf16[256,384]{1,0:T(8,128)(2,1)S(1)}, u32[]{:S(2)}, u32[]{:S(2)}) collective-permute-start(bf16[256,384]{1,0:T(8,128)(2,1)S(1)} %get-tuple-element.29), channel_id=1, source_target_pairs={{0,16},{16,0},{32,48},{48,32},{64,80},{80,64},{96,112},{112,96},{1... | collective-permute-start | bytes 589832 | tf_op jit(solution)/shard_map/ppermute | solution.py:137
  (5 other events, 3.5 us)

commit v5 on v4

--- a/solution.py
+++ b/solution.py
@@ -60,13 +60,6 @@
     out_ref[:, width:] = lax.dot_general(
         rows, got_ref[...], CONTRACT_LAST, preferred_element_type=jnp.float32
     )
-
-
-def spread_body(left_ref, right_ref, out_ref):
-    width = left_ref.shape[1]
-    for copy in range(out_ref.shape[0]):
-        out_ref[copy, :, :width] = left_ref[...]
-        out_ref[copy, :, width:] = right_ref[...]
 
 
 def place_body(spots_ref, *refs):
@@ -150,8 +143,8 @@
     pre_other = lax.dynamic_index_in_dim(mine, other, 1, keepdims=False).reshape(share, width)
     _, slope = gelu_parts(jnp.concatenate([pre_own, partner(pre_other)], axis=1))
 
-    both = local(spread_body, struct((far, own, 2 * features), jnp.bfloat16), 0, out_grad, inputs)
-    rows = swap(both, "hid", far_groups)
+    both = jnp.concatenate([out_grad, inputs], axis=1)
+    rows = swap(jnp.broadcast_to(both[None], (far, own, 2 * features)), "hid", far_groups)
     rows, w_out_got, w_in_got, slope, w_in_eff, w_out_eff = lax.optimization_barrier(
         (rows, w_out_got, w_in_got, slope, w_in_eff, w_out_eff)
     )
@@ -161,13 +154,16 @@
     rows = swap(rows, "hid", near_groups).reshape(half, features)
 
     n = lax.axis_index("hid") // 2 % NEAR
-    spots = jnp.stack([(n + NEAR - step) % NEAR for step in range(NEAR)]).astype(jnp.int32)
-    in_blocks = [in_block]
-    for step in range(1, NEAR):
-        pairs = [
-            (i, i - 2 * (i // 2 % NEAR) + 2 * ((i // 2 + step) % NEAR)) for i in range(n_hid)
-        ]
-        in_blocks.append(lax.ppermute(in_block, "hid", pairs))
+    steps = [0, 1, NEAR - 1, 2]
+    spots = jnp.stack([(n + NEAR - step) % NEAR for step in steps]).astype(jnp.int32)
+
+    def shifted(step):
+        step = step - NEAR if step == NEAR - 1 else step
+        pairs = [(i, (i + 2 * step) % n_hid) for i in range(n_hid)]
+        return lax.ppermute(in_block, "hid", pairs)
+
+    in_blocks = [in_block] + [shifted(step) for step in steps[1:]]
+
     partial = local(
         act_grad_body,
         struct((half, 2 * width), jnp.float32),
@@ -177,7 +173,6 @@
         w_out_got,
     )
     parts = swap(partial.reshape(n_row, share, 2 * width), "row")
-    parts, *in_blocks[1:3] = lax.optimization_barrier((parts, *in_blocks[1:3]))
     copies = local(
         delta_body,
         struct((n_row, share, 2 * width), jnp.bfloat16),
@@ -186,7 +181,20 @@
         slope,
     )
     delta = swap(copies, "row").reshape(half, 2 * width)
-    delta, *in_blocks[3:] = lax.optimization_barrier((delta, *in_blocks[3:]))
+
+    back = local(
+        in_grad_body,
+        struct((half, features), jnp.bfloat16),
+        4 * half * features * width,
+        delta,
+        w_in_eff,
+        w_in_got,
+    )
+    back = swap(back.reshape(NEAR, far * own, features), "hid", near_groups)
+    back, in_blocks[1] = lax.optimization_barrier((back, in_blocks[1]))
+    back = local(sum_body, struct((far * own, features), jnp.bfloat16), back.size, back)
+    back = swap(back.reshape(far, own, features), "hid", far_groups)
+    in_grad = local(sum_body, struct((own, features), jnp.bfloat16), back.size, back)
 
     in_rows = pl.pallas_call(
         place_body,
@@ -200,19 +208,6 @@
         ),
     )(spots, *in_blocks)
 
-    back = local(
-        in_grad_body,
-        struct((half, features), jnp.bfloat16),
-        4 * half * features * width,
-        delta,
-        w_in_eff,
-        w_in_got,
-    )
-    back = swap(back.reshape(NEAR, far * own, features), "hid", near_groups)
-    back = local(sum_body, struct((far * own, features), jnp.bfloat16), back.size, back)
-    back = swap(back.reshape(far, own, features), "hid", far_groups)
-    in_grad = local(sum_body, struct((own, features), jnp.bfloat16), back.size, back)
-
     scale = 1.0 / math.sqrt(tokens)
     w_in_grad = local(
         lambda *refs: w_in_grad_body(scale, *refs),

time: 165 us -> 160 us (0.970)
  the two profiles are of different devices: /device:TPU:4 before, /device:TPU:1 now
where the time goes in v5:
time: 160 us; the launch traced here: 159 us
  starting transfers between devices  73.8 us (46%)
  blocking collectives  50 us (31%)
  waiting for transfers between devices  19.7 us (12%)
  Pallas kernels  7.63 us (5%)
  other arithmetic  3.47 us (2%)
  local copies, waits for them, and re-layouts  3.18 us (2%)
    all_to_all x3, blocking collectives, swap(): return lax.all_to_all(x, axis, 0, 0, axis_index_groups=within, tiled=True)  50 us
    all_to_all x3, starting transfers between devices, swap(): return lax.all_to_all(x, axis, 0, 0, axis_index_groups=within, tiled=True)  38.8 us
    ppermute x6, starting transfers between devices, partner(): return lax.ppermute(x, 'hid', [(i, i ^ 1) for i in range(n_hid)])  21.7 us
    all_to_all x3, waiting for transfers between devices, swap(): return lax.all_to_all(x, axis, 0, 0, axis_index_groups=within, tiled=True)  16.8 us
    ppermute x3, starting transfers between devices, shifted(): return lax.ppermute(in_block, 'hid', pairs)  13.3 us
    pallas_call x7, Pallas kernels, local(): pl.pallas_call(body, out_shape=out_shape, in_specs=[pl.BlockSpec(memory_s...  7.06 us
  transfers between devices with their start and end apart: 12, of which 4 were waited for; matrix products, arithmetic and copies ran while one was open for 3% of the time, Pallas kernels for 2%

profile of v5, /device:TPU:1, one launch (start us, length us, event | category | flops | bytes accessed | tf_op | source)
XLA Modules:
  0.0 158.7 jit_solution(9989540817617998336)
XLA Ops:
  2.1 29.0 %all-to-all-start = ((bf16[8,8,1536]{2,1,0:T(8,128)(2,1)}), bf16[8,8,1536]{2,1,0:T(8,128)(2,1)S(1)}, u32[]{:S(2)}, u32[]{:S(2)}) async-start(bf16[8,8,1536]{2,1,0:T(8,128)(2,1)} %broadcast_in_dim.8), calls=%async_computation | async-start | bytes 393216 | tf_op jit(solution)/shard_map/all_to_all | solution.py:39
  31.4 2.9 %collective-permute-start = (bf16[384,768]{1,0:T(8,128)(2,1)S(1)}, bf16[384,768]{1,0:T(8,128)(2,1)S(1)}, u32[]{:S(2)}, u32[]{:S(2)}) collective-permute-start(bf16[384,768]{1,0:T(8,128)(2,1)S(1)} %get-tuple-element.12.own_ref), channel_id=1, source_target_pairs={{0,16},{16,0},{32,48},{48,32},{64,80},{80,64},{96,112},{112,96},{1... | collective-permute-start | bytes 1769480 | tf_op jit(solution)/shard_map/ppermute | solution.py:130
  34.9 1.2 mul.62.own_ref
  36.1 1.9 %collective-permute-start.1 = (bf16[768,384]{1,0:T(8,128)(2,1)S(1)}, bf16[768,384]{1,0:T(8,128)(2,1)}, u32[]{:S(2)}, u32[]{:S(2)}) collective-permute-start(bf16[768,384]{1,0:T(8,128)(2,1)S(1)} %mul.62.own_ref), channel_id=1, source_target_pairs={{0,16},{16,0},{32,48},{48,32},{64,80},{80,64},{96,112},{112,96},{1... | collective-permute-start | bytes 1769480 | tf_op jit(solution)/shard_map/ppermute | solution.py:130
  38.8 2.4 %collective-permute-start.2 = (bf16[16,384]{1,0:T(8,128)(2,1)S(1)}, bf16[16,384]{1,0:T(8,128)(2,1)S(1)}, u32[]{:S(2)}, u32[]{:S(2)}) collective-permute-start(bf16[16,384]{1,0:T(8,128)(2,1)S(1)} %get-tuple-element.26), channel_id=1, source_target_pairs={{0,16},{16,0},{32,48},{48,32},{64,80},{80,64},{96,112},{112,96},{1... | collective-permute-start | bytes 36872 | tf_op jit(solution)/shard_map/ppermute | solution.py:130
  41.2 0.8 collective-permute-done.2
  42.9 15.6 %all-to-all-done = bf16[8,8,1536]{2,1,0:T(8,128)(2,1)S(1)} async-done(((bf16[8,8,1536]{2,1,0:T(8,128)(2,1)}), bf16[8,8,1536]{2,1,0:T(8,128)(2,1)S(1)}, u32[]{:S(2)}, u32[]{:S(2)}) %all-to-all-start) | async-done | bytes 196640 | tf_op jit(solution)/shard_map/all_to_all | solution.py:39
  58.6 20.6 %all_to_all.30 = bf16[4,64,768]{2,1,0:T(8,128)(2,1)S(1)} all-to-all(bf16[4,64,768]{2,1,0:T(8,128)(2,1)S(1)} %broadcast_in_dim.11), channel_id=1, replica_groups={{0,32,64,96},{16,48,80,112},{128,160,192,224},{144,176,208,240},{256,28..., dimensions={0} | all-to-all | bytes 786432 | tf_op jit(solution)/shard_map/all_to_all | solution.py:39
  79.7 17.7 %all_to_all.31.parts_ref = f32[16,16,768]{2,1,0:T(8,128)S(1)} all-to-all(f32[16,16,768]{2,1,0:T(8,128)S(1)} %bitcast.44), channel_id=1, replica_groups=mesh['hid'=64,'row'=16] {'row'}, dimensions={0} | all-to-all | bytes 1572864 | tf_op jit(solution)/shard_map/all_to_all | solution.py:39
  97.4 11.8 %all_to_all.32 = bf16[16,16,768]{2,1,0:T(8,128)(2,1)S(1)} all-to-all(bf16[16,16,768]{2,1,0:T(8,128)(2,1)S(1)} %shard_map.95), channel_id=1, replica_groups=mesh['hid'=64,'row'=16] {'row'}, dimensions={0} | all-to-all | bytes 786432 | tf_op jit(solution)/shard_map/all_to_all | solution.py:39
  109.2 2.4 %shard_map.96 = bf16[256,768]{1,0:T(8,128)(2,1)} custom-call(bf16[256,768]{1,0:T(8,128)(2,1)S(1)} %bitcast.42, bf16[768,384]{1,0:T(8,128)(2,1)S(1)} %mul.62.own_ref, bf16[768,384]{1,0:T(8,128)(2,1)} %collective-permute-done.1.got_ref), custom_call_target="tpu_custom_call" | custom-call | flops 301989888 | bytes 1966080 | tf_op jit(solution)/shard_map/pallas_call | solution.py:44
  111.6 4.3 %all-to-all-start.4 = ((bf16[4,64,768]{2,1,0:T(8,128)(2,1)}), bf16[4,64,768]{2,1,0:T(8,128)(2,1)S(1)}, u32[]{:S(2)}, u32[]{:S(2)}) async-start(bf16[4,64,768]{2,1,0:T(8,128)(2,1)} %bitcast.7), calls=%async_computation.4 | async-start | bytes 786432 | tf_op jit(solution)/shard_map/all_to_all | solution.py:39
  115.9 3.4 %collective-permute-start.3 = (bf16[64,768]{1,0:T(8,128)(2,1)S(1)}, bf16[64,768]{1,0:T(8,128)(2,1)S(1)}, u32[]{:S(2)}, u32[]{:S(2)}) collective-permute-start(bf16[64,768]{1,0:T(8,128)(2,1)S(1)} %get-tuple-element.27.refs_0_), channel_id=1, source_target_pairs={{0,32},{16,48},{32,64},{48,80},{64,96},{80,112},{96,128},{112,144}... | collective-permute-start | bytes 294920 | tf_op jit(solution)/shard_map/ppermute | solution.py:163
  119.2 1.1 convert_bitcast_fusion
  120.4 2.0 %collective-permute-done.3.refs_1_ = bf16[64,768]{1,0:T(8,128)(2,1)S(1)} collective-permute-done((bf16[64,768]{1,0:T(8,128)(2,1)S(1)}, bf16[64,768]{1,0:T(8,128)(2,1)S(1)}, u32[]{:S(2)}, u32[]{:S(2)}) %collective-permute-start.3) | collective-permute-done | bytes 98336 | tf_op jit(solution)/shard_map/ppermute | solution.py:163
  122.4 1.2 all-to-all-done.4.parts_ref
  124.3 5.5 %all-to-all-start.5 = ((bf16[8,8,768]{2,1,0:T(8,128)(2,1)}), bf16[8,8,768]{2,1,0:T(8,128)(2,1)S(1)}, u32[]{:S(2)}, u32[]{:S(2)}) async-start(bf16[8,8,768]{2,1,0:T(8,128)(2,1)} %bitcast.8), calls=%async_computation.5 | async-start | bytes 196608 | tf_op jit(solution)/shard_map/all_to_all | solution.py:39
  129.9 8.0 %collective-permute-start.4 = (bf16[64,768]{1,0:T(8,128)(2,1)S(1)}, bf16[64,768]{1,0:T(8,128)(2,1)S(1)}, u32[]{:S(2)}, u32[]{:S(2)}) collective-permute-start(bf16[64,768]{1,0:T(8,128)(2,1)S(1)} %get-tuple-element.27.refs_0_), channel_id=1, source_target_pairs={{0,992},{16,1008},{32,0},{48,16},{64,32},{80,48},{96,64},{112,80},... | collective-permute-start | bytes 294920 | tf_op jit(solution)/shard_map/ppermute | solution.py:163
  137.9 1.9 %collective-permute-start.5 = (bf16[64,768]{1,0:T(8,128)(2,1)S(1)}, bf16[64,768]{1,0:T(8,128)(2,1)S(1)}, u32[]{:S(2)}, u32[]{:S(2)}) collective-permute-start(bf16[64,768]{1,0:T(8,128)(2,1)S(1)} %get-tuple-element.27.refs_0_), channel_id=1, source_target_pairs={{0,64},{16,80},{32,96},{48,112},{64,128},{80,144},{96,160},{112,17... | collective-permute-start | bytes 294920 | tf_op jit(solution)/shard_map/ppermute | solution.py:163
  139.9 6.4 %collective-permute-start.8 = (bf16[256,768]{1,0:T(8,128)(2,1)S(1)}, bf16[256,768]{1,0:T(8,128)(2,1)S(1)}, u32[]{:S(2)}, u32[]{:S(2)}) collective-permute-start(bf16[256,768]{1,0:T(8,128)(2,1)S(1)} %bitcast.40), channel_id=1, source_target_pairs={{0,16},{16,0},{32,48},{48,32},{64,80},{80,64},{96,112},{112,96},{1... | collective-permute-start | bytes 1179656 | tf_op jit(solution)/shard_map/ppermute | solution.py:130
  146.4 1.9 %collective-permute-start.7 = (bf16[256,384]{1,0:T(8,128)(2,1)S(1)}, bf16[256,384]{1,0:T(8,128)(2,1)S(1)}, u32[]{:S(2)}, u32[]{:S(2)}) collective-permute-start(bf16[256,384]{1,0:T(8,128)(2,1)S(1)} %get-tuple-element.23), channel_id=1, source_target_pairs={{0,16},{16,0},{32,48},{48,32},{64,80},{80,64},{96,112},{112,96},{1... | collective-permute-start | bytes 589832 | tf_op jit(solution)/shard_map/ppermute | solution.py:130
  148.9 6.1 %collective-permute-start.6 = (bf16[256,768]{1,0:T(8,128)(2,1)S(1)}, bf16[256,768]{1,0:T(8,128)(2,1)S(1)}, u32[]{:S(2)}, u32[]{:S(2)}) collective-permute-start(bf16[256,768]{1,0:T(8,128)(2,1)S(1)} %shard_map.99.refs_0_), channel_id=1, source_target_pairs={{0,16},{16,0},{32,48},{48,32},{64,80},{80,64},{96,112},{112,96},{1... | collective-permute-start | bytes 1179656 | tf_op jit(solution)/shard_map/ppermute | solution.py:130
  155.4 1.3 shard_map.101
  156.7 1.4 shard_map.100
  (41 shorter events, 6.9 us)
Async XLA Ops:
  1.4 29.7 %copy-start.3 = (s32[3,6]{1,0:T(4,128)S(1)}, s32[3,6]{1,0:T(4,128)}, u32[]{:S(2)}) copy-start(s32[3,6]{1,0:T(4,128)} %param.13) | copy-start | bytes 220
  2.0 29.2 %copy-start.2 = (bf16[384,768]{1,0:T(8,128)(2,1)S(1)}, bf16[384,768]{1,0:T(8,128)(2,1)}, u32[]{:S(2)}) copy-start(bf16[384,768]{1,0:T(8,128)(2,1)} %param.11) | copy-start | bytes 1769476
  2.1 56.5 %all-to-all-start = ((bf16[8,8,1536]{2,1,0:T(8,128)(2,1)}), bf16[8,8,1536]{2,1,0:T(8,128)(2,1)S(1)}, u32[]{:S(2)}, u32[]{:S(2)}) async-start(bf16[8,8,1536]{2,1,0:T(8,128)(2,1)} %broadcast_in_dim.8), calls=%async_computation | async-start | bytes 393216 | tf_op jit(solution)/shard_map/all_to_all | solution.py:39
  31.3 3.0 %copy-start.4 = (s32[6,3]{0,1:T(4,128)S(1)}, s32[6,3]{0,1:T(4,128)}, u32[]{:S(2)}) copy-start(s32[6,3]{0,1:T(4,128)} %param.12) | copy-start | bytes 220
  31.4 10.7 %collective-permute-start = (bf16[384,768]{1,0:T(8,128)(2,1)S(1)}, bf16[384,768]{1,0:T(8,128)(2,1)S(1)}, u32[]{:S(2)}, u32[]{:S(2)}) collective-permute-start(bf16[384,768]{1,0:T(8,128)(2,1)S(1)} %get-tuple-element.12.own_ref), channel_id=1, source_target_pairs={{0,16},{16,0},{32,48},{48,32},{64,80},{80,64},{96,112},{112,96},{1... | collective-permute-start | bytes 1769480 | tf_op jit(solution)/shard_map/ppermute | solution.py:130
  36.1 6.8 %collective-permute-start.1 = (bf16[768,384]{1,0:T(8,128)(2,1)S(1)}, bf16[768,384]{1,0:T(8,128)(2,1)}, u32[]{:S(2)}, u32[]{:S(2)}) collective-permute-start(bf16[768,384]{1,0:T(8,128)(2,1)S(1)} %mul.62.own_ref), channel_id=1, source_target_pairs={{0,16},{16,0},{32,48},{48,32},{64,80},{80,64},{96,112},{112,96},{1... | collective-permute-start | bytes 1769480 | tf_op jit(solution)/shard_map/ppermute | solution.py:130
  38.8 3.2 %collective-permute-start.2 = (bf16[16,384]{1,0:T(8,128)(2,1)S(1)}, bf16[16,384]{1,0:T(8,128)(2,1)S(1)}, u32[]{:S(2)}, u32[]{:S(2)}) collective-permute-start(bf16[16,384]{1,0:T(8,128)(2,1)S(1)} %get-tuple-element.26), channel_id=1, source_target_pairs={{0,16},{16,0},{32,48},{48,32},{64,80},{80,64},{96,112},{112,96},{1... | collective-permute-start | bytes 36872 | tf_op jit(solution)/shard_map/ppermute | solution.py:130
  42.1 0.8 copy-start
  58.5 20.6 %copy-start.1 = (bf16[384,768]{1,0:T(8,128)(2,1)S(1)}, bf16[384,768]{1,0:T(8,128)(2,1)}, u32[]{:S(2)}) copy-start(bf16[384,768]{1,0:T(8,128)(2,1)} %copy-done) | copy-start | bytes 1769476
  111.6 12.0 %all-to-all-start.4 = ((bf16[4,64,768]{2,1,0:T(8,128)(2,1)}), bf16[4,64,768]{2,1,0:T(8,128)(2,1)S(1)}, u32[]{:S(2)}, u32[]{:S(2)}) async-start(bf16[4,64,768]{2,1,0:T(8,128)(2,1)} %bitcast.7), calls=%async_computation.4 | async-start | bytes 786432 | tf_op jit(solution)/shard_map/all_to_all | solution.py:39
  115.9 6.6 %collective-permute-start.3 = (bf16[64,768]{1,0:T(8,128)(2,1)S(1)}, bf16[64,768]{1,0:T(8,128)(2,1)S(1)}, u32[]{:S(2)}, u32[]{:S(2)}) collective-permute-start(bf16[64,768]{1,0:T(8,128)(2,1)S(1)} %get-tuple-element.27.refs_0_), channel_id=1, source_target_pairs={{0,32},{16,48},{32,64},{48,80},{64,96},{80,112},{96,128},{112,144}... | collective-permute-start | bytes 294920 | tf_op jit(solution)/shard_map/ppermute | solution.py:163
  124.3 33.8 %all-to-all-start.5 = ((bf16[8,8,768]{2,1,0:T(8,128)(2,1)}), bf16[8,8,768]{2,1,0:T(8,128)(2,1)S(1)}, u32[]{:S(2)}, u32[]{:S(2)}) async-start(bf16[8,8,768]{2,1,0:T(8,128)(2,1)} %bitcast.8), calls=%async_computation.5 | async-start | bytes 196608 | tf_op jit(solution)/shard_map/all_to_all | solution.py:39
  129.9 18.4 %collective-permute-start.4 = (bf16[64,768]{1,0:T(8,128)(2,1)S(1)}, bf16[64,768]{1,0:T(8,128)(2,1)S(1)}, u32[]{:S(2)}, u32[]{:S(2)}) collective-permute-start(bf16[64,768]{1,0:T(8,128)(2,1)S(1)} %get-tuple-element.27.refs_0_), channel_id=1, source_target_pairs={{0,992},{16,1008},{32,0},{48,16},{64,32},{80,48},{96,64},{112,80},... | collective-permute-start | bytes 294920 | tf_op jit(solution)/shard_map/ppermute | solution.py:163
  137.9 10.4 %collective-permute-start.5 = (bf16[64,768]{1,0:T(8,128)(2,1)S(1)}, bf16[64,768]{1,0:T(8,128)(2,1)S(1)}, u32[]{:S(2)}, u32[]{:S(2)}) collective-permute-start(bf16[64,768]{1,0:T(8,128)(2,1)S(1)} %get-tuple-element.27.refs_0_), channel_id=1, source_target_pairs={{0,64},{16,80},{32,96},{48,112},{64,128},{80,144},{96,160},{112,17... | collective-permute-start | bytes 294920 | tf_op jit(solution)/shard_map/ppermute | solution.py:163
  139.9 15.5 %collective-permute-start.8 = (bf16[256,768]{1,0:T(8,128)(2,1)S(1)}, bf16[256,768]{1,0:T(8,128)(2,1)S(1)}, u32[]{:S(2)}, u32[]{:S(2)}) collective-permute-start(bf16[256,768]{1,0:T(8,128)(2,1)S(1)} %bitcast.40), channel_id=1, source_target_pairs={{0,16},{16,0},{32,48},{48,32},{64,80},{80,64},{96,112},{112,96},{1... | collective-permute-start | bytes 1179656 | tf_op jit(solution)/shard_map/ppermute | solution.py:130
  146.4 10.3 %collective-permute-start.7 = (bf16[256,384]{1,0:T(8,128)(2,1)S(1)}, bf16[256,384]{1,0:T(8,128)(2,1)S(1)}, u32[]{:S(2)}, u32[]{:S(2)}) collective-permute-start(bf16[256,384]{1,0:T(8,128)(2,1)S(1)} %get-tuple-element.23), channel_id=1, source_target_pairs={{0,16},{16,0},{32,48},{48,32},{64,80},{80,64},{96,112},{112,96},{1... | collective-permute-start | bytes 589832 | tf_op jit(solution)/shard_map/ppermute | solution.py:130
  148.9 7.8 %collective-permute-start.6 = (bf16[256,768]{1,0:T(8,128)(2,1)S(1)}, bf16[256,768]{1,0:T(8,128)(2,1)S(1)}, u32[]{:S(2)}, u32[]{:S(2)}) collective-permute-start(bf16[256,768]{1,0:T(8,128)(2,1)S(1)} %shard_map.99.refs_0_), channel_id=1, source_target_pairs={{0,16},{16,0},{32,48},{48,32},{64,80},{80,64},{96,112},{112,96},{1... | collective-permute-start | bytes 1179656 | tf_op jit(solution)/shard_map/ppermute | solution.py:130

commit v6 on v5

--- a/solution.py
+++ b/solution.py
@@ -54,12 +54,11 @@
 def act_grad_body(rows_ref, own_ref, got_ref, out_ref):
     width = own_ref.shape[0]
     rows = rows_ref[...]
-    out_ref[:, :width] = lax.dot_general(
-        rows, own_ref[...], CONTRACT_LAST, preferred_element_type=jnp.float32
-    )
-    out_ref[:, width:] = lax.dot_general(
-        rows, got_ref[...], CONTRACT_LAST, preferred_element_type=jnp.float32
-    )
+    for place, weight_ref in ((0, own_ref), (width, got_ref)):
+        partial = lax.dot_general(
+            rows, weight_ref[...], CONTRACT_LAST, preferred_element_type=jnp.float32
+        )
+        out_ref[:, place : place + width] = partial.astype(out_ref.dtype)
 
 
 def place_body(spots_ref, *refs):
@@ -70,9 +69,9 @@
 
 
 def delta_body(parts_ref, slope_ref, out_ref):
-    total = parts_ref[0]
+    total = parts_ref[0].astype(jnp.float32)
     for part in range(1, parts_ref.shape[0]):
-        total = total + parts_ref[part]
+        total = total + parts_ref[part].astype(jnp.float32)
     delta = (total * slope_ref[...]).astype(out_ref.dtype)
     for copy in range(out_ref.shape[0]):
         out_ref[copy] = delta
@@ -143,10 +142,14 @@
     pre_other = lax.dynamic_index_in_dim(mine, other, 1, keepdims=False).reshape(share, width)
     _, slope = gelu_parts(jnp.concatenate([pre_own, partner(pre_other)], axis=1))
 
+    value, _ = gelu_parts(pre_act)
+    act = value.astype(jnp.bfloat16).reshape(placed.shape)
+    act = act.transpose(2, 1, 0, 3, 4).reshape(2, half, width)
+
     both = jnp.concatenate([out_grad, inputs], axis=1)
     rows = swap(jnp.broadcast_to(both[None], (far, own, 2 * features)), "hid", far_groups)
-    rows, w_out_got, w_in_got, slope, w_in_eff, w_out_eff = lax.optimization_barrier(
-        (rows, w_out_got, w_in_got, slope, w_in_eff, w_out_eff)
+    rows, w_out_got, w_in_got, slope, w_in_eff, w_out_eff, act = lax.optimization_barrier(
+        (rows, w_out_got, w_in_got, slope, w_in_eff, w_out_eff, act)
     )
     rows = rows.reshape(far * own, 2 * features)
     in_block = rows[:, features:]
@@ -166,7 +169,7 @@
 
     partial = local(
         act_grad_body,
-        struct((half, 2 * width), jnp.float32),
+        struct((half, 2 * width), jnp.bfloat16),
         4 * half * features * width,
         rows,
         w_out_eff,
@@ -219,8 +222,6 @@
         partner(delta[:, width:]),
         mask_in,
     )
-    value, _ = gelu_parts(placed.transpose(2, 1, 0, 3, 4).reshape(2, half, width))
-    act = value.astype(jnp.bfloat16)
     w_out_grad = local(
         lambda *refs: w_out_grad_body(scale, *refs),
         struct((width, features), jnp.bfloat16),

time: 160 us -> 157 us (0.981)
  blocking collectives: 50 us -> 46.6 us
    all_to_all x3, blocking collectives: 50 us -> 46.6 us  [swap(): return lax.all_to_all(x, axis, 0, 0, axis_index_groups=within, tiled=True)]
    ppermute x3, waiting for transfers between devices: 2.05 us -> 4.98 us  [shifted(): return lax.ppermute(in_block, 'hid', pairs)]
where the time goes in v6:
time: 157 us; the launch traced here: 156 us
  starting transfers between devices  73.4 us (47%)
  blocking collectives  46.6 us (30%)
  waiting for transfers between devices  20.5 us (13%)
  Pallas kernels  7.64 us (5%)
  local copies, waits for them, and re-layouts  3.92 us (2%)
  other arithmetic  3.43 us (2%)
    all_to_all x3, blocking collectives, swap(): return lax.all_to_all(x, axis, 0, 0, axis_index_groups=within, tiled=True)  46.6 us
    all_to_all x3, starting transfers between devices, swap(): return lax.all_to_all(x, axis, 0, 0, axis_index_groups=within, tiled=True)  38.1 us
    ppermute x6, starting transfers between devices, partner(): return lax.ppermute(x, 'hid', [(i, i ^ 1) for i in range(n_hid)])  22.1 us
    all_to_all x3, waiting for transfers between devices, swap(): return lax.all_to_all(x, axis, 0, 0, axis_index_groups=within, tiled=True)  15.5 us
    ppermute x3, starting transfers between devices, shifted(): return lax.ppermute(in_block, 'hid', pairs)  13.2 us
    pallas_call x7, Pallas kernels, local(): pl.pallas_call(body, out_shape=out_shape, in_specs=[pl.BlockSpec(memory_s...  7.07 us
    ppermute x3, waiting for transfers between devices, shifted(): return lax.ppermute(in_block, 'hid', pairs)  4.98 us
  transfers between devices with their start and end apart: 12, of which 4 were waited for; matrix products, arithmetic and copies ran while one was open for 3% of the time, Pallas kernels for 2%

profile of v6, /device:TPU:1, one launch (start us, length us, event | category | flops | bytes accessed | tf_op | source)
XLA Modules:
  0.0 156.4 jit_solution(567266765337972845)
XLA Ops:
  2.1 29.0 %all-to-all-start = ((bf16[8,8,1536]{2,1,0:T(8,128)(2,1)}), bf16[8,8,1536]{2,1,0:T(8,128)(2,1)S(1)}, u32[]{:S(2)}, u32[]{:S(2)}) async-start(bf16[8,8,1536]{2,1,0:T(8,128)(2,1)} %broadcast_in_dim.8), calls=%async_computation | async-start | bytes 393216 | tf_op jit(solution)/shard_map/all_to_all | solution.py:39
  31.4 2.9 %collective-permute-start = (bf16[384,768]{1,0:T(8,128)(2,1)S(1)}, bf16[384,768]{1,0:T(8,128)(2,1)S(1)}, u32[]{:S(2)}, u32[]{:S(2)}) collective-permute-start(bf16[384,768]{1,0:T(8,128)(2,1)S(1)} %get-tuple-element.13.own_ref), channel_id=1, source_target_pairs={{0,16},{16,0},{32,48},{48,32},{64,80},{80,64},{96,112},{112,96},{1... | collective-permute-start | bytes 1769480 | tf_op jit(solution)/shard_map/ppermute | solution.py:129
  34.9 1.2 mul.62.own_ref
  36.1 1.9 %collective-permute-start.1 = (bf16[768,384]{1,0:T(8,128)(2,1)S(1)}, bf16[768,384]{1,0:T(8,128)(2,1)}, u32[]{:S(2)}, u32[]{:S(2)}) collective-permute-start(bf16[768,384]{1,0:T(8,128)(2,1)S(1)} %mul.62.own_ref), channel_id=1, source_target_pairs={{0,16},{16,0},{32,48},{48,32},{64,80},{80,64},{96,112},{112,96},{1... | collective-permute-start | bytes 1769480 | tf_op jit(solution)/shard_map/ppermute | solution.py:129
  38.8 2.4 %collective-permute-start.2 = (bf16[16,384]{1,0:T(8,128)(2,1)S(1)}, bf16[16,384]{1,0:T(8,128)(2,1)S(1)}, u32[]{:S(2)}, u32[]{:S(2)}) collective-permute-start(bf16[16,384]{1,0:T(8,128)(2,1)S(1)} %get-tuple-element.28), channel_id=1, source_target_pairs={{0,16},{16,0},{32,48},{48,32},{64,80},{80,64},{96,112},{112,96},{1... | collective-permute-start | bytes 36872 | tf_op jit(solution)/shard_map/ppermute | solution.py:129
  41.2 1.3 fusion.5
  44.1 14.4 %all-to-all-done = bf16[8,8,1536]{2,1,0:T(8,128)(2,1)S(1)} async-done(((bf16[8,8,1536]{2,1,0:T(8,128)(2,1)}), bf16[8,8,1536]{2,1,0:T(8,128)(2,1)S(1)}, u32[]{:S(2)}, u32[]{:S(2)}) %all-to-all-start) | async-done | bytes 196640 | tf_op jit(solution)/shard_map/all_to_all | solution.py:39
  58.6 20.6 %all_to_all.30 = bf16[4,64,768]{2,1,0:T(8,128)(2,1)S(1)} all-to-all(bf16[4,64,768]{2,1,0:T(8,128)(2,1)S(1)} %broadcast_in_dim.11), channel_id=1, replica_groups={{0,32,64,96},{16,48,80,112},{128,160,192,224},{144,176,208,240},{256,28..., dimensions={0} | all-to-all | bytes 786432 | tf_op jit(solution)/shard_map/all_to_all | solution.py:39
  79.7 14.6 %all_to_all.31.parts_ref = bf16[16,16,768]{2,1,0:T(8,128)(2,1)S(1)} all-to-all(bf16[16,16,768]{2,1,0:T(8,128)(2,1)S(1)} %bitcast.44), channel_id=1, replica_groups=mesh['hid'=64,'row'=16] {'row'}, dimensions={0} | all-to-all | bytes 786432 | tf_op jit(solution)/shard_map/all_to_all | solution.py:39
  94.4 11.5 %all_to_all.32 = bf16[16,16,768]{2,1,0:T(8,128)(2,1)S(1)} all-to-all(bf16[16,16,768]{2,1,0:T(8,128)(2,1)S(1)} %shard_map.95), channel_id=1, replica_groups=mesh['hid'=64,'row'=16] {'row'}, dimensions={0} | all-to-all | bytes 786432 | tf_op jit(solution)/shard_map/all_to_all | solution.py:39
  105.8 2.4 %shard_map.96 = bf16[256,768]{1,0:T(8,128)(2,1)} custom-call(bf16[256,768]{1,0:T(8,128)(2,1)S(1)} %bitcast.42, bf16[768,384]{1,0:T(8,128)(2,1)S(1)} %mul.62.own_ref, bf16[768,384]{1,0:T(8,128)(2,1)} %collective-permute-done.1.got_ref), custom_call_target="tpu_custom_call" | custom-call | flops 301989888 | bytes 1966080 | tf_op jit(solution)/shard_map/pallas_call | solution.py:44
  108.2 3.5 %all-to-all-start.4 = ((bf16[4,64,768]{2,1,0:T(8,128)(2,1)}), bf16[4,64,768]{2,1,0:T(8,128)(2,1)S(1)}, u32[]{:S(2)}, u32[]{:S(2)}) async-start(bf16[4,64,768]{2,1,0:T(8,128)(2,1)} %bitcast.10), calls=%async_computation.4 | async-start | bytes 786432 | tf_op jit(solution)/shard_map/all_to_all | solution.py:39
  111.7 3.3 %collective-permute-start.3 = (bf16[64,768]{1,0:T(8,128)(2,1)S(1)}, bf16[64,768]{1,0:T(8,128)(2,1)S(1)}, u32[]{:S(2)}, u32[]{:S(2)}) collective-permute-start(bf16[64,768]{1,0:T(8,128)(2,1)S(1)} %get-tuple-element.29.refs_0_), channel_id=1, source_target_pairs={{0,32},{16,48},{32,64},{48,80},{64,96},{80,112},{96,128},{112,144}... | collective-permute-start | bytes 294920 | tf_op jit(solution)/shard_map/ppermute | solution.py:166
  115.0 3.2 %collective-permute-done.3.refs_1_ = bf16[64,768]{1,0:T(8,128)(2,1)S(1)} collective-permute-done((bf16[64,768]{1,0:T(8,128)(2,1)S(1)}, bf16[64,768]{1,0:T(8,128)(2,1)S(1)}, u32[]{:S(2)}, u32[]{:S(2)}) %collective-permute-start.3) | collective-permute-done | bytes 98336 | tf_op jit(solution)/shard_map/ppermute | solution.py:166
  118.3 1.1 all-to-all-done.4.parts_ref
  120.1 5.6 %all-to-all-start.5 = ((bf16[8,8,768]{2,1,0:T(8,128)(2,1)}), bf16[8,8,768]{2,1,0:T(8,128)(2,1)S(1)}, u32[]{:S(2)}, u32[]{:S(2)}) async-start(bf16[8,8,768]{2,1,0:T(8,128)(2,1)} %bitcast.11), calls=%async_computation.5 | async-start | bytes 196608 | tf_op jit(solution)/shard_map/all_to_all | solution.py:39
  125.7 8.0 %collective-permute-start.4 = (bf16[64,768]{1,0:T(8,128)(2,1)S(1)}, bf16[64,768]{1,0:T(8,128)(2,1)S(1)}, u32[]{:S(2)}, u32[]{:S(2)}) collective-permute-start(bf16[64,768]{1,0:T(8,128)(2,1)S(1)} %get-tuple-element.29.refs_0_), channel_id=1, source_target_pairs={{0,992},{16,1008},{32,0},{48,16},{64,32},{80,48},{96,64},{112,80},... | collective-permute-start | bytes 294920 | tf_op jit(solution)/shard_map/ppermute | solution.py:166
  133.7 1.9 %collective-permute-start.5 = (bf16[64,768]{1,0:T(8,128)(2,1)S(1)}, bf16[64,768]{1,0:T(8,128)(2,1)S(1)}, u32[]{:S(2)}, u32[]{:S(2)}) collective-permute-start(bf16[64,768]{1,0:T(8,128)(2,1)S(1)} %get-tuple-element.29.refs_0_), channel_id=1, source_target_pairs={{0,64},{16,80},{32,96},{48,112},{64,128},{80,144},{96,160},{112,17... | collective-permute-start | bytes 294920 | tf_op jit(solution)/shard_map/ppermute | solution.py:166
  135.7 6.4 %collective-permute-start.8 = (bf16[256,768]{1,0:T(8,128)(2,1)S(1)}, bf16[256,768]{1,0:T(8,128)(2,1)S(1)}, u32[]{:S(2)}, u32[]{:S(2)}) collective-permute-start(bf16[256,768]{1,0:T(8,128)(2,1)S(1)} %bitcast.40), channel_id=1, source_target_pairs={{0,16},{16,0},{32,48},{48,32},{64,80},{80,64},{96,112},{112,96},{1... | collective-permute-start | bytes 1179656 | tf_op jit(solution)/shard_map/ppermute | solution.py:129
  142.1 1.7 %collective-permute-done.5.refs_3_ = bf16[64,768]{1,0:T(8,128)(2,1)S(1)} collective-permute-done((bf16[64,768]{1,0:T(8,128)(2,1)S(1)}, bf16[64,768]{1,0:T(8,128)(2,1)S(1)}, u32[]{:S(2)}, u32[]{:S(2)}) %collective-permute-start.5) | collective-permute-done | bytes 98336 | tf_op jit(solution)/shard_map/ppermute | solution.py:166
  144.4 6.6 %collective-permute-start.6 = (bf16[256,768]{1,0:T(8,128)(2,1)S(1)}, bf16[256,768]{1,0:T(8,128)(2,1)S(1)}, u32[]{:S(2)}, u32[]{:S(2)}) collective-permute-start(bf16[256,768]{1,0:T(8,128)(2,1)S(1)} %shard_map.99.refs_0_), channel_id=1, source_target_pairs={{0,16},{16,0},{32,48},{48,32},{64,80},{80,64},{96,112},{112,96},{1... | collective-permute-start | bytes 1179656 | tf_op jit(solution)/shard_map/ppermute | solution.py:129
  151.0 1.9 %collective-permute-start.7 = (bf16[256,384]{1,0:T(8,128)(2,1)S(1)}, bf16[256,384]{1,0:T(8,128)(2,1)S(1)}, u32[]{:S(2)}, u32[]{:S(2)}) collective-permute-start(bf16[256,384]{1,0:T(8,128)(2,1)S(1)} %get-tuple-element.25), channel_id=1, source_target_pairs={{0,16},{16,0},{32,48},{48,32},{64,80},{80,64},{96,112},{112,96},{1... | collective-permute-start | bytes 589832 | tf_op jit(solution)/shard_map/ppermute | solution.py:129
  153.1 1.3 shard_map.101
  154.4 1.4 shard_map.100
  (42 shorter events, 7.4 us)
Async XLA Ops:
  1.4 29.7 %copy-start.4 = (s32[3,6]{1,0:T(4,128)S(1)}, s32[3,6]{1,0:T(4,128)}, u32[]{:S(2)}) copy-start(s32[3,6]{1,0:T(4,128)} %param.13) | copy-start | bytes 220
  2.0 29.2 %copy-start.3 = (bf16[384,768]{1,0:T(8,128)(2,1)S(1)}, bf16[384,768]{1,0:T(8,128)(2,1)}, u32[]{:S(2)}) copy-start(bf16[384,768]{1,0:T(8,128)(2,1)} %param.11) | copy-start | bytes 1769476
  2.1 56.5 %all-to-all-start = ((bf16[8,8,1536]{2,1,0:T(8,128)(2,1)}), bf16[8,8,1536]{2,1,0:T(8,128)(2,1)S(1)}, u32[]{:S(2)}, u32[]{:S(2)}) async-start(bf16[8,8,1536]{2,1,0:T(8,128)(2,1)} %broadcast_in_dim.8), calls=%async_computation | async-start | bytes 393216 | tf_op jit(solution)/shard_map/all_to_all | solution.py:39
  31.3 3.0 %copy-start.5 = (s32[6,3]{0,1:T(4,128)S(1)}, s32[6,3]{0,1:T(4,128)}, u32[]{:S(2)}) copy-start(s32[6,3]{0,1:T(4,128)} %param.12) | copy-start | bytes 220
  31.4 11.9 %collective-permute-start = (bf16[384,768]{1,0:T(8,128)(2,1)S(1)}, bf16[384,768]{1,0:T(8,128)(2,1)S(1)}, u32[]{:S(2)}, u32[]{:S(2)}) collective-permute-start(bf16[384,768]{1,0:T(8,128)(2,1)S(1)} %get-tuple-element.13.own_ref), channel_id=1, source_target_pairs={{0,16},{16,0},{32,48},{48,32},{64,80},{80,64},{96,112},{112,96},{1... | collective-permute-start | bytes 1769480 | tf_op jit(solution)/shard_map/ppermute | solution.py:129
  36.1 8.1 %collective-permute-start.1 = (bf16[768,384]{1,0:T(8,128)(2,1)S(1)}, bf16[768,384]{1,0:T(8,128)(2,1)}, u32[]{:S(2)}, u32[]{:S(2)}) collective-permute-start(bf16[768,384]{1,0:T(8,128)(2,1)S(1)} %mul.62.own_ref), channel_id=1, source_target_pairs={{0,16},{16,0},{32,48},{48,32},{64,80},{80,64},{96,112},{112,96},{1... | collective-permute-start | bytes 1769480 | tf_op jit(solution)/shard_map/ppermute | solution.py:129
  38.8 4.5 %collective-permute-start.2 = (bf16[16,384]{1,0:T(8,128)(2,1)S(1)}, bf16[16,384]{1,0:T(8,128)(2,1)S(1)}, u32[]{:S(2)}, u32[]{:S(2)}) collective-permute-start(bf16[16,384]{1,0:T(8,128)(2,1)S(1)} %get-tuple-element.28), channel_id=1, source_target_pairs={{0,16},{16,0},{32,48},{48,32},{64,80},{80,64},{96,112},{112,96},{1... | collective-permute-start | bytes 36872 | tf_op jit(solution)/shard_map/ppermute | solution.py:129
  43.3 0.8 copy-start
  58.5 20.6 %copy-start.1 = (bf16[384,768]{1,0:T(8,128)(2,1)S(1)}, bf16[384,768]{1,0:T(8,128)(2,1)}, u32[]{:S(2)}) copy-start(bf16[384,768]{1,0:T(8,128)(2,1)} %copy-done) | copy-start | bytes 1769476
  108.2 11.2 %all-to-all-start.4 = ((bf16[4,64,768]{2,1,0:T(8,128)(2,1)}), bf16[4,64,768]{2,1,0:T(8,128)(2,1)S(1)}, u32[]{:S(2)}, u32[]{:S(2)}) async-start(bf16[4,64,768]{2,1,0:T(8,128)(2,1)} %bitcast.10), calls=%async_computation.4 | async-start | bytes 786432 | tf_op jit(solution)/shard_map/all_to_all | solution.py:39
  111.7 6.6 %collective-permute-start.3 = (bf16[64,768]{1,0:T(8,128)(2,1)S(1)}, bf16[64,768]{1,0:T(8,128)(2,1)S(1)}, u32[]{:S(2)}, u32[]{:S(2)}) collective-permute-start(bf16[64,768]{1,0:T(8,128)(2,1)S(1)} %get-tuple-element.29.refs_0_), channel_id=1, source_target_pairs={{0,32},{16,48},{32,64},{48,80},{64,96},{80,112},{96,128},{112,144}... | collective-permute-start | bytes 294920 | tf_op jit(solution)/shard_map/ppermute | solution.py:166
  120.1 35.7 %all-to-all-start.5 = ((bf16[8,8,768]{2,1,0:T(8,128)(2,1)}), bf16[8,8,768]{2,1,0:T(8,128)(2,1)S(1)}, u32[]{:S(2)}, u32[]{:S(2)}) async-start(bf16[8,8,768]{2,1,0:T(8,128)(2,1)} %bitcast.11), calls=%async_computation.5 | async-start | bytes 196608 | tf_op jit(solution)/shard_map/all_to_all | solution.py:39
  125.7 16.4 %collective-permute-start.4 = (bf16[64,768]{1,0:T(8,128)(2,1)S(1)}, bf16[64,768]{1,0:T(8,128)(2,1)S(1)}, u32[]{:S(2)}, u32[]{:S(2)}) collective-permute-start(bf16[64,768]{1,0:T(8,128)(2,1)S(1)} %get-tuple-element.29.refs_0_), channel_id=1, source_target_pairs={{0,992},{16,1008},{32,0},{48,16},{64,32},{80,48},{96,64},{112,80},... | collective-permute-start | bytes 294920 | tf_op jit(solution)/shard_map/ppermute | solution.py:166
  133.7 10.2 %collective-permute-start.5 = (bf16[64,768]{1,0:T(8,128)(2,1)S(1)}, bf16[64,768]{1,0:T(8,128)(2,1)S(1)}, u32[]{:S(2)}, u32[]{:S(2)}) collective-permute-start(bf16[64,768]{1,0:T(8,128)(2,1)S(1)} %get-tuple-element.29.refs_0_), channel_id=1, source_target_pairs={{0,64},{16,80},{32,96},{48,112},{64,128},{80,144},{96,160},{112,17... | collective-permute-start | bytes 294920 | tf_op jit(solution)/shard_map/ppermute | solution.py:166
  135.7 17.4 %collective-permute-start.8 = (bf16[256,768]{1,0:T(8,128)(2,1)S(1)}, bf16[256,768]{1,0:T(8,128)(2,1)S(1)}, u32[]{:S(2)}, u32[]{:S(2)}) collective-permute-start(bf16[256,768]{1,0:T(8,128)(2,1)S(1)} %bitcast.40), channel_id=1, source_target_pairs={{0,16},{16,0},{32,48},{48,32},{64,80},{80,64},{96,112},{112,96},{1... | collective-permute-start | bytes 1179656 | tf_op jit(solution)/shard_map/ppermute | solution.py:129
  144.4 8.6 %copy-start.2 = (bf16[2,4,8,8,384]{4,3,2,1,0:T(8,128)(2,1)S(1)}, bf16[2,4,8,8,384]{4,3,2,1,0:T(8,128)(2,1)}, u32[]{:S(2)}) copy-start(bf16[2,4,8,8,384]{4,3,2,1,0:T(8,128)(2,1)} %copy.17) | copy-start | bytes 1179652
  144.4 10.0 %collective-permute-start.6 = (bf16[256,768]{1,0:T(8,128)(2,1)S(1)}, bf16[256,768]{1,0:T(8,128)(2,1)S(1)}, u32[]{:S(2)}, u32[]{:S(2)}) collective-permute-start(bf16[256,768]{1,0:T(8,128)(2,1)S(1)} %shard_map.99.refs_0_), channel_id=1, source_target_pairs={{0,16},{16,0},{32,48},{48,32},{64,80},{80,64},{96,112},{112,96},{1... | collective-permute-start | bytes 1179656 | tf_op jit(solution)/shard_map/ppermute | solution.py:129
  151.0 3.3 %collective-permute-start.7 = (bf16[256,384]{1,0:T(8,128)(2,1)S(1)}, bf16[256,384]{1,0:T(8,128)(2,1)S(1)}, u32[]{:S(2)}, u32[]{:S(2)}) collective-permute-start(bf16[256,384]{1,0:T(8,128)(2,1)S(1)} %get-tuple-element.25), channel_id=1, source_target_pairs={{0,16},{16,0},{32,48},{48,32},{64,80},{80,64},{96,112},{112,96},{1... | collective-permute-start | bytes 589832 | tf_op jit(solution)/shard_map/ppermute | solution.py:129

commit v7 on v6

--- a/solution.py
+++ b/solution.py
@@ -176,6 +176,7 @@
         w_out_got,
     )
     parts = swap(partial.reshape(n_row, share, 2 * width), "row")
+    parts, *in_blocks[1:3] = lax.optimization_barrier((parts, *in_blocks[1:3]))
     copies = local(
         delta_body,
         struct((n_row, share, 2 * width), jnp.bfloat16),
@@ -194,7 +195,19 @@
         w_in_got,
     )
     back = swap(back.reshape(NEAR, far * own, features), "hid", near_groups)
-    back, in_blocks[1] = lax.optimization_barrier((back, in_blocks[1]))
+    scale = 1.0 / math.sqrt(tokens)
+    delta_got = partner(delta[:, width:])
+    w_out_grad = local(
+        lambda *refs: w_out_grad_body(scale, *refs),
+        struct((width, features), jnp.bfloat16),
+        2 * tokens * features * width,
+        lax.dynamic_index_in_dim(act, core, 0, keepdims=False),
+        lax.dynamic_index_in_dim(act, other, 0, keepdims=False),
+        rows,
+        partner(rows),
+        mask_out,
+    )
+    back, delta_got, w_out_grad = lax.optimization_barrier((back, delta_got, w_out_grad))
     back = local(sum_body, struct((far * own, features), jnp.bfloat16), back.size, back)
     back = swap(back.reshape(far, own, features), "hid", far_groups)
     in_grad = local(sum_body, struct((own, features), jnp.bfloat16), back.size, back)
@@ -211,7 +224,6 @@
         ),
     )(spots, *in_blocks)
 
-    scale = 1.0 / math.sqrt(tokens)
     w_in_grad = local(
         lambda *refs: w_in_grad_body(scale, *refs),
         struct((features, width), jnp.bfloat16),
@@ -219,18 +231,8 @@
         in_rows,
         partner(in_rows),
         delta[:, :width],
-        partner(delta[:, width:]),
+        delta_got,
         mask_in,
-    )
-    w_out_grad = local(
-        lambda *refs: w_out_grad_body(scale, *refs),
-        struct((width, features), jnp.bfloat16),
-        2 * tokens * features * width,
-        lax.dynamic_index_in_dim(act, core, 0, keepdims=False),
-        lax.dynamic_index_in_dim(act, other, 0, keepdims=False),
-        rows,
-        partner(rows),
-        mask_out,
     )
     return (in_grad, w_in_grad, w_out_grad)
 

time: 157 us -> 167 us (1.064)
  the two profiles are of different devices: /device:TPU:1 before, /device:TPU:8 now
where the time goes in v7:
time: 167 us; the launch traced here: 166 us
  starting transfers between devices  70.1 us (42%)
  waiting for transfers between devices  48.6 us (29%)
  blocking collectives  32.4 us (19%)
  Pallas kernels  8.39 us (5%)
  local copies, waits for them, and re-layouts  3.96 us (2%)
    all_to_all x4, starting transfers between devices, swap(): return lax.all_to_all(x, axis, 0, 0, axis_index_groups=within, tiled=True)  48.5 us
    all_to_all x4, waiting for transfers between devices, swap(): return lax.all_to_all(x, axis, 0, 0, axis_index_groups=within, tiled=True)  35.7 us
    all_to_all x2, blocking collectives, swap(): return lax.all_to_all(x, axis, 0, 0, axis_index_groups=within, tiled=True)  32.4 us
    ppermute x6, starting transfers between devices, partner(): return lax.ppermute(x, 'hid', [(i, i ^ 1) for i in range(n_hid)])  12.6 us
    ppermute x3, waiting for transfers between devices, shifted(): return lax.ppermute(in_block, 'hid', pairs)  11.2 us
    ppermute x3, starting transfers between devices, shifted(): return lax.ppermute(in_block, 'hid', pairs)  8.95 us
    pallas_call x7, Pallas kernels, local(): pl.pallas_call(body, out_shape=out_shape, in_specs=[pl.BlockSpec(memory_s...  7.82 us
  transfers between devices with their start and end apart: 13, of which 8 were waited for; matrix products, arithmetic and copies ran while one was open for 1% of the time, Pallas kernels for 2%

profile of v7, /device:TPU:8, one launch (start us, length us, event | category | flops | bytes accessed | tf_op | source)
XLA Modules:
  0.0 165.9 jit_solution(18424159192885774658)
XLA Ops:
  2.1 28.5 %all-to-all-start = ((bf16[8,8,1536]{2,1,0:T(8,128)(2,1)}), bf16[8,8,1536]{2,1,0:T(8,128)(2,1)S(1)}, u32[]{:S(2)}, u32[]{:S(2)}) async-start(bf16[8,8,1536]{2,1,0:T(8,128)(2,1)} %broadcast_in_dim.8), calls=%async_computation | async-start | bytes 393216 | tf_op jit(solution)/shard_map/all_to_all | solution.py:39
  30.8 1.9 %collective-permute-start = (bf16[384,768]{1,0:T(8,128)(2,1)S(1)}, bf16[384,768]{1,0:T(8,128)(2,1)}, u32[]{:S(2)}, u32[]{:S(2)}) collective-permute-start(bf16[384,768]{1,0:T(8,128)(2,1)S(1)} %get-tuple-element.17.own_ref), channel_id=1, source_target_pairs={{0,16},{16,0},{32,48},{48,32},{64,80},{80,64},{96,112},{112,96},{1... | collective-permute-start | bytes 1769480 | tf_op jit(solution)/shard_map/ppermute | solution.py:129
  34.3 2.4 %collective-permute-start.1 = (bf16[768,384]{1,0:T(8,128)(2,1)S(1)}, bf16[768,384]{1,0:T(8,128)(2,1)S(1)}, u32[]{:S(2)}, u32[]{:S(2)}) collective-permute-start(bf16[768,384]{1,0:T(8,128)(2,1)S(1)} %mul.62.own_ref), channel_id=1, source_target_pairs={{0,16},{16,0},{32,48},{48,32},{64,80},{80,64},{96,112},{112,96},{1... | collective-permute-start | bytes 1769480 | tf_op jit(solution)/shard_map/ppermute | solution.py:129
  36.8 1.9 %collective-permute-start.2 = (bf16[16,384]{1,0:T(8,128)(2,1)S(1)}, bf16[16,384]{1,0:T(8,128)(2,1)S(1)}, u32[]{:S(2)}, u32[]{:S(2)}) collective-permute-start(bf16[16,384]{1,0:T(8,128)(2,1)S(1)} %get-tuple-element.36), channel_id=1, source_target_pairs={{0,16},{16,0},{32,48},{48,32},{64,80},{80,64},{96,112},{112,96},{1... | collective-permute-start | bytes 36872 | tf_op jit(solution)/shard_map/ppermute | solution.py:129
  40.7 21.2 %all-to-all-done = bf16[8,8,1536]{2,1,0:T(8,128)(2,1)S(1)} async-done(((bf16[8,8,1536]{2,1,0:T(8,128)(2,1)}), bf16[8,8,1536]{2,1,0:T(8,128)(2,1)S(1)}, u32[]{:S(2)}, u32[]{:S(2)}) %all-to-all-start) | async-done | bytes 196640 | tf_op jit(solution)/shard_map/all_to_all | solution.py:39
  62.0 17.8 %all_to_all.30 = bf16[4,64,768]{2,1,0:T(8,128)(2,1)S(1)} all-to-all(bf16[4,64,768]{2,1,0:T(8,128)(2,1)S(1)} %broadcast_in_dim.11), channel_id=1, replica_groups={{0,32,64,96},{16,48,80,112},{128,160,192,224},{144,176,208,240},{256,28..., dimensions={0} | all-to-all | bytes 786432 | tf_op jit(solution)/shard_map/all_to_all | solution.py:39
  79.7 2.4 %shard_map.94 = bf16[256,768]{1,0:T(8,128)(2,1)} custom-call(bf16[256,768]{1,0:T(8,128)(2,1)S(1)} %bitcast.39, bf16[384,768]{1,0:T(8,128)(2,1)S(1)} %get-tuple-element.17.own_ref, bf16[384,768]{1,0:T(8,128)(2,1)} %collective-permute-done.got_ref), custom_call_target="tpu_custom_call" | custom-call | flops 301989888 | bytes 1966080 | tf_op jit(solution)/shard_map/pallas_call | solution.py:44
  82.1 7.4 %all-to-all-start.2 = ((bf16[16,16,768]{2,1,0:T(8,128)(2,1)}), bf16[16,16,768]{2,1,0:T(8,128)(2,1)S(1)}, u32[]{:S(2)}, u32[]{:S(2)}) async-start(bf16[16,16,768]{2,1,0:T(8,128)(2,1)} %bitcast.8), calls=%async_computation.2 | async-start | bytes 786432 | tf_op jit(solution)/shard_map/all_to_all | solution.py:39
  89.5 2.1 %collective-permute-start.3 = (bf16[64,768]{1,0:T(8,128)(2,1)S(1)}, bf16[64,768]{1,0:T(8,128)(2,1)S(1)}, u32[]{:S(2)}, u32[]{:S(2)}) collective-permute-start(bf16[64,768]{1,0:T(8,128)(2,1)S(1)} %get-tuple-element.37.refs_0_), channel_id=1, source_target_pairs={{0,32},{16,48},{32,64},{48,80},{64,96},{80,112},{96,128},{112,144}... | collective-permute-start | bytes 294920 | tf_op jit(solution)/shard_map/ppermute | solution.py:166
  91.6 4.9 %collective-permute-start.4 = (bf16[64,768]{1,0:T(8,128)(2,1)S(1)}, bf16[64,768]{1,0:T(8,128)(2,1)S(1)}, u32[]{:S(2)}, u32[]{:S(2)}) collective-permute-start(bf16[64,768]{1,0:T(8,128)(2,1)S(1)} %get-tuple-element.37.refs_0_), channel_id=1, source_target_pairs={{0,992},{16,1008},{32,0},{48,16},{64,32},{80,48},{96,64},{112,80},... | collective-permute-start | bytes 294920 | tf_op jit(solution)/shard_map/ppermute | solution.py:166
  97.2 1.5 collective-permute-done.4.refs_2_
  98.8 14.7 %all_to_all.31 = bf16[16,16,768]{2,1,0:T(8,128)(2,1)S(1)} all-to-all(bf16[16,16,768]{2,1,0:T(8,128)(2,1)S(1)} %shard_map.95), channel_id=1, replica_groups=mesh['hid'=64,'row'=16] {'row'}, dimensions={0} | all-to-all | bytes 786432 | tf_op jit(solution)/shard_map/all_to_all | solution.py:39
  113.5 1.3 shard_map.96
  114.9 4.0 %all-to-all-start.4 = ((bf16[4,64,768]{2,1,0:T(8,128)(2,1)}), bf16[4,64,768]{2,1,0:T(8,128)(2,1)S(1)}, u32[]{:S(2)}, u32[]{:S(2)}) async-start(bf16[4,64,768]{2,1,0:T(8,128)(2,1)} %bitcast.10), calls=%async_computation.4 | async-start | bytes 786432 | tf_op jit(solution)/shard_map/all_to_all | solution.py:39
  118.8 2.0 %collective-permute-start.6 = (bf16[256,768]{1,0:T(8,128)(2,1)S(1)}, bf16[256,768]{1,0:T(8,128)(2,1)S(1)}, u32[]{:S(2)}, u32[]{:S(2)}) collective-permute-start(bf16[256,768]{1,0:T(8,128)(2,1)S(1)} %bitcast.40), channel_id=1, source_target_pairs={{0,16},{16,0},{32,48},{48,32},{64,80},{80,64},{96,112},{112,96},{1... | collective-permute-start | bytes 1179656 | tf_op jit(solution)/shard_map/ppermute | solution.py:129
  120.9 2.4 %collective-permute-start.5 = (bf16[256,384]{1,0:T(8,128)(2,1)S(1)}, bf16[256,384]{1,0:T(8,128)(2,1)S(1)}, u32[]{:S(2)}, u32[]{:S(2)}) collective-permute-start(bf16[256,384]{1,0:T(8,128)(2,1)S(1)} %get-tuple-element.32), channel_id=1, source_target_pairs={{0,16},{16,0},{32,48},{48,32},{64,80},{80,64},{96,112},{112,96},{1... | collective-permute-start | bytes 589832 | tf_op jit(solution)/shard_map/ppermute | solution.py:129
  124.7 3.0 %all-to-all-done.4.parts_ref = bf16[4,64,768]{2,1,0:T(8,128)(2,1)S(1)} async-done(((bf16[4,64,768]{2,1,0:T(8,128)(2,1)}), bf16[4,64,768]{2,1,0:T(8,128)(2,1)S(1)}, u32[]{:S(2)}, u32[]{:S(2)}) %all-to-all-start.4) | async-done | bytes 393248 | tf_op jit(solution)/shard_map/all_to_all | solution.py:39
  128.4 8.7 %all-to-all-start.5 = ((bf16[8,8,768]{2,1,0:T(8,128)(2,1)}), bf16[8,8,768]{2,1,0:T(8,128)(2,1)S(1)}, u32[]{:S(2)}, u32[]{:S(2)}) async-start(bf16[8,8,768]{2,1,0:T(8,128)(2,1)} %bitcast.13), calls=%async_computation.5 | async-start | bytes 196608 | tf_op jit(solution)/shard_map/all_to_all | solution.py:39
  137.1 1.9 %collective-permute-start.7 = (bf16[64,768]{1,0:T(8,128)(2,1)S(1)}, bf16[64,768]{1,0:T(8,128)(2,1)S(1)}, u32[]{:S(2)}, u32[]{:S(2)}) collective-permute-start(bf16[64,768]{1,0:T(8,128)(2,1)S(1)} %get-tuple-element.37.refs_0_), channel_id=1, source_target_pairs={{0,64},{16,80},{32,96},{48,112},{64,128},{80,144},{96,160},{112,17... | collective-permute-start | bytes 294920 | tf_op jit(solution)/shard_map/ppermute | solution.py:166
  139.1 9.0 %collective-permute-done.7.refs_3_ = bf16[64,768]{1,0:T(8,128)(2,1)S(1)} collective-permute-done((bf16[64,768]{1,0:T(8,128)(2,1)S(1)}, bf16[64,768]{1,0:T(8,128)(2,1)S(1)}, u32[]{:S(2)}, u32[]{:S(2)}) %collective-permute-start.7) | collective-permute-done | bytes 98336 | tf_op jit(solution)/shard_map/ppermute | solution.py:166
  148.7 1.9 %collective-permute-start.8 = (bf16[256,768]{1,0:T(8,128)(2,1)S(1)}, bf16[256,768]{1,0:T(8,128)(2,1)S(1)}, u32[]{:S(2)}, u32[]{:S(2)}) collective-permute-start(bf16[256,768]{1,0:T(8,128)(2,1)S(1)} %shard_map.100.refs_0_), channel_id=1, source_target_pairs={{0,16},{16,0},{32,48},{48,32},{64,80},{80,64},{96,112},{112,96},{1... | collective-permute-start | bytes 1179656 | tf_op jit(solution)/shard_map/ppermute | solution.py:129
  150.6 1.7 %collective-permute-done.8.refs_1_ = bf16[256,768]{1,0:T(8,128)(2,1)S(1)} collective-permute-done((bf16[256,768]{1,0:T(8,128)(2,1)S(1)}, bf16[256,768]{1,0:T(8,128)(2,1)S(1)}, u32[]{:S(2)}, u32[]{:S(2)}) %collective-permute-start.8) | collective-permute-done | bytes 393248 | tf_op jit(solution)/shard_map/ppermute | solution.py:129
  152.3 1.4 shard_map.101
  153.7 11.5 %all-to-all-done.5.parts_ref = bf16[8,8,768]{2,1,0:T(8,128)(2,1)S(1)} async-done(((bf16[8,8,768]{2,1,0:T(8,128)(2,1)}), bf16[8,8,768]{2,1,0:T(8,128)(2,1)S(1)}, u32[]{:S(2)}, u32[]{:S(2)}) %all-to-all-start.5) | async-done | bytes 98336 | tf_op jit(solution)/shard_map/all_to_all | solution.py:39
  (47 shorter events, 9.3 us)
Async XLA Ops:
  1.4 29.2 %copy-start.6 = (s32[3,6]{1,0:T(4,128)S(1)}, s32[3,6]{1,0:T(4,128)}, u32[]{:S(2)}) copy-start(s32[3,6]{1,0:T(4,128)} %param.13) | copy-start | bytes 220
  2.0 28.7 %copy-start.3 = (bf16[384,768]{1,0:T(8,128)(2,1)S(1)}, bf16[384,768]{1,0:T(8,128)(2,1)}, u32[]{:S(2)}) copy-start(bf16[384,768]{1,0:T(8,128)(2,1)} %param.11) | copy-start | bytes 1769476
  2.1 59.9 %all-to-all-start = ((bf16[8,8,1536]{2,1,0:T(8,128)(2,1)}), bf16[8,8,1536]{2,1,0:T(8,128)(2,1)S(1)}, u32[]{:S(2)}, u32[]{:S(2)}) async-start(bf16[8,8,1536]{2,1,0:T(8,128)(2,1)} %broadcast_in_dim.8), calls=%async_computation | async-start | bytes 393216 | tf_op jit(solution)/shard_map/all_to_all | solution.py:39
  30.7 2.0 %copy-start.7 = (s32[6,3]{0,1:T(4,128)S(1)}, s32[6,3]{0,1:T(4,128)}, u32[]{:S(2)}) copy-start(s32[6,3]{0,1:T(4,128)} %param.12) | copy-start | bytes 220
  30.8 9.1 %collective-permute-start = (bf16[384,768]{1,0:T(8,128)(2,1)S(1)}, bf16[384,768]{1,0:T(8,128)(2,1)}, u32[]{:S(2)}, u32[]{:S(2)}) collective-permute-start(bf16[384,768]{1,0:T(8,128)(2,1)S(1)} %get-tuple-element.17.own_ref), channel_id=1, source_target_pairs={{0,16},{16,0},{32,48},{48,32},{64,80},{80,64},{96,112},{112,96},{1... | collective-permute-start | bytes 1769480 | tf_op jit(solution)/shard_map/ppermute | solution.py:129
  33.1 1.1 copy-start.4
  34.1 2.6 %copy-start.5 = (bf16[512,384]{1,0:T(8,128)(2,1)S(1)}, bf16[512,384]{1,0:T(8,128)(2,1)}, u32[]{:S(2)}) copy-start(bf16[512,384]{1,0:T(8,128)(2,1)} %param.9) | copy-start | bytes 1179652
  34.3 5.6 %collective-permute-start.1 = (bf16[768,384]{1,0:T(8,128)(2,1)S(1)}, bf16[768,384]{1,0:T(8,128)(2,1)S(1)}, u32[]{:S(2)}, u32[]{:S(2)}) collective-permute-start(bf16[768,384]{1,0:T(8,128)(2,1)S(1)} %mul.62.own_ref), channel_id=1, source_target_pairs={{0,16},{16,0},{32,48},{48,32},{64,80},{80,64},{96,112},{112,96},{1... | collective-permute-start | bytes 1769480 | tf_op jit(solution)/shard_map/ppermute | solution.py:129
  36.8 3.1 %collective-permute-start.2 = (bf16[16,384]{1,0:T(8,128)(2,1)S(1)}, bf16[16,384]{1,0:T(8,128)(2,1)S(1)}, u32[]{:S(2)}, u32[]{:S(2)}) collective-permute-start(bf16[16,384]{1,0:T(8,128)(2,1)S(1)} %get-tuple-element.36), channel_id=1, source_target_pairs={{0,16},{16,0},{32,48},{48,32},{64,80},{80,64},{96,112},{112,96},{1... | collective-permute-start | bytes 36872 | tf_op jit(solution)/shard_map/ppermute | solution.py:129
  39.9 0.8 copy-start
  82.1 16.6 %all-to-all-start.2 = ((bf16[16,16,768]{2,1,0:T(8,128)(2,1)}), bf16[16,16,768]{2,1,0:T(8,128)(2,1)S(1)}, u32[]{:S(2)}, u32[]{:S(2)}) async-start(bf16[16,16,768]{2,1,0:T(8,128)(2,1)} %bitcast.8), calls=%async_computation.2 | async-start | bytes 786432 | tf_op jit(solution)/shard_map/all_to_all | solution.py:39
  89.5 7.7 %collective-permute-start.3 = (bf16[64,768]{1,0:T(8,128)(2,1)S(1)}, bf16[64,768]{1,0:T(8,128)(2,1)S(1)}, u32[]{:S(2)}, u32[]{:S(2)}) collective-permute-start(bf16[64,768]{1,0:T(8,128)(2,1)S(1)} %get-tuple-element.37.refs_0_), channel_id=1, source_target_pairs={{0,32},{16,48},{32,64},{48,80},{64,96},{80,112},{96,128},{112,144}... | collective-permute-start | bytes 294920 | tf_op jit(solution)/shard_map/ppermute | solution.py:166
  91.6 7.1 %collective-permute-start.4 = (bf16[64,768]{1,0:T(8,128)(2,1)S(1)}, bf16[64,768]{1,0:T(8,128)(2,1)S(1)}, u32[]{:S(2)}, u32[]{:S(2)}) collective-permute-start(bf16[64,768]{1,0:T(8,128)(2,1)S(1)} %get-tuple-element.37.refs_0_), channel_id=1, source_target_pairs={{0,992},{16,1008},{32,0},{48,16},{64,32},{80,48},{96,64},{112,80},... | collective-permute-start | bytes 294920 | tf_op jit(solution)/shard_map/ppermute | solution.py:166
  98.8 14.7 %copy-start.1 = (bf16[768,384]{1,0:T(8,128)(2,1)S(1)}, bf16[768,384]{1,0:T(8,128)(2,1)}, u32[]{:S(2)}) copy-start(bf16[768,384]{1,0:T(8,128)(2,1)} %copy-done) | copy-start | bytes 1769476
  114.9 12.8 %all-to-all-start.4 = ((bf16[4,64,768]{2,1,0:T(8,128)(2,1)}), bf16[4,64,768]{2,1,0:T(8,128)(2,1)S(1)}, u32[]{:S(2)}, u32[]{:S(2)}) async-start(bf16[4,64,768]{2,1,0:T(8,128)(2,1)} %bitcast.10), calls=%async_computation.4 | async-start | bytes 786432 | tf_op jit(solution)/shard_map/all_to_all | solution.py:39
  118.8 4.5 %copy-start.2 = (bf16[2,4,8,8,384]{4,3,2,1,0:T(8,128)(2,1)S(1)}, bf16[2,4,8,8,384]{4,3,2,1,0:T(8,128)(2,1)}, u32[]{:S(2)}) copy-start(bf16[2,4,8,8,384]{4,3,2,1,0:T(8,128)(2,1)} %copy.17) | copy-start | bytes 1179652
  118.8 4.6 %collective-permute-start.6 = (bf16[256,768]{1,0:T(8,128)(2,1)S(1)}, bf16[256,768]{1,0:T(8,128)(2,1)S(1)}, u32[]{:S(2)}, u32[]{:S(2)}) collective-permute-start(bf16[256,768]{1,0:T(8,128)(2,1)S(1)} %bitcast.40), channel_id=1, source_target_pairs={{0,16},{16,0},{32,48},{48,32},{64,80},{80,64},{96,112},{112,96},{1... | collective-permute-start | bytes 1179656 | tf_op jit(solution)/shard_map/ppermute | solution.py:129
  120.9 3.8 %collective-permute-start.5 = (bf16[256,384]{1,0:T(8,128)(2,1)S(1)}, bf16[256,384]{1,0:T(8,128)(2,1)S(1)}, u32[]{:S(2)}, u32[]{:S(2)}) collective-permute-start(bf16[256,384]{1,0:T(8,128)(2,1)S(1)} %get-tuple-element.32), channel_id=1, source_target_pairs={{0,16},{16,0},{32,48},{48,32},{64,80},{80,64},{96,112},{112,96},{1... | collective-permute-start | bytes 589832 | tf_op jit(solution)/shard_map/ppermute | solution.py:129
  128.4 36.9 %all-to-all-start.5 = ((bf16[8,8,768]{2,1,0:T(8,128)(2,1)}), bf16[8,8,768]{2,1,0:T(8,128)(2,1)S(1)}, u32[]{:S(2)}, u32[]{:S(2)}) async-start(bf16[8,8,768]{2,1,0:T(8,128)(2,1)} %bitcast.13), calls=%async_computation.5 | async-start | bytes 196608 | tf_op jit(solution)/shard_map/all_to_all | solution.py:39
  137.1 11.0 %collective-permute-start.7 = (bf16[64,768]{1,0:T(8,128)(2,1)S(1)}, bf16[64,768]{1,0:T(8,128)(2,1)S(1)}, u32[]{:S(2)}, u32[]{:S(2)}) collective-permute-start(bf16[64,768]{1,0:T(8,128)(2,1)S(1)} %get-tuple-element.37.refs_0_), channel_id=1, source_target_pairs={{0,64},{16,80},{32,96},{48,112},{64,128},{80,144},{96,160},{112,17... | collective-permute-start | bytes 294920 | tf_op jit(solution)/shard_map/ppermute | solution.py:166
  148.7 3.6 %collective-permute-start.8 = (bf16[256,768]{1,0:T(8,128)(2,1)S(1)}, bf16[256,768]{1,0:T(8,128)(2,1)S(1)}, u32[]{:S(2)}, u32[]{:S(2)}) collective-permute-start(bf16[256,768]{1,0:T(8,128)(2,1)S(1)} %shard_map.100.refs_0_), channel_id=1, source_target_pairs={{0,16},{16,0},{32,48},{48,32},{64,80},{80,64},{96,112},{112,96},{1... | collective-permute-start | bytes 1179656 | tf_op jit(solution)/shard_map/ppermute | solution.py:129

commit v8 on v7

--- a/solution.py
+++ b/solution.py
@@ -176,7 +176,6 @@
         w_out_got,
     )
     parts = swap(partial.reshape(n_row, share, 2 * width), "row")
-    parts, *in_blocks[1:3] = lax.optimization_barrier((parts, *in_blocks[1:3]))
     copies = local(
         delta_body,
         struct((n_row, share, 2 * width), jnp.bfloat16),

time: 167 us -> 157 us (0.940)
  the two profiles are of different devices: /device:TPU:8 before, /device:TPU:1 now
where the time goes in v8:
time: 157 us; the launch traced here: 156 us
  starting transfers between devices  67.8 us (43%)
  blocking collectives  46.6 us (30%)
  waiting for transfers between devices  26 us (17%)
  Pallas kernels  7.64 us (5%)
  local copies, waits for them, and re-layouts  3.92 us (2%)
  other arithmetic  3.43 us (2%)
    all_to_all x3, blocking collectives, swap(): return lax.all_to_all(x, axis, 0, 0, axis_index_groups=within, tiled=True)  46.6 us
    all_to_all x3, starting transfers between devices, swap(): return lax.all_to_all(x, axis, 0, 0, axis_index_groups=within, tiled=True)  37.3 us
    ppermute x6, starting transfers between devices, partner(): return lax.ppermute(x, 'hid', [(i, i ^ 1) for i in range(n_hid)])  18.9 us
    all_to_all x3, waiting for transfers between devices, swap(): return lax.all_to_all(x, axis, 0, 0, axis_index_groups=within, tiled=True)  14.4 us
    ppermute x3, starting transfers between devices, shifted(): return lax.ppermute(in_block, 'hid', pairs)  11.6 us
    ppermute x3, waiting for transfers between devices, shifted(): return lax.ppermute(in_block, 'hid', pairs)  10.3 us
    pallas_call x7, Pallas kernels, local(): pl.pallas_call(body, out_shape=out_shape, in_specs=[pl.BlockSpec(memory_s...  7.07 us
  transfers between devices with their start and end apart: 12, of which 4 were waited for; matrix products, arithmetic and copies ran while one was open for 3% of the time, Pallas kernels for 2%

profile of v8, /device:TPU:1, one launch (start us, length us, event | category | flops | bytes accessed | tf_op | source)
XLA Modules:
  0.0 156.3 jit_solution(8053696744047020266)
XLA Ops:
  2.1 29.0 %all-to-all-start = ((bf16[8,8,1536]{2,1,0:T(8,128)(2,1)}), bf16[8,8,1536]{2,1,0:T(8,128)(2,1)S(1)}, u32[]{:S(2)}, u32[]{:S(2)}) async-start(bf16[8,8,1536]{2,1,0:T(8,128)(2,1)} %broadcast_in_dim.8), calls=%async_computation | async-start | bytes 393216 | tf_op jit(solution)/shard_map/all_to_all | solution.py:39
  31.4 2.9 %collective-permute-start = (bf16[384,768]{1,0:T(8,128)(2,1)S(1)}, bf16[384,768]{1,0:T(8,128)(2,1)S(1)}, u32[]{:S(2)}, u32[]{:S(2)}) collective-permute-start(bf16[384,768]{1,0:T(8,128)(2,1)S(1)} %get-tuple-element.14.own_ref), channel_id=1, source_target_pairs={{0,16},{16,0},{32,48},{48,32},{64,80},{80,64},{96,112},{112,96},{1... | collective-permute-start | bytes 1769480 | tf_op jit(solution)/shard_map/ppermute | solution.py:129
  34.9 1.2 mul.62.own_ref
  36.1 1.9 %collective-permute-start.1 = (bf16[768,384]{1,0:T(8,128)(2,1)S(1)}, bf16[768,384]{1,0:T(8,128)(2,1)}, u32[]{:S(2)}, u32[]{:S(2)}) collective-permute-start(bf16[768,384]{1,0:T(8,128)(2,1)S(1)} %mul.62.own_ref), channel_id=1, source_target_pairs={{0,16},{16,0},{32,48},{48,32},{64,80},{80,64},{96,112},{112,96},{1... | collective-permute-start | bytes 1769480 | tf_op jit(solution)/shard_map/ppermute | solution.py:129
  38.8 2.4 %collective-permute-start.2 = (bf16[16,384]{1,0:T(8,128)(2,1)S(1)}, bf16[16,384]{1,0:T(8,128)(2,1)S(1)}, u32[]{:S(2)}, u32[]{:S(2)}) collective-permute-start(bf16[16,384]{1,0:T(8,128)(2,1)S(1)} %get-tuple-element.30), channel_id=1, source_target_pairs={{0,16},{16,0},{32,48},{48,32},{64,80},{80,64},{96,112},{112,96},{1... | collective-permute-start | bytes 36872 | tf_op jit(solution)/shard_map/ppermute | solution.py:129
  41.2 1.3 fusion.5
  43.3 0.8 copy-done
  44.1 14.4 %all-to-all-done = bf16[8,8,1536]{2,1,0:T(8,128)(2,1)S(1)} async-done(((bf16[8,8,1536]{2,1,0:T(8,128)(2,1)}), bf16[8,8,1536]{2,1,0:T(8,128)(2,1)S(1)}, u32[]{:S(2)}, u32[]{:S(2)}) %all-to-all-start) | async-done | bytes 196640 | tf_op jit(solution)/shard_map/all_to_all | solution.py:39
  58.6 20.6 %all_to_all.30 = bf16[4,64,768]{2,1,0:T(8,128)(2,1)S(1)} all-to-all(bf16[4,64,768]{2,1,0:T(8,128)(2,1)S(1)} %broadcast_in_dim.11), channel_id=1, replica_groups={{0,32,64,96},{16,48,80,112},{128,160,192,224},{144,176,208,240},{256,28..., dimensions={0} | all-to-all | bytes 786432 | tf_op jit(solution)/shard_map/all_to_all | solution.py:39
  79.7 14.6 %all_to_all.31.parts_ref = bf16[16,16,768]{2,1,0:T(8,128)(2,1)S(1)} all-to-all(bf16[16,16,768]{2,1,0:T(8,128)(2,1)S(1)} %bitcast.44), channel_id=1, replica_groups=mesh['hid'=64,'row'=16] {'row'}, dimensions={0} | all-to-all | bytes 786432 | tf_op jit(solution)/shard_map/all_to_all | solution.py:39
  94.4 11.5 %all_to_all.32 = bf16[16,16,768]{2,1,0:T(8,128)(2,1)S(1)} all-to-all(bf16[16,16,768]{2,1,0:T(8,128)(2,1)S(1)} %shard_map.95), channel_id=1, replica_groups=mesh['hid'=64,'row'=16] {'row'}, dimensions={0} | all-to-all | bytes 786432 | tf_op jit(solution)/shard_map/all_to_all | solution.py:39
  105.8 2.4 %shard_map.96 = bf16[256,768]{1,0:T(8,128)(2,1)} custom-call(bf16[256,768]{1,0:T(8,128)(2,1)S(1)} %bitcast.42, bf16[768,384]{1,0:T(8,128)(2,1)S(1)} %mul.62.own_ref, bf16[768,384]{1,0:T(8,128)(2,1)} %collective-permute-done.1.got_ref), custom_call_target="tpu_custom_call" | custom-call | flops 301989888 | bytes 1966080 | tf_op jit(solution)/shard_map/pallas_call | solution.py:44
  108.2 3.5 %all-to-all-start.4 = ((bf16[4,64,768]{2,1,0:T(8,128)(2,1)}), bf16[4,64,768]{2,1,0:T(8,128)(2,1)S(1)}, u32[]{:S(2)}, u32[]{:S(2)}) async-start(bf16[4,64,768]{2,1,0:T(8,128)(2,1)} %bitcast.10), calls=%async_computation.4 | async-start | bytes 786432 | tf_op jit(solution)/shard_map/all_to_all | solution.py:39
  111.7 6.8 %collective-permute-start.4 = (bf16[256,768]{1,0:T(8,128)(2,1)S(1)}, bf16[256,768]{1,0:T(8,128)(2,1)S(1)}, u32[]{:S(2)}, u32[]{:S(2)}) collective-permute-start(bf16[256,768]{1,0:T(8,128)(2,1)S(1)} %bitcast.40), channel_id=1, source_target_pairs={{0,16},{16,0},{32,48},{48,32},{64,80},{80,64},{96,112},{112,96},{1... | collective-permute-start | bytes 1179656 | tf_op jit(solution)/shard_map/ppermute | solution.py:129
  118.6 1.9 %collective-permute-start.3 = (bf16[256,384]{1,0:T(8,128)(2,1)S(1)}, bf16[256,384]{1,0:T(8,128)(2,1)S(1)}, u32[]{:S(2)}, u32[]{:S(2)}) collective-permute-start(bf16[256,384]{1,0:T(8,128)(2,1)S(1)} %get-tuple-element.26), channel_id=1, source_target_pairs={{0,16},{16,0},{32,48},{48,32},{64,80},{80,64},{96,112},{112,96},{1... | collective-permute-start | bytes 589832 | tf_op jit(solution)/shard_map/ppermute | solution.py:129
  120.6 1.3 shard_map.97
  122.6 4.8 %all-to-all-start.5 = ((bf16[8,8,768]{2,1,0:T(8,128)(2,1)}), bf16[8,8,768]{2,1,0:T(8,128)(2,1)S(1)}, u32[]{:S(2)}, u32[]{:S(2)}) async-start(bf16[8,8,768]{2,1,0:T(8,128)(2,1)} %bitcast.13), calls=%async_computation.5 | async-start | bytes 196608 | tf_op jit(solution)/shard_map/all_to_all | solution.py:39
  127.4 3.6 %collective-permute-start.5 = (bf16[64,768]{1,0:T(8,128)(2,1)S(1)}, bf16[64,768]{1,0:T(8,128)(2,1)S(1)}, u32[]{:S(2)}, u32[]{:S(2)}) collective-permute-start(bf16[64,768]{1,0:T(8,128)(2,1)S(1)} %get-tuple-element.31.refs_0_), channel_id=1, source_target_pairs={{0,32},{16,48},{32,64},{48,80},{64,96},{80,112},{96,128},{112,144}... | collective-permute-start | bytes 294920 | tf_op jit(solution)/shard_map/ppermute | solution.py:166
  131.0 6.1 %collective-permute-start.6 = (bf16[64,768]{1,0:T(8,128)(2,1)S(1)}, bf16[64,768]{1,0:T(8,128)(2,1)S(1)}, u32[]{:S(2)}, u32[]{:S(2)}) collective-permute-start(bf16[64,768]{1,0:T(8,128)(2,1)S(1)} %get-tuple-element.31.refs_0_), channel_id=1, source_target_pairs={{0,992},{16,1008},{32,0},{48,16},{64,32},{80,48},{96,64},{112,80},... | collective-permute-start | bytes 294920 | tf_op jit(solution)/shard_map/ppermute | solution.py:166
  137.1 1.9 %collective-permute-start.7 = (bf16[64,768]{1,0:T(8,128)(2,1)S(1)}, bf16[64,768]{1,0:T(8,128)(2,1)S(1)}, u32[]{:S(2)}, u32[]{:S(2)}) collective-permute-start(bf16[64,768]{1,0:T(8,128)(2,1)S(1)} %get-tuple-element.31.refs_0_), channel_id=1, source_target_pairs={{0,64},{16,80},{32,96},{48,112},{64,128},{80,144},{96,160},{112,17... | collective-permute-start | bytes 294920 | tf_op jit(solution)/shard_map/ppermute | solution.py:166
  139.8 9.7 %collective-permute-done.7.refs_3_ = bf16[64,768]{1,0:T(8,128)(2,1)S(1)} collective-permute-done((bf16[64,768]{1,0:T(8,128)(2,1)S(1)}, bf16[64,768]{1,0:T(8,128)(2,1)S(1)}, u32[]{:S(2)}, u32[]{:S(2)}) %collective-permute-start.7) | collective-permute-done | bytes 98336 | tf_op jit(solution)/shard_map/ppermute | solution.py:166
  150.0 2.9 %collective-permute-start.8 = (bf16[256,768]{1,0:T(8,128)(2,1)S(1)}, bf16[256,768]{1,0:T(8,128)(2,1)S(1)}, u32[]{:S(2)}, u32[]{:S(2)}) collective-permute-start(bf16[256,768]{1,0:T(8,128)(2,1)S(1)} %shard_map.100.refs_0_), channel_id=1, source_target_pairs={{0,16},{16,0},{32,48},{48,32},{64,80},{80,64},{96,112},{112,96},{1... | collective-permute-start | bytes 1179656 | tf_op jit(solution)/shard_map/ppermute | solution.py:129
  153.0 1.3 collective-permute-done.8.refs_1_
  154.3 1.4 shard_map.101
  (42 shorter events, 7.2 us)
Async XLA Ops:
  1.4 29.7 %copy-start.4 = (s32[3,6]{1,0:T(4,128)S(1)}, s32[3,6]{1,0:T(4,128)}, u32[]{:S(2)}) copy-start(s32[3,6]{1,0:T(4,128)} %param.13) | copy-start | bytes 220
  2.0 29.2 %copy-start.3 = (bf16[384,768]{1,0:T(8,128)(2,1)S(1)}, bf16[384,768]{1,0:T(8,128)(2,1)}, u32[]{:S(2)}) copy-start(bf16[384,768]{1,0:T(8,128)(2,1)} %param.11) | copy-start | bytes 1769476
  2.1 56.5 %all-to-all-start = ((bf16[8,8,1536]{2,1,0:T(8,128)(2,1)}), bf16[8,8,1536]{2,1,0:T(8,128)(2,1)S(1)}, u32[]{:S(2)}, u32[]{:S(2)}) async-start(bf16[8,8,1536]{2,1,0:T(8,128)(2,1)} %broadcast_in_dim.8), calls=%async_computation | async-start | bytes 393216 | tf_op jit(solution)/shard_map/all_to_all | solution.py:39
  31.3 3.0 %copy-start.5 = (s32[6,3]{0,1:T(4,128)S(1)}, s32[6,3]{0,1:T(4,128)}, u32[]{:S(2)}) copy-start(s32[6,3]{0,1:T(4,128)} %param.12) | copy-start | bytes 220
  31.4 11.9 %collective-permute-start = (bf16[384,768]{1,0:T(8,128)(2,1)S(1)}, bf16[384,768]{1,0:T(8,128)(2,1)S(1)}, u32[]{:S(2)}, u32[]{:S(2)}) collective-permute-start(bf16[384,768]{1,0:T(8,128)(2,1)S(1)} %get-tuple-element.14.own_ref), channel_id=1, source_target_pairs={{0,16},{16,0},{32,48},{48,32},{64,80},{80,64},{96,112},{112,96},{1... | collective-permute-start | bytes 1769480 | tf_op jit(solution)/shard_map/ppermute | solution.py:129
  36.1 8.1 %collective-permute-start.1 = (bf16[768,384]{1,0:T(8,128)(2,1)S(1)}, bf16[768,384]{1,0:T(8,128)(2,1)}, u32[]{:S(2)}, u32[]{:S(2)}) collective-permute-start(bf16[768,384]{1,0:T(8,128)(2,1)S(1)} %mul.62.own_ref), channel_id=1, source_target_pairs={{0,16},{16,0},{32,48},{48,32},{64,80},{80,64},{96,112},{112,96},{1... | collective-permute-start | bytes 1769480 | tf_op jit(solution)/shard_map/ppermute | solution.py:129
  38.8 4.5 %collective-permute-start.2 = (bf16[16,384]{1,0:T(8,128)(2,1)S(1)}, bf16[16,384]{1,0:T(8,128)(2,1)S(1)}, u32[]{:S(2)}, u32[]{:S(2)}) collective-permute-start(bf16[16,384]{1,0:T(8,128)(2,1)S(1)} %get-tuple-element.30), channel_id=1, source_target_pairs={{0,16},{16,0},{32,48},{48,32},{64,80},{80,64},{96,112},{112,96},{1... | collective-permute-start | bytes 36872 | tf_op jit(solution)/shard_map/ppermute | solution.py:129
  43.3 0.8 copy-start
  58.5 20.6 %copy-start.1 = (bf16[384,768]{1,0:T(8,128)(2,1)S(1)}, bf16[384,768]{1,0:T(8,128)(2,1)}, u32[]{:S(2)}) copy-start(bf16[384,768]{1,0:T(8,128)(2,1)} %copy-done) | copy-start | bytes 1769476
  108.2 13.7 %all-to-all-start.4 = ((bf16[4,64,768]{2,1,0:T(8,128)(2,1)}), bf16[4,64,768]{2,1,0:T(8,128)(2,1)S(1)}, u32[]{:S(2)}, u32[]{:S(2)}) async-start(bf16[4,64,768]{2,1,0:T(8,128)(2,1)} %bitcast.10), calls=%async_computation.4 | async-start | bytes 786432 | tf_op jit(solution)/shard_map/all_to_all | solution.py:39
  111.7 8.8 %copy-start.2 = (bf16[2,4,8,8,384]{4,3,2,1,0:T(8,128)(2,1)S(1)}, bf16[2,4,8,8,384]{4,3,2,1,0:T(8,128)(2,1)}, u32[]{:S(2)}) copy-start(bf16[2,4,8,8,384]{4,3,2,1,0:T(8,128)(2,1)} %copy.17) | copy-start | bytes 1179652
  111.7 8.9 %collective-permute-start.4 = (bf16[256,768]{1,0:T(8,128)(2,1)S(1)}, bf16[256,768]{1,0:T(8,128)(2,1)S(1)}, u32[]{:S(2)}, u32[]{:S(2)}) collective-permute-start(bf16[256,768]{1,0:T(8,128)(2,1)S(1)} %bitcast.40), channel_id=1, source_target_pairs={{0,16},{16,0},{32,48},{48,32},{64,80},{80,64},{96,112},{112,96},{1... | collective-permute-start | bytes 1179656 | tf_op jit(solution)/shard_map/ppermute | solution.py:129
  118.6 3.3 %collective-permute-start.3 = (bf16[256,384]{1,0:T(8,128)(2,1)S(1)}, bf16[256,384]{1,0:T(8,128)(2,1)S(1)}, u32[]{:S(2)}, u32[]{:S(2)}) collective-permute-start(bf16[256,384]{1,0:T(8,128)(2,1)S(1)} %get-tuple-element.26), channel_id=1, source_target_pairs={{0,16},{16,0},{32,48},{48,32},{64,80},{80,64},{96,112},{112,96},{1... | collective-permute-start | bytes 589832 | tf_op jit(solution)/shard_map/ppermute | solution.py:129
  122.6 33.1 %all-to-all-start.5 = ((bf16[8,8,768]{2,1,0:T(8,128)(2,1)}), bf16[8,8,768]{2,1,0:T(8,128)(2,1)S(1)}, u32[]{:S(2)}, u32[]{:S(2)}) async-start(bf16[8,8,768]{2,1,0:T(8,128)(2,1)} %bitcast.13), calls=%async_computation.5 | async-start | bytes 196608 | tf_op jit(solution)/shard_map/all_to_all | solution.py:39
  127.4 11.7 %collective-permute-start.5 = (bf16[64,768]{1,0:T(8,128)(2,1)S(1)}, bf16[64,768]{1,0:T(8,128)(2,1)S(1)}, u32[]{:S(2)}, u32[]{:S(2)}) collective-permute-start(bf16[64,768]{1,0:T(8,128)(2,1)S(1)} %get-tuple-element.31.refs_0_), channel_id=1, source_target_pairs={{0,32},{16,48},{32,64},{48,80},{64,96},{80,112},{96,128},{112,144}... | collective-permute-start | bytes 294920 | tf_op jit(solution)/shard_map/ppermute | solution.py:166
  131.0 8.8 %collective-permute-start.6 = (bf16[64,768]{1,0:T(8,128)(2,1)S(1)}, bf16[64,768]{1,0:T(8,128)(2,1)S(1)}, u32[]{:S(2)}, u32[]{:S(2)}) collective-permute-start(bf16[64,768]{1,0:T(8,128)(2,1)S(1)} %get-tuple-element.31.refs_0_), channel_id=1, source_target_pairs={{0,992},{16,1008},{32,0},{48,16},{64,32},{80,48},{96,64},{112,80},... | collective-permute-start | bytes 294920 | tf_op jit(solution)/shard_map/ppermute | solution.py:166
  137.1 12.3 %collective-permute-start.7 = (bf16[64,768]{1,0:T(8,128)(2,1)S(1)}, bf16[64,768]{1,0:T(8,128)(2,1)S(1)}, u32[]{:S(2)}, u32[]{:S(2)}) collective-permute-start(bf16[64,768]{1,0:T(8,128)(2,1)S(1)} %get-tuple-element.31.refs_0_), channel_id=1, source_target_pairs={{0,64},{16,80},{32,96},{48,112},{64,128},{80,144},{96,160},{112,17... | collective-permute-start | bytes 294920 | tf_op jit(solution)/shard_map/ppermute | solution.py:166
  150.0 4.3 %collective-permute-start.8 = (bf16[256,768]{1,0:T(8,128)(2,1)S(1)}, bf16[256,768]{1,0:T(8,128)(2,1)S(1)}, u32[]{:S(2)}, u32[]{:S(2)}) collective-permute-start(bf16[256,768]{1,0:T(8,128)(2,1)S(1)} %shard_map.100.refs_0_), channel_id=1, source_target_pairs={{0,16},{16,0},{32,48},{48,32},{64,80},{80,64},{96,112},{112,96},{1... | collective-permute-start | bytes 1179656 | tf_op jit(solution)/shard_map/ppermute | solution.py:129

commit v9 on v8

--- a/solution.py
+++ b/solution.py
@@ -146,14 +146,14 @@
     act = value.astype(jnp.bfloat16).reshape(placed.shape)
     act = act.transpose(2, 1, 0, 3, 4).reshape(2, half, width)
 
-    both = jnp.concatenate([out_grad, inputs], axis=1)
-    rows = swap(jnp.broadcast_to(both[None], (far, own, 2 * features)), "hid", far_groups)
+    which = lax.broadcasted_iota(jnp.int32, (far, 2, own, features), 1)
+    rows = swap(jnp.where(which == 0, out_grad, inputs), "hid", far_groups)
     rows, w_out_got, w_in_got, slope, w_in_eff, w_out_eff, act = lax.optimization_barrier(
         (rows, w_out_got, w_in_got, slope, w_in_eff, w_out_eff, act)
     )
-    rows = rows.reshape(far * own, 2 * features)
-    in_block = rows[:, features:]
-    rows = jnp.broadcast_to(rows[None, :, :features], (NEAR, far * own, features))
+    in_block = rows[:, 1].reshape(far * own, features)
+    rows = rows[:, 0].reshape(1, far * own, features)
+    rows = jnp.broadcast_to(rows, (NEAR, far * own, features))
     rows = swap(rows, "hid", near_groups).reshape(half, features)
 
     n = lax.axis_index("hid") // 2 % NEAR
@@ -185,14 +185,21 @@
     )
     delta = swap(copies, "row").reshape(half, 2 * width)
 
-    back = local(
+    block = 2 * BLOCK
+    back = pl.pallas_call(
         in_grad_body,
-        struct((half, features), jnp.bfloat16),
-        4 * half * features * width,
-        delta,
-        w_in_eff,
-        w_in_got,
-    )
+        out_shape=struct((half, features), jnp.bfloat16),
+        grid=(features // block,),
+        in_specs=[pl.BlockSpec((half, 2 * width), lambda i: (0, 0))]
+        + [pl.BlockSpec((block, width), lambda i: (i, 0))] * 2,
+        out_specs=pl.BlockSpec((half, block), lambda i: (0, i)),
+        compiler_params=pltpu.CompilerParams(vmem_limit_bytes=24 * 2**20),
+        cost_estimate=pl.CostEstimate(
+            flops=4 * half * features * width,
+            bytes_accessed=8 * half * features,
+            transcendentals=0,
+        ),
+    )(delta, w_in_eff, w_in_got)
     back = swap(back.reshape(NEAR, far * own, features), "hid", near_groups)
     scale = 1.0 / math.sqrt(tokens)
     delta_got = partner(delta[:, width:])

time: 157 us -> 158 us (level)
    pallas_call x0 -> x1, Pallas kernels: none -> 3.18 us  [shards(): pl.pallas_call(in_grad_body, out_shape=struct((half, features), jnp.bfloa...]
    pallas_call x7 -> x6, Pallas kernels: 7.07 us -> 4.68 us  [local(): pl.pallas_call(body, out_shape=out_shape, in_specs=[pl.BlockSpec(memory_s...]
where the time goes in v9:
time: 158 us; the launch traced here: 157 us
  starting transfers between devices  67.8 us (43%)
  blocking collectives  46.6 us (29%)
  waiting for transfers between devices  26 us (16%)
  Pallas kernels  8.43 us (5%)
  other arithmetic  4.2 us (3%)
  local copies, waits for them, and re-layouts  3.23 us (2%)
    all_to_all x3, blocking collectives, swap(): return lax.all_to_all(x, axis, 0, 0, axis_index_groups=within, tiled=True)  46.6 us
    all_to_all x3, starting transfers between devices, swap(): return lax.all_to_all(x, axis, 0, 0, axis_index_groups=within, tiled=True)  37.3 us
    ppermute x6, starting transfers between devices, partner(): return lax.ppermute(x, 'hid', [(i, i ^ 1) for i in range(n_hid)])  18.9 us
    all_to_all x3, waiting for transfers between devices, swap(): return lax.all_to_all(x, axis, 0, 0, axis_index_groups=within, tiled=True)  14.4 us
    ppermute x3, starting transfers between devices, shifted(): return lax.ppermute(in_block, 'hid', pairs)  11.6 us
    ppermute x3, waiting for transfers between devices, shifted(): return lax.ppermute(in_block, 'hid', pairs)  10.3 us
    pallas_call x6, Pallas kernels, local(): pl.pallas_call(body, out_shape=out_shape, in_specs=[pl.BlockSpec(memory_s...  4.68 us
    pallas_call x1, Pallas kernels, shards(): pl.pallas_call(in_grad_body, out_shape=struct((half, features), jnp.bfloa...  3.18 us
  transfers between devices with their start and end apart: 12, of which 4 were waited for; matrix products, arithmetic and copies ran while one was open for 3% of the time, Pallas kernels for 2%

profile of v9, /device:TPU:1, one launch (start us, length us, event | category | flops | bytes accessed | tf_op | source)
XLA Modules:
  0.0 157.2 jit_solution(9013561546427620102)
XLA Ops:
  0.7 1.5 broadcast_select_fusion
  2.1 29.0 %all-to-all-start = ((bf16[8,2,8,768]{3,2,1,0:T(8,128)(2,1)}), bf16[8,2,8,768]{3,2,1,0:T(8,128)(2,1)S(1)}, u32[]{:S(2)}, u32[]{:S(2)}) async-start(bf16[8,2,8,768]{3,2,1,0:T(8,128)(2,1)} %broadcast_select_fusion), calls=%async_computation | async-start | bytes 393216 | tf_op jit(solution)/shard_map/all_to_all | solution.py:39
  31.5 2.9 %collective-permute-start = (bf16[384,768]{1,0:T(8,128)(2,1)S(1)}, bf16[384,768]{1,0:T(8,128)(2,1)S(1)}, u32[]{:S(2)}, u32[]{:S(2)}) collective-permute-start(bf16[384,768]{1,0:T(8,128)(2,1)S(1)} %get-tuple-element.14.own_ref), channel_id=1, source_target_pairs={{0,16},{16,0},{32,48},{48,32},{64,80},{80,64},{96,112},{112,96},{1... | collective-permute-start | bytes 1769480 | tf_op jit(solution)/shard_map/ppermute | solution.py:129
  34.9 1.2 mul.62.own_ref
  36.2 1.9 %collective-permute-start.1 = (bf16[768,384]{1,0:T(8,128)(2,1)S(1)}, bf16[768,384]{1,0:T(8,128)(2,1)}, u32[]{:S(2)}, u32[]{:S(2)}) collective-permute-start(bf16[768,384]{1,0:T(8,128)(2,1)S(1)} %mul.62.own_ref), channel_id=1, source_target_pairs={{0,16},{16,0},{32,48},{48,32},{64,80},{80,64},{96,112},{112,96},{1... | collective-permute-start | bytes 1769480 | tf_op jit(solution)/shard_map/ppermute | solution.py:129
  38.9 2.4 %collective-permute-start.2 = (bf16[16,384]{1,0:T(8,128)(2,1)S(1)}, bf16[16,384]{1,0:T(8,128)(2,1)S(1)}, u32[]{:S(2)}, u32[]{:S(2)}) collective-permute-start(bf16[16,384]{1,0:T(8,128)(2,1)S(1)} %get-tuple-element.30), channel_id=1, source_target_pairs={{0,16},{16,0},{32,48},{48,32},{64,80},{80,64},{96,112},{112,96},{1... | collective-permute-start | bytes 36872 | tf_op jit(solution)/shard_map/ppermute | solution.py:129
  41.3 1.3 fusion.5
  44.2 14.4 %all-to-all-done = bf16[8,2,8,768]{3,2,1,0:T(8,128)(2,1)S(1)} async-done(((bf16[8,2,8,768]{3,2,1,0:T(8,128)(2,1)}), bf16[8,2,8,768]{3,2,1,0:T(8,128)(2,1)S(1)}, u32[]{:S(2)}, u32[]{:S(2)}) %all-to-all-start) | async-done | bytes 196640 | tf_op jit(solution)/shard_map/all_to_all | solution.py:39
  58.7 20.6 %all_to_all.30 = bf16[4,64,768]{2,1,0:T(8,128)(2,1)S(1)} all-to-all(bf16[4,64,768]{2,1,0:T(8,128)(2,1)S(1)} %broadcast_in_dim.32), channel_id=1, replica_groups={{0,32,64,96},{16,48,80,112},{128,160,192,224},{144,176,208,240},{256,28..., dimensions={0} | all-to-all | bytes 786432 | tf_op jit(solution)/shard_map/all_to_all | solution.py:39
  79.8 14.6 %all_to_all.31.parts_ref = bf16[16,16,768]{2,1,0:T(8,128)(2,1)S(1)} all-to-all(bf16[16,16,768]{2,1,0:T(8,128)(2,1)S(1)} %bitcast.47), channel_id=1, replica_groups=mesh['hid'=64,'row'=16] {'row'}, dimensions={0} | all-to-all | bytes 786432 | tf_op jit(solution)/shard_map/all_to_all | solution.py:39
  94.4 11.5 %all_to_all.32 = bf16[16,16,768]{2,1,0:T(8,128)(2,1)S(1)} all-to-all(bf16[16,16,768]{2,1,0:T(8,128)(2,1)S(1)} %shard_map.95), channel_id=1, replica_groups=mesh['hid'=64,'row'=16] {'row'}, dimensions={0} | all-to-all | bytes 786432 | tf_op jit(solution)/shard_map/all_to_all | solution.py:39
  105.9 3.2 %shard_map.96 = bf16[256,768]{1,0:T(8,128)(2,1)} custom-call(bf16[256,768]{1,0:T(8,128)(2,1)S(1)} %bitcast.45, bf16[768,384]{1,0:T(8,128)(2,1)S(1)} %mul.62.own_ref, bf16[768,384]{1,0:T(8,128)(2,1)} %collective-permute-done.1.got_ref), custom_call_target="tpu_custom_call" | custom-call | flops 301989888 | bytes 1572864 | tf_op jit(solution)/shard_map/pallas_call | solution.py:189
  109.1 3.5 %all-to-all-start.4 = ((bf16[4,64,768]{2,1,0:T(8,128)(2,1)}), bf16[4,64,768]{2,1,0:T(8,128)(2,1)S(1)}, u32[]{:S(2)}, u32[]{:S(2)}) async-start(bf16[4,64,768]{2,1,0:T(8,128)(2,1)} %bitcast.10), calls=%async_computation.4 | async-start | bytes 786432 | tf_op jit(solution)/shard_map/all_to_all | solution.py:39
  112.6 6.8 %collective-permute-start.4 = (bf16[256,768]{1,0:T(8,128)(2,1)S(1)}, bf16[256,768]{1,0:T(8,128)(2,1)S(1)}, u32[]{:S(2)}, u32[]{:S(2)}) collective-permute-start(bf16[256,768]{1,0:T(8,128)(2,1)S(1)} %bitcast.43), channel_id=1, source_target_pairs={{0,16},{16,0},{32,48},{48,32},{64,80},{80,64},{96,112},{112,96},{1... | collective-permute-start | bytes 1179656 | tf_op jit(solution)/shard_map/ppermute | solution.py:129
  119.5 1.9 %collective-permute-start.3 = (bf16[256,384]{1,0:T(8,128)(2,1)S(1)}, bf16[256,384]{1,0:T(8,128)(2,1)S(1)}, u32[]{:S(2)}, u32[]{:S(2)}) collective-permute-start(bf16[256,384]{1,0:T(8,128)(2,1)S(1)} %get-tuple-element.26), channel_id=1, source_target_pairs={{0,16},{16,0},{32,48},{48,32},{64,80},{80,64},{96,112},{112,96},{1... | collective-permute-start | bytes 589832 | tf_op jit(solution)/shard_map/ppermute | solution.py:129
  121.5 1.3 shard_map.97
  123.5 4.8 %all-to-all-start.5 = ((bf16[8,8,768]{2,1,0:T(8,128)(2,1)}), bf16[8,8,768]{2,1,0:T(8,128)(2,1)S(1)}, u32[]{:S(2)}, u32[]{:S(2)}) async-start(bf16[8,8,768]{2,1,0:T(8,128)(2,1)} %bitcast.13), calls=%async_computation.5 | async-start | bytes 196608 | tf_op jit(solution)/shard_map/all_to_all | solution.py:39
  128.3 3.6 %collective-permute-start.5 = (bf16[64,768]{1,0:T(8,128)(2,1)S(1)}, bf16[64,768]{1,0:T(8,128)(2,1)S(1)}, u32[]{:S(2)}, u32[]{:S(2)}) collective-permute-start(bf16[64,768]{1,0:T(8,128)(2,1)S(1)} %get-tuple-element.31.refs_0_), channel_id=1, source_target_pairs={{0,32},{16,48},{32,64},{48,80},{64,96},{80,112},{96,128},{112,144}... | collective-permute-start | bytes 294920 | tf_op jit(solution)/shard_map/ppermute | solution.py:166
  131.9 6.1 %collective-permute-start.6 = (bf16[64,768]{1,0:T(8,128)(2,1)S(1)}, bf16[64,768]{1,0:T(8,128)(2,1)S(1)}, u32[]{:S(2)}, u32[]{:S(2)}) collective-permute-start(bf16[64,768]{1,0:T(8,128)(2,1)S(1)} %get-tuple-element.31.refs_0_), channel_id=1, source_target_pairs={{0,992},{16,1008},{32,0},{48,16},{64,32},{80,48},{96,64},{112,80},... | collective-permute-start | bytes 294920 | tf_op jit(solution)/shard_map/ppermute | solution.py:166
  138.0 1.9 %collective-permute-start.7 = (bf16[64,768]{1,0:T(8,128)(2,1)S(1)}, bf16[64,768]{1,0:T(8,128)(2,1)S(1)}, u32[]{:S(2)}, u32[]{:S(2)}) collective-permute-start(bf16[64,768]{1,0:T(8,128)(2,1)S(1)} %get-tuple-element.31.refs_0_), channel_id=1, source_target_pairs={{0,64},{16,80},{32,96},{48,112},{64,128},{80,144},{96,160},{112,17... | collective-permute-start | bytes 294920 | tf_op jit(solution)/shard_map/ppermute | solution.py:166
  140.7 9.7 %collective-permute-done.7.refs_3_ = bf16[64,768]{1,0:T(8,128)(2,1)S(1)} collective-permute-done((bf16[64,768]{1,0:T(8,128)(2,1)S(1)}, bf16[64,768]{1,0:T(8,128)(2,1)S(1)}, u32[]{:S(2)}, u32[]{:S(2)}) %collective-permute-start.7) | collective-permute-done | bytes 98336 | tf_op jit(solution)/shard_map/ppermute | solution.py:166
  150.9 2.9 %collective-permute-start.8 = (bf16[256,768]{1,0:T(8,128)(2,1)S(1)}, bf16[256,768]{1,0:T(8,128)(2,1)S(1)}, u32[]{:S(2)}, u32[]{:S(2)}) collective-permute-start(bf16[256,768]{1,0:T(8,128)(2,1)S(1)} %shard_map.100.refs_0_), channel_id=1, source_target_pairs={{0,16},{16,0},{32,48},{48,32},{64,80},{80,64},{96,112},{112,96},{1... | collective-permute-start | bytes 1179656 | tf_op jit(solution)/shard_map/ppermute | solution.py:129
  153.9 1.3 collective-permute-done.8.refs_1_
  155.2 1.4 shard_map.101
  (42 shorter events, 6.6 us)
Async XLA Ops:
  0.6 30.5 %copy-start.4 = (s32[3,6]{1,0:T(4,128)S(1)}, s32[3,6]{1,0:T(4,128)}, u32[]{:S(2)}) copy-start(s32[3,6]{1,0:T(4,128)} %param.13) | copy-start | bytes 220
  2.1 29.2 %copy-start.3 = (bf16[384,768]{1,0:T(8,128)(2,1)S(1)}, bf16[384,768]{1,0:T(8,128)(2,1)}, u32[]{:S(2)}) copy-start(bf16[384,768]{1,0:T(8,128)(2,1)} %param.11) | copy-start | bytes 1769476
  2.1 56.5 %all-to-all-start = ((bf16[8,2,8,768]{3,2,1,0:T(8,128)(2,1)}), bf16[8,2,8,768]{3,2,1,0:T(8,128)(2,1)S(1)}, u32[]{:S(2)}, u32[]{:S(2)}) async-start(bf16[8,2,8,768]{3,2,1,0:T(8,128)(2,1)} %broadcast_select_fusion), calls=%async_computation | async-start | bytes 393216 | tf_op jit(solution)/shard_map/all_to_all | solution.py:39
  31.4 3.0 %copy-start.5 = (s32[6,3]{0,1:T(4,128)S(1)}, s32[6,3]{0,1:T(4,128)}, u32[]{:S(2)}) copy-start(s32[6,3]{0,1:T(4,128)} %param.12) | copy-start | bytes 220
  31.5 11.9 %collective-permute-start = (bf16[384,768]{1,0:T(8,128)(2,1)S(1)}, bf16[384,768]{1,0:T(8,128)(2,1)S(1)}, u32[]{:S(2)}, u32[]{:S(2)}) collective-permute-start(bf16[384,768]{1,0:T(8,128)(2,1)S(1)} %get-tuple-element.14.own_ref), channel_id=1, source_target_pairs={{0,16},{16,0},{32,48},{48,32},{64,80},{80,64},{96,112},{112,96},{1... | collective-permute-start | bytes 1769480 | tf_op jit(solution)/shard_map/ppermute | solution.py:129
  36.2 8.1 %collective-permute-start.1 = (bf16[768,384]{1,0:T(8,128)(2,1)S(1)}, bf16[768,384]{1,0:T(8,128)(2,1)}, u32[]{:S(2)}, u32[]{:S(2)}) collective-permute-start(bf16[768,384]{1,0:T(8,128)(2,1)S(1)} %mul.62.own_ref), channel_id=1, source_target_pairs={{0,16},{16,0},{32,48},{48,32},{64,80},{80,64},{96,112},{112,96},{1... | collective-permute-start | bytes 1769480 | tf_op jit(solution)/shard_map/ppermute | solution.py:129
  38.9 4.5 %collective-permute-start.2 = (bf16[16,384]{1,0:T(8,128)(2,1)S(1)}, bf16[16,384]{1,0:T(8,128)(2,1)S(1)}, u32[]{:S(2)}, u32[]{:S(2)}) collective-permute-start(bf16[16,384]{1,0:T(8,128)(2,1)S(1)} %get-tuple-element.30), channel_id=1, source_target_pairs={{0,16},{16,0},{32,48},{48,32},{64,80},{80,64},{96,112},{112,96},{1... | collective-permute-start | bytes 36872 | tf_op jit(solution)/shard_map/ppermute | solution.py:129
  43.4 0.8 copy-start
  58.6 20.6 %copy-start.1 = (bf16[384,768]{1,0:T(8,128)(2,1)S(1)}, bf16[384,768]{1,0:T(8,128)(2,1)}, u32[]{:S(2)}) copy-start(bf16[384,768]{1,0:T(8,128)(2,1)} %copy-done) | copy-start | bytes 1769476
  109.1 13.7 %all-to-all-start.4 = ((bf16[4,64,768]{2,1,0:T(8,128)(2,1)}), bf16[4,64,768]{2,1,0:T(8,128)(2,1)S(1)}, u32[]{:S(2)}, u32[]{:S(2)}) async-start(bf16[4,64,768]{2,1,0:T(8,128)(2,1)} %bitcast.10), calls=%async_computation.4 | async-start | bytes 786432 | tf_op jit(solution)/shard_map/all_to_all | solution.py:39
  112.6 8.8 %copy-start.2 = (bf16[2,4,8,8,384]{4,3,2,1,0:T(8,128)(2,1)S(1)}, bf16[2,4,8,8,384]{4,3,2,1,0:T(8,128)(2,1)}, u32[]{:S(2)}) copy-start(bf16[2,4,8,8,384]{4,3,2,1,0:T(8,128)(2,1)} %copy.22) | copy-start | bytes 1179652
  112.6 8.9 %collective-permute-start.4 = (bf16[256,768]{1,0:T(8,128)(2,1)S(1)}, bf16[256,768]{1,0:T(8,128)(2,1)S(1)}, u32[]{:S(2)}, u32[]{:S(2)}) collective-permute-start(bf16[256,768]{1,0:T(8,128)(2,1)S(1)} %bitcast.43), channel_id=1, source_target_pairs={{0,16},{16,0},{32,48},{48,32},{64,80},{80,64},{96,112},{112,96},{1... | collective-permute-start | bytes 1179656 | tf_op jit(solution)/shard_map/ppermute | solution.py:129
  119.5 3.3 %collective-permute-start.3 = (bf16[256,384]{1,0:T(8,128)(2,1)S(1)}, bf16[256,384]{1,0:T(8,128)(2,1)S(1)}, u32[]{:S(2)}, u32[]{:S(2)}) collective-permute-start(bf16[256,384]{1,0:T(8,128)(2,1)S(1)} %get-tuple-element.26), channel_id=1, source_target_pairs={{0,16},{16,0},{32,48},{48,32},{64,80},{80,64},{96,112},{112,96},{1... | collective-permute-start | bytes 589832 | tf_op jit(solution)/shard_map/ppermute | solution.py:129
  123.5 33.1 %all-to-all-start.5 = ((bf16[8,8,768]{2,1,0:T(8,128)(2,1)}), bf16[8,8,768]{2,1,0:T(8,128)(2,1)S(1)}, u32[]{:S(2)}, u32[]{:S(2)}) async-start(bf16[8,8,768]{2,1,0:T(8,128)(2,1)} %bitcast.13), calls=%async_computation.5 | async-start | bytes 196608 | tf_op jit(solution)/shard_map/all_to_all | solution.py:39
  128.3 11.7 %collective-permute-start.5 = (bf16[64,768]{1,0:T(8,128)(2,1)S(1)}, bf16[64,768]{1,0:T(8,128)(2,1)S(1)}, u32[]{:S(2)}, u32[]{:S(2)}) collective-permute-start(bf16[64,768]{1,0:T(8,128)(2,1)S(1)} %get-tuple-element.31.refs_0_), channel_id=1, source_target_pairs={{0,32},{16,48},{32,64},{48,80},{64,96},{80,112},{96,128},{112,144}... | collective-permute-start | bytes 294920 | tf_op jit(solution)/shard_map/ppermute | solution.py:166
  131.9 8.8 %collective-permute-start.6 = (bf16[64,768]{1,0:T(8,128)(2,1)S(1)}, bf16[64,768]{1,0:T(8,128)(2,1)S(1)}, u32[]{:S(2)}, u32[]{:S(2)}) collective-permute-start(bf16[64,768]{1,0:T(8,128)(2,1)S(1)} %get-tuple-element.31.refs_0_), channel_id=1, source_target_pairs={{0,992},{16,1008},{32,0},{48,16},{64,32},{80,48},{96,64},{112,80},... | collective-permute-start | bytes 294920 | tf_op jit(solution)/shard_map/ppermute | solution.py:166
  138.0 12.3 %collective-permute-start.7 = (bf16[64,768]{1,0:T(8,128)(2,1)S(1)}, bf16[64,768]{1,0:T(8,128)(2,1)S(1)}, u32[]{:S(2)}, u32[]{:S(2)}) collective-permute-start(bf16[64,768]{1,0:T(8,128)(2,1)S(1)} %get-tuple-element.31.refs_0_), channel_id=1, source_target_pairs={{0,64},{16,80},{32,96},{48,112},{64,128},{80,144},{96,160},{112,17... | collective-permute-start | bytes 294920 | tf_op jit(solution)/shard_map/ppermute | solution.py:166
  150.9 4.3 %collective-permute-start.8 = (bf16[256,768]{1,0:T(8,128)(2,1)S(1)}, bf16[256,768]{1,0:T(8,128)(2,1)S(1)}, u32[]{:S(2)}, u32[]{:S(2)}) collective-permute-start(bf16[256,768]{1,0:T(8,128)(2,1)S(1)} %shard_map.100.refs_0_), channel_id=1, source_target_pairs={{0,16},{16,0},{32,48},{48,32},{64,80},{80,64},{96,112},{112,96},{1... | collective-permute-start | bytes 1179656 | tf_op jit(solution)/shard_map/ppermute | solution.py:129

commit v10 on v8

--- a/solution.py
+++ b/solution.py
@@ -161,8 +161,8 @@
     spots = jnp.stack([(n + NEAR - step) % NEAR for step in steps]).astype(jnp.int32)
 
     def shifted(step):
-        step = step - NEAR if step == NEAR - 1 else step
-        pairs = [(i, (i + 2 * step) % n_hid) for i in range(n_hid)]
+        ways = {1: (1, 1), NEAR - 1: (-1, -1), 2: (2, 2 - NEAR)}[step]
+        pairs = [(i, (i + 2 * ways[i % 2]) % n_hid) for i in range(n_hid)]
         return lax.ppermute(in_block, "hid", pairs)
 
     in_blocks = [in_block] + [shifted(step) for step in steps[1:]]

time: 157 us -> 157 us (level)
  waiting for transfers between devices: 26 us -> 20.4 us
  starting transfers between devices: 67.8 us -> 71.8 us
    ppermute x3, waiting for transfers between devices: 10.3 us -> 4.7 us  [shifted(): return lax.ppermute(in_block, 'hid', pairs)]
    ppermute x6, starting transfers between devices: 18.9 us -> 21.5 us  [partner(): return lax.ppermute(x, 'hid', [(i, i ^ 1) for i in range(n_hid)])]
  transfers between devices with their start and end apart: 12 -> 12, of which waited for: 4 -> 3; matrix products, arithmetic and copies ran while one was open for 3% -> 3% of each run, Pallas kernels for 2% -> 2%
where the time goes in v10:
time: 157 us; the launch traced here: 155 us
  starting transfers between devices  71.8 us (46%)
  blocking collectives  46.6 us (30%)
  waiting for transfers between devices  20.4 us (13%)
  Pallas kernels  7.64 us (5%)
  local copies, waits for them, and re-layouts  3.92 us (2%)
  other arithmetic  3.43 us (2%)
    all_to_all x3, blocking collectives, swap(): return lax.all_to_all(x, axis, 0, 0, axis_index_groups=within, tiled=True)  46.6 us
    all_to_all x3, starting transfers between devices, swap(): return lax.all_to_all(x, axis, 0, 0, axis_index_groups=within, tiled=True)  37.3 us
    ppermute x6, starting transfers between devices, partner(): return lax.ppermute(x, 'hid', [(i, i ^ 1) for i in range(n_hid)])  21.5 us
    all_to_all x3, waiting for transfers between devices, swap(): return lax.all_to_all(x, axis, 0, 0, axis_index_groups=within, tiled=True)  14.4 us
    ppermute x3, starting transfers between devices, shifted(): return lax.ppermute(in_block, 'hid', pairs)  13.1 us
    pallas_call x7, Pallas kernels, local(): pl.pallas_call(body, out_shape=out_shape, in_specs=[pl.BlockSpec(memory_s...  7.07 us
    ppermute x3, waiting for transfers between devices, shifted(): return lax.ppermute(in_block, 'hid', pairs)  4.7 us
  transfers between devices with their start and end apart: 12, of which 3 were waited for; matrix products, arithmetic and copies ran while one was open for 3% of the time, Pallas kernels for 2%

profile of v10, /device:TPU:1, one launch (start us, length us, event | category | flops | bytes accessed | tf_op | source)
XLA Modules:
  0.0 154.8 jit_solution(3919404841291886005)
XLA Ops:
  2.1 29.0 %all-to-all-start = ((bf16[8,8,1536]{2,1,0:T(8,128)(2,1)}), bf16[8,8,1536]{2,1,0:T(8,128)(2,1)S(1)}, u32[]{:S(2)}, u32[]{:S(2)}) async-start(bf16[8,8,1536]{2,1,0:T(8,128)(2,1)} %broadcast_in_dim.8), calls=%async_computation | async-start | bytes 393216 | tf_op jit(solution)/shard_map/all_to_all | solution.py:39
  31.4 2.9 %collective-permute-start = (bf16[384,768]{1,0:T(8,128)(2,1)S(1)}, bf16[384,768]{1,0:T(8,128)(2,1)S(1)}, u32[]{:S(2)}, u32[]{:S(2)}) collective-permute-start(bf16[384,768]{1,0:T(8,128)(2,1)S(1)} %get-tuple-element.14.own_ref), channel_id=1, source_target_pairs={{0,16},{16,0},{32,48},{48,32},{64,80},{80,64},{96,112},{112,96},{1... | collective-permute-start | bytes 1769480 | tf_op jit(solution)/shard_map/ppermute | solution.py:129
  34.9 1.2 mul.62.own_ref
  36.1 1.9 %collective-permute-start.1 = (bf16[768,384]{1,0:T(8,128)(2,1)S(1)}, bf16[768,384]{1,0:T(8,128)(2,1)}, u32[]{:S(2)}, u32[]{:S(2)}) collective-permute-start(bf16[768,384]{1,0:T(8,128)(2,1)S(1)} %mul.62.own_ref), channel_id=1, source_target_pairs={{0,16},{16,0},{32,48},{48,32},{64,80},{80,64},{96,112},{112,96},{1... | collective-permute-start | bytes 1769480 | tf_op jit(solution)/shard_map/ppermute | solution.py:129
  38.8 2.4 %collective-permute-start.2 = (bf16[16,384]{1,0:T(8,128)(2,1)S(1)}, bf16[16,384]{1,0:T(8,128)(2,1)S(1)}, u32[]{:S(2)}, u32[]{:S(2)}) collective-permute-start(bf16[16,384]{1,0:T(8,128)(2,1)S(1)} %get-tuple-element.30), channel_id=1, source_target_pairs={{0,16},{16,0},{32,48},{48,32},{64,80},{80,64},{96,112},{112,96},{1... | collective-permute-start | bytes 36872 | tf_op jit(solution)/shard_map/ppermute | solution.py:129
  41.2 1.3 fusion.5
  43.3 0.8 copy-done
  44.1 14.4 %all-to-all-done = bf16[8,8,1536]{2,1,0:T(8,128)(2,1)S(1)} async-done(((bf16[8,8,1536]{2,1,0:T(8,128)(2,1)}), bf16[8,8,1536]{2,1,0:T(8,128)(2,1)S(1)}, u32[]{:S(2)}, u32[]{:S(2)}) %all-to-all-start) | async-done | bytes 196640 | tf_op jit(solution)/shard_map/all_to_all | solution.py:39
  58.6 20.6 %all_to_all.30 = bf16[4,64,768]{2,1,0:T(8,128)(2,1)S(1)} all-to-all(bf16[4,64,768]{2,1,0:T(8,128)(2,1)S(1)} %broadcast_in_dim.11), channel_id=1, replica_groups={{0,32,64,96},{16,48,80,112},{128,160,192,224},{144,176,208,240},{256,28..., dimensions={0} | all-to-all | bytes 786432 | tf_op jit(solution)/shard_map/all_to_all | solution.py:39
  79.7 14.6 %all_to_all.31.parts_ref = bf16[16,16,768]{2,1,0:T(8,128)(2,1)S(1)} all-to-all(bf16[16,16,768]{2,1,0:T(8,128)(2,1)S(1)} %bitcast.44), channel_id=1, replica_groups=mesh['hid'=64,'row'=16] {'row'}, dimensions={0} | all-to-all | bytes 786432 | tf_op jit(solution)/shard_map/all_to_all | solution.py:39
  94.4 11.5 %all_to_all.32 = bf16[16,16,768]{2,1,0:T(8,128)(2,1)S(1)} all-to-all(bf16[16,16,768]{2,1,0:T(8,128)(2,1)S(1)} %shard_map.95), channel_id=1, replica_groups=mesh['hid'=64,'row'=16] {'row'}, dimensions={0} | all-to-all | bytes 786432 | tf_op jit(solution)/shard_map/all_to_all | solution.py:39
  105.8 2.4 %shard_map.96 = bf16[256,768]{1,0:T(8,128)(2,1)} custom-call(bf16[256,768]{1,0:T(8,128)(2,1)S(1)} %bitcast.42, bf16[768,384]{1,0:T(8,128)(2,1)S(1)} %mul.62.own_ref, bf16[768,384]{1,0:T(8,128)(2,1)} %collective-permute-done.1.got_ref), custom_call_target="tpu_custom_call" | custom-call | flops 301989888 | bytes 1966080 | tf_op jit(solution)/shard_map/pallas_call | solution.py:44
  108.2 3.5 %all-to-all-start.4 = ((bf16[4,64,768]{2,1,0:T(8,128)(2,1)}), bf16[4,64,768]{2,1,0:T(8,128)(2,1)S(1)}, u32[]{:S(2)}, u32[]{:S(2)}) async-start(bf16[4,64,768]{2,1,0:T(8,128)(2,1)} %bitcast.10), calls=%async_computation.4 | async-start | bytes 786432 | tf_op jit(solution)/shard_map/all_to_all | solution.py:39
  111.7 6.8 %collective-permute-start.4 = (bf16[256,768]{1,0:T(8,128)(2,1)S(1)}, bf16[256,768]{1,0:T(8,128)(2,1)S(1)}, u32[]{:S(2)}, u32[]{:S(2)}) collective-permute-start(bf16[256,768]{1,0:T(8,128)(2,1)S(1)} %bitcast.40), channel_id=1, source_target_pairs={{0,16},{16,0},{32,48},{48,32},{64,80},{80,64},{96,112},{112,96},{1... | collective-permute-start | bytes 1179656 | tf_op jit(solution)/shard_map/ppermute | solution.py:129
  118.6 1.9 %collective-permute-start.3 = (bf16[256,384]{1,0:T(8,128)(2,1)S(1)}, bf16[256,384]{1,0:T(8,128)(2,1)S(1)}, u32[]{:S(2)}, u32[]{:S(2)}) collective-permute-start(bf16[256,384]{1,0:T(8,128)(2,1)S(1)} %get-tuple-element.26), channel_id=1, source_target_pairs={{0,16},{16,0},{32,48},{48,32},{64,80},{80,64},{96,112},{112,96},{1... | collective-permute-start | bytes 589832 | tf_op jit(solution)/shard_map/ppermute | solution.py:129
  120.6 1.3 shard_map.97
  122.6 4.8 %all-to-all-start.5 = ((bf16[8,8,768]{2,1,0:T(8,128)(2,1)}), bf16[8,8,768]{2,1,0:T(8,128)(2,1)S(1)}, u32[]{:S(2)}, u32[]{:S(2)}) async-start(bf16[8,8,768]{2,1,0:T(8,128)(2,1)} %bitcast.13), calls=%async_computation.5 | async-start | bytes 196608 | tf_op jit(solution)/shard_map/all_to_all | solution.py:39
  127.4 3.6 %collective-permute-start.5 = (bf16[64,768]{1,0:T(8,128)(2,1)S(1)}, bf16[64,768]{1,0:T(8,128)(2,1)S(1)}, u32[]{:S(2)}, u32[]{:S(2)}) collective-permute-start(bf16[64,768]{1,0:T(8,128)(2,1)S(1)} %get-tuple-element.31.refs_0_), channel_id=1, source_target_pairs={{0,32},{16,48},{32,64},{48,80},{64,96},{80,112},{96,128},{112,144}... | collective-permute-start | bytes 294920 | tf_op jit(solution)/shard_map/ppermute | solution.py:166
  131.0 6.1 %collective-permute-start.6 = (bf16[64,768]{1,0:T(8,128)(2,1)S(1)}, bf16[64,768]{1,0:T(8,128)(2,1)S(1)}, u32[]{:S(2)}, u32[]{:S(2)}) collective-permute-start(bf16[64,768]{1,0:T(8,128)(2,1)S(1)} %get-tuple-element.31.refs_0_), channel_id=1, source_target_pairs={{0,992},{16,1008},{32,0},{48,16},{64,32},{80,48},{96,64},{112,80},... | collective-permute-start | bytes 294920 | tf_op jit(solution)/shard_map/ppermute | solution.py:166
  137.1 3.4 %collective-permute-start.7 = (bf16[64,768]{1,0:T(8,128)(2,1)S(1)}, bf16[64,768]{1,0:T(8,128)(2,1)S(1)}, u32[]{:S(2)}, u32[]{:S(2)}) collective-permute-start(bf16[64,768]{1,0:T(8,128)(2,1)S(1)} %get-tuple-element.31.refs_0_), channel_id=1, source_target_pairs={{0,64},{16,976},{32,96},{48,1008},{64,128},{80,16},{96,160},{112,4... | collective-permute-start | bytes 294920 | tf_op jit(solution)/shard_map/ppermute | solution.py:166
  140.6 4.7 %collective-permute-done.7.refs_3_ = bf16[64,768]{1,0:T(8,128)(2,1)S(1)} collective-permute-done((bf16[64,768]{1,0:T(8,128)(2,1)S(1)}, bf16[64,768]{1,0:T(8,128)(2,1)S(1)}, u32[]{:S(2)}, u32[]{:S(2)}) %collective-permute-start.7) | collective-permute-done | bytes 98336 | tf_op jit(solution)/shard_map/ppermute | solution.py:166
  145.9 5.5 %collective-permute-start.8 = (bf16[256,768]{1,0:T(8,128)(2,1)S(1)}, bf16[256,768]{1,0:T(8,128)(2,1)S(1)}, u32[]{:S(2)}, u32[]{:S(2)}) collective-permute-start(bf16[256,768]{1,0:T(8,128)(2,1)S(1)} %shard_map.100.refs_0_), channel_id=1, source_target_pairs={{0,16},{16,0},{32,48},{48,32},{64,80},{80,64},{96,112},{112,96},{1... | collective-permute-start | bytes 1179656 | tf_op jit(solution)/shard_map/ppermute | solution.py:129
  151.4 1.3 collective-permute-done.8.refs_1_
  152.7 1.4 shard_map.101
  (42 shorter events, 6.6 us)
Async XLA Ops:
  1.4 29.7 %copy-start.4 = (s32[3,6]{1,0:T(4,128)S(1)}, s32[3,6]{1,0:T(4,128)}, u32[]{:S(2)}) copy-start(s32[3,6]{1,0:T(4,128)} %param.13) | copy-start | bytes 220
  2.0 29.2 %copy-start.3 = (bf16[384,768]{1,0:T(8,128)(2,1)S(1)}, bf16[384,768]{1,0:T(8,128)(2,1)}, u32[]{:S(2)}) copy-start(bf16[384,768]{1,0:T(8,128)(2,1)} %param.11) | copy-start | bytes 1769476
  2.1 56.5 %all-to-all-start = ((bf16[8,8,1536]{2,1,0:T(8,128)(2,1)}), bf16[8,8,1536]{2,1,0:T(8,128)(2,1)S(1)}, u32[]{:S(2)}, u32[]{:S(2)}) async-start(bf16[8,8,1536]{2,1,0:T(8,128)(2,1)} %broadcast_in_dim.8), calls=%async_computation | async-start | bytes 393216 | tf_op jit(solution)/shard_map/all_to_all | solution.py:39
  31.3 3.0 %copy-start.5 = (s32[6,3]{0,1:T(4,128)S(1)}, s32[6,3]{0,1:T(4,128)}, u32[]{:S(2)}) copy-start(s32[6,3]{0,1:T(4,128)} %param.12) | copy-start | bytes 220
  31.4 11.9 %collective-permute-start = (bf16[384,768]{1,0:T(8,128)(2,1)S(1)}, bf16[384,768]{1,0:T(8,128)(2,1)S(1)}, u32[]{:S(2)}, u32[]{:S(2)}) collective-permute-start(bf16[384,768]{1,0:T(8,128)(2,1)S(1)} %get-tuple-element.14.own_ref), channel_id=1, source_target_pairs={{0,16},{16,0},{32,48},{48,32},{64,80},{80,64},{96,112},{112,96},{1... | collective-permute-start | bytes 1769480 | tf_op jit(solution)/shard_map/ppermute | solution.py:129
  36.1 8.1 %collective-permute-start.1 = (bf16[768,384]{1,0:T(8,128)(2,1)S(1)}, bf16[768,384]{1,0:T(8,128)(2,1)}, u32[]{:S(2)}, u32[]{:S(2)}) collective-permute-start(bf16[768,384]{1,0:T(8,128)(2,1)S(1)} %mul.62.own_ref), channel_id=1, source_target_pairs={{0,16},{16,0},{32,48},{48,32},{64,80},{80,64},{96,112},{112,96},{1... | collective-permute-start | bytes 1769480 | tf_op jit(solution)/shard_map/ppermute | solution.py:129
  38.8 4.5 %collective-permute-start.2 = (bf16[16,384]{1,0:T(8,128)(2,1)S(1)}, bf16[16,384]{1,0:T(8,128)(2,1)S(1)}, u32[]{:S(2)}, u32[]{:S(2)}) collective-permute-start(bf16[16,384]{1,0:T(8,128)(2,1)S(1)} %get-tuple-element.30), channel_id=1, source_target_pairs={{0,16},{16,0},{32,48},{48,32},{64,80},{80,64},{96,112},{112,96},{1... | collective-permute-start | bytes 36872 | tf_op jit(solution)/shard_map/ppermute | solution.py:129
  43.3 0.8 copy-start
  58.5 20.6 %copy-start.1 = (bf16[384,768]{1,0:T(8,128)(2,1)S(1)}, bf16[384,768]{1,0:T(8,128)(2,1)}, u32[]{:S(2)}) copy-start(bf16[384,768]{1,0:T(8,128)(2,1)} %copy-done) | copy-start | bytes 1769476
  108.2 13.7 %all-to-all-start.4 = ((bf16[4,64,768]{2,1,0:T(8,128)(2,1)}), bf16[4,64,768]{2,1,0:T(8,128)(2,1)S(1)}, u32[]{:S(2)}, u32[]{:S(2)}) async-start(bf16[4,64,768]{2,1,0:T(8,128)(2,1)} %bitcast.10), calls=%async_computation.4 | async-start | bytes 786432 | tf_op jit(solution)/shard_map/all_to_all | solution.py:39
  111.7 8.8 %copy-start.2 = (bf16[2,4,8,8,384]{4,3,2,1,0:T(8,128)(2,1)S(1)}, bf16[2,4,8,8,384]{4,3,2,1,0:T(8,128)(2,1)}, u32[]{:S(2)}) copy-start(bf16[2,4,8,8,384]{4,3,2,1,0:T(8,128)(2,1)} %copy.17) | copy-start | bytes 1179652
  111.7 8.9 %collective-permute-start.4 = (bf16[256,768]{1,0:T(8,128)(2,1)S(1)}, bf16[256,768]{1,0:T(8,128)(2,1)S(1)}, u32[]{:S(2)}, u32[]{:S(2)}) collective-permute-start(bf16[256,768]{1,0:T(8,128)(2,1)S(1)} %bitcast.40), channel_id=1, source_target_pairs={{0,16},{16,0},{32,48},{48,32},{64,80},{80,64},{96,112},{112,96},{1... | collective-permute-start | bytes 1179656 | tf_op jit(solution)/shard_map/ppermute | solution.py:129
  118.6 3.3 %collective-permute-start.3 = (bf16[256,384]{1,0:T(8,128)(2,1)S(1)}, bf16[256,384]{1,0:T(8,128)(2,1)S(1)}, u32[]{:S(2)}, u32[]{:S(2)}) collective-permute-start(bf16[256,384]{1,0:T(8,128)(2,1)S(1)} %get-tuple-element.26), channel_id=1, source_target_pairs={{0,16},{16,0},{32,48},{48,32},{64,80},{80,64},{96,112},{112,96},{1... | collective-permute-start | bytes 589832 | tf_op jit(solution)/shard_map/ppermute | solution.py:129
  122.6 31.5 %all-to-all-start.5 = ((bf16[8,8,768]{2,1,0:T(8,128)(2,1)}), bf16[8,8,768]{2,1,0:T(8,128)(2,1)S(1)}, u32[]{:S(2)}, u32[]{:S(2)}) async-start(bf16[8,8,768]{2,1,0:T(8,128)(2,1)} %bitcast.13), calls=%async_computation.5 | async-start | bytes 196608 | tf_op jit(solution)/shard_map/all_to_all | solution.py:39
  127.4 13.2 %collective-permute-start.5 = (bf16[64,768]{1,0:T(8,128)(2,1)S(1)}, bf16[64,768]{1,0:T(8,128)(2,1)S(1)}, u32[]{:S(2)}, u32[]{:S(2)}) collective-permute-start(bf16[64,768]{1,0:T(8,128)(2,1)S(1)} %get-tuple-element.31.refs_0_), channel_id=1, source_target_pairs={{0,32},{16,48},{32,64},{48,80},{64,96},{80,112},{96,128},{112,144}... | collective-permute-start | bytes 294920 | tf_op jit(solution)/shard_map/ppermute | solution.py:166
  131.0 9.6 %collective-permute-start.6 = (bf16[64,768]{1,0:T(8,128)(2,1)S(1)}, bf16[64,768]{1,0:T(8,128)(2,1)S(1)}, u32[]{:S(2)}, u32[]{:S(2)}) collective-permute-start(bf16[64,768]{1,0:T(8,128)(2,1)S(1)} %get-tuple-element.31.refs_0_), channel_id=1, source_target_pairs={{0,992},{16,1008},{32,0},{48,16},{64,32},{80,48},{96,64},{112,80},... | collective-permute-start | bytes 294920 | tf_op jit(solution)/shard_map/ppermute | solution.py:166
  137.1 8.1 %collective-permute-start.7 = (bf16[64,768]{1,0:T(8,128)(2,1)S(1)}, bf16[64,768]{1,0:T(8,128)(2,1)S(1)}, u32[]{:S(2)}, u32[]{:S(2)}) collective-permute-start(bf16[64,768]{1,0:T(8,128)(2,1)S(1)} %get-tuple-element.31.refs_0_), channel_id=1, source_target_pairs={{0,64},{16,976},{32,96},{48,1008},{64,128},{80,16},{96,160},{112,4... | collective-permute-start | bytes 294920 | tf_op jit(solution)/shard_map/ppermute | solution.py:166
  145.9 6.9 %collective-permute-start.8 = (bf16[256,768]{1,0:T(8,128)(2,1)S(1)}, bf16[256,768]{1,0:T(8,128)(2,1)S(1)}, u32[]{:S(2)}, u32[]{:S(2)}) collective-permute-start(bf16[256,768]{1,0:T(8,128)(2,1)S(1)} %shard_map.100.refs_0_), channel_id=1, source_target_pairs={{0,16},{16,0},{32,48},{48,32},{64,80},{80,64},{96,112},{112,96},{1... | collective-permute-start | bytes 1179656 | tf_op jit(solution)/shard_map/ppermute | solution.py:129

commit v11 on v9

--- a/solution.py
+++ b/solution.py
@@ -77,11 +77,14 @@
         out_ref[copy] = delta
 
 
-def in_grad_body(delta_ref, own_ref, got_ref, out_ref):
+def in_grad_body(delta_ref, own_ref, got_hbm, out_ref, got_ref, arrived):
     width = own_ref.shape[1]
+    load = pltpu.make_async_copy(got_hbm, got_ref, arrived)
+    load.start()
     total = lax.dot_general(
         delta_ref[:, :width], own_ref[...], CONTRACT_LAST, preferred_element_type=jnp.float32
     )
+    load.wait()
     total = total + lax.dot_general(
         delta_ref[:, width:], got_ref[...], CONTRACT_LAST, preferred_element_type=jnp.float32
     )
@@ -146,14 +149,14 @@
     act = value.astype(jnp.bfloat16).reshape(placed.shape)
     act = act.transpose(2, 1, 0, 3, 4).reshape(2, half, width)
 
-    which = lax.broadcasted_iota(jnp.int32, (far, 2, own, features), 1)
-    rows = swap(jnp.where(which == 0, out_grad, inputs), "hid", far_groups)
+    both = jnp.concatenate([out_grad, inputs], axis=1)
+    rows = swap(jnp.broadcast_to(both[None], (far, own, 2 * features)), "hid", far_groups)
     rows, w_out_got, w_in_got, slope, w_in_eff, w_out_eff, act = lax.optimization_barrier(
         (rows, w_out_got, w_in_got, slope, w_in_eff, w_out_eff, act)
     )
-    in_block = rows[:, 1].reshape(far * own, features)
-    rows = rows[:, 0].reshape(1, far * own, features)
-    rows = jnp.broadcast_to(rows, (NEAR, far * own, features))
+    rows = rows.reshape(far * own, 2 * features)
+    in_block = rows[:, features:]
+    rows = jnp.broadcast_to(rows[None, :, :features], (NEAR, far * own, features))
     rows = swap(rows, "hid", near_groups).reshape(half, features)
 
     n = lax.axis_index("hid") // 2 % NEAR
@@ -185,14 +188,13 @@
     )
     delta = swap(copies, "row").reshape(half, 2 * width)
 
-    block = 2 * BLOCK
     back = pl.pallas_call(
         in_grad_body,
         out_shape=struct((half, features), jnp.bfloat16),
-        grid=(features // block,),
-        in_specs=[pl.BlockSpec((half, 2 * width), lambda i: (0, 0))]
-        + [pl.BlockSpec((block, width), lambda i: (i, 0))] * 2,
-        out_specs=pl.BlockSpec((half, block), lambda i: (0, i)),
+        in_specs=[pl.BlockSpec(memory_space=pltpu.VMEM)] * 2
+        + [pl.BlockSpec(memory_space=pl.ANY)],
+        out_specs=pl.BlockSpec(memory_space=pltpu.VMEM),
+        scratch_shapes=[pltpu.VMEM((features, width), jnp.bfloat16), pltpu.SemaphoreType.DMA],
         compiler_params=pltpu.CompilerParams(vmem_limit_bytes=24 * 2**20),
         cost_estimate=pl.CostEstimate(
             flops=4 * half * features * width,

time: 158 us -> 157 us (level)
  no operation moved by 1% of the time
where the time goes in v11:
time: 157 us; the launch traced here: 156 us
  starting transfers between devices  67.8 us (43%)
  blocking collectives  46.6 us (30%)
  waiting for transfers between devices  26 us (17%)
  Pallas kernels  7.65 us (5%)
  local copies, waits for them, and re-layouts  3.92 us (2%)
  other arithmetic  3.43 us (2%)
    all_to_all x3, blocking collectives, swap(): return lax.all_to_all(x, axis, 0, 0, axis_index_groups=within, tiled=True)  46.6 us
    all_to_all x3, starting transfers between devices, swap(): return lax.all_to_all(x, axis, 0, 0, axis_index_groups=within, tiled=True)  37.3 us
    ppermute x6, starting transfers between devices, partner(): return lax.ppermute(x, 'hid', [(i, i ^ 1) for i in range(n_hid)])  18.9 us
    all_to_all x3, waiting for transfers between devices, swap(): return lax.all_to_all(x, axis, 0, 0, axis_index_groups=within, tiled=True)  14.4 us
    ppermute x3, starting transfers between devices, shifted(): return lax.ppermute(in_block, 'hid', pairs)  11.6 us
    ppermute x3, waiting for transfers between devices, shifted(): return lax.ppermute(in_block, 'hid', pairs)  10.3 us
    pallas_call x6, Pallas kernels, local(): pl.pallas_call(body, out_shape=out_shape, in_specs=[pl.BlockSpec(memory_s...  4.68 us
  transfers between devices with their start and end apart: 12, of which 4 were waited for; matrix products, arithmetic and copies ran while one was open for 3% of the time, Pallas kernels for 2%

profile of v11, /device:TPU:1, one launch (start us, length us, event | category | flops | bytes accessed | tf_op | source)
XLA Modules:
  0.0 156.4 jit_solution(2271328496487893281)
XLA Ops:
  2.1 29.0 %all-to-all-start = ((bf16[8,8,1536]{2,1,0:T(8,128)(2,1)}), bf16[8,8,1536]{2,1,0:T(8,128)(2,1)S(1)}, u32[]{:S(2)}, u32[]{:S(2)}) async-start(bf16[8,8,1536]{2,1,0:T(8,128)(2,1)} %broadcast_in_dim.8), calls=%async_computation | async-start | bytes 393216 | tf_op jit(solution)/shard_map/all_to_all | solution.py:39
  31.4 2.9 %collective-permute-start = (bf16[384,768]{1,0:T(8,128)(2,1)S(1)}, bf16[384,768]{1,0:T(8,128)(2,1)S(1)}, u32[]{:S(2)}, u32[]{:S(2)}) collective-permute-start(bf16[384,768]{1,0:T(8,128)(2,1)S(1)} %get-tuple-element.14.own_ref), channel_id=1, source_target_pairs={{0,16},{16,0},{32,48},{48,32},{64,80},{80,64},{96,112},{112,96},{1... | collective-permute-start | bytes 1769480 | tf_op jit(solution)/shard_map/ppermute | solution.py:132
  34.9 1.2 mul.62.own_ref
  36.1 1.9 %collective-permute-start.1 = (bf16[768,384]{1,0:T(8,128)(2,1)S(1)}, bf16[768,384]{1,0:T(8,128)(2,1)}, u32[]{:S(2)}, u32[]{:S(2)}) collective-permute-start(bf16[768,384]{1,0:T(8,128)(2,1)S(1)} %mul.62.own_ref), channel_id=1, source_target_pairs={{0,16},{16,0},{32,48},{48,32},{64,80},{80,64},{96,112},{112,96},{1... | collective-permute-start | bytes 1769480 | tf_op jit(solution)/shard_map/ppermute | solution.py:132
  38.8 2.4 %collective-permute-start.2 = (bf16[16,384]{1,0:T(8,128)(2,1)S(1)}, bf16[16,384]{1,0:T(8,128)(2,1)S(1)}, u32[]{:S(2)}, u32[]{:S(2)}) collective-permute-start(bf16[16,384]{1,0:T(8,128)(2,1)S(1)} %get-tuple-element.30), channel_id=1, source_target_pairs={{0,16},{16,0},{32,48},{48,32},{64,80},{80,64},{96,112},{112,96},{1... | collective-permute-start | bytes 36872 | tf_op jit(solution)/shard_map/ppermute | solution.py:132
  41.2 1.3 fusion.5
  43.3 0.8 copy-done
  44.1 14.4 %all-to-all-done = bf16[8,8,1536]{2,1,0:T(8,128)(2,1)S(1)} async-done(((bf16[8,8,1536]{2,1,0:T(8,128)(2,1)}), bf16[8,8,1536]{2,1,0:T(8,128)(2,1)S(1)}, u32[]{:S(2)}, u32[]{:S(2)}) %all-to-all-start) | async-done | bytes 196640 | tf_op jit(solution)/shard_map/all_to_all | solution.py:39
  58.6 20.6 %all_to_all.30 = bf16[4,64,768]{2,1,0:T(8,128)(2,1)S(1)} all-to-all(bf16[4,64,768]{2,1,0:T(8,128)(2,1)S(1)} %broadcast_in_dim.11), channel_id=1, replica_groups={{0,32,64,96},{16,48,80,112},{128,160,192,224},{144,176,208,240},{256,28..., dimensions={0} | all-to-all | bytes 786432 | tf_op jit(solution)/shard_map/all_to_all | solution.py:39
  79.7 14.6 %all_to_all.31.parts_ref = bf16[16,16,768]{2,1,0:T(8,128)(2,1)S(1)} all-to-all(bf16[16,16,768]{2,1,0:T(8,128)(2,1)S(1)} %bitcast.44), channel_id=1, replica_groups=mesh['hid'=64,'row'=16] {'row'}, dimensions={0} | all-to-all | bytes 786432 | tf_op jit(solution)/shard_map/all_to_all | solution.py:39
  94.4 11.5 %all_to_all.32 = bf16[16,16,768]{2,1,0:T(8,128)(2,1)S(1)} all-to-all(bf16[16,16,768]{2,1,0:T(8,128)(2,1)S(1)} %shard_map.95), channel_id=1, replica_groups=mesh['hid'=64,'row'=16] {'row'}, dimensions={0} | all-to-all | bytes 786432 | tf_op jit(solution)/shard_map/all_to_all | solution.py:39
  105.8 2.4 %shard_map.96 = bf16[256,768]{1,0:T(8,128)(2,1)} custom-call(bf16[256,768]{1,0:T(8,128)(2,1)S(1)} %bitcast.42, bf16[768,384]{1,0:T(8,128)(2,1)S(1)} %mul.62.own_ref, bf16[768,384]{1,0:T(8,128)(2,1)} %collective-permute-done.1.got_hbm), custom_call_target="tpu_custom_call" | custom-call | flops 301989888 | bytes 1572864 | tf_op jit(solution)/shard_map/pallas_call | solution.py:191
  108.2 3.5 %all-to-all-start.4 = ((bf16[4,64,768]{2,1,0:T(8,128)(2,1)}), bf16[4,64,768]{2,1,0:T(8,128)(2,1)S(1)}, u32[]{:S(2)}, u32[]{:S(2)}) async-start(bf16[4,64,768]{2,1,0:T(8,128)(2,1)} %bitcast.10), calls=%async_computation.4 | async-start | bytes 786432 | tf_op jit(solution)/shard_map/all_to_all | solution.py:39
  111.7 6.8 %collective-permute-start.4 = (bf16[256,768]{1,0:T(8,128)(2,1)S(1)}, bf16[256,768]{1,0:T(8,128)(2,1)S(1)}, u32[]{:S(2)}, u32[]{:S(2)}) collective-permute-start(bf16[256,768]{1,0:T(8,128)(2,1)S(1)} %bitcast.40), channel_id=1, source_target_pairs={{0,16},{16,0},{32,48},{48,32},{64,80},{80,64},{96,112},{112,96},{1... | collective-permute-start | bytes 1179656 | tf_op jit(solution)/shard_map/ppermute | solution.py:132
  118.6 1.9 %collective-permute-start.3 = (bf16[256,384]{1,0:T(8,128)(2,1)S(1)}, bf16[256,384]{1,0:T(8,128)(2,1)S(1)}, u32[]{:S(2)}, u32[]{:S(2)}) collective-permute-start(bf16[256,384]{1,0:T(8,128)(2,1)S(1)} %get-tuple-element.26), channel_id=1, source_target_pairs={{0,16},{16,0},{32,48},{48,32},{64,80},{80,64},{96,112},{112,96},{1... | collective-permute-start | bytes 589832 | tf_op jit(solution)/shard_map/ppermute | solution.py:132
  120.6 1.3 shard_map.97
  122.7 4.8 %all-to-all-start.5 = ((bf16[8,8,768]{2,1,0:T(8,128)(2,1)}), bf16[8,8,768]{2,1,0:T(8,128)(2,1)S(1)}, u32[]{:S(2)}, u32[]{:S(2)}) async-start(bf16[8,8,768]{2,1,0:T(8,128)(2,1)} %bitcast.13), calls=%async_computation.5 | async-start | bytes 196608 | tf_op jit(solution)/shard_map/all_to_all | solution.py:39
  127.5 3.6 %collective-permute-start.5 = (bf16[64,768]{1,0:T(8,128)(2,1)S(1)}, bf16[64,768]{1,0:T(8,128)(2,1)S(1)}, u32[]{:S(2)}, u32[]{:S(2)}) collective-permute-start(bf16[64,768]{1,0:T(8,128)(2,1)S(1)} %get-tuple-element.31.refs_0_), channel_id=1, source_target_pairs={{0,32},{16,48},{32,64},{48,80},{64,96},{80,112},{96,128},{112,144}... | collective-permute-start | bytes 294920 | tf_op jit(solution)/shard_map/ppermute | solution.py:169
  131.0 6.1 %collective-permute-start.6 = (bf16[64,768]{1,0:T(8,128)(2,1)S(1)}, bf16[64,768]{1,0:T(8,128)(2,1)S(1)}, u32[]{:S(2)}, u32[]{:S(2)}) collective-permute-start(bf16[64,768]{1,0:T(8,128)(2,1)S(1)} %get-tuple-element.31.refs_0_), channel_id=1, source_target_pairs={{0,992},{16,1008},{32,0},{48,16},{64,32},{80,48},{96,64},{112,80},... | collective-permute-start | bytes 294920 | tf_op jit(solution)/shard_map/ppermute | solution.py:169
  137.2 1.9 %collective-permute-start.7 = (bf16[64,768]{1,0:T(8,128)(2,1)S(1)}, bf16[64,768]{1,0:T(8,128)(2,1)S(1)}, u32[]{:S(2)}, u32[]{:S(2)}) collective-permute-start(bf16[64,768]{1,0:T(8,128)(2,1)S(1)} %get-tuple-element.31.refs_0_), channel_id=1, source_target_pairs={{0,64},{16,80},{32,96},{48,112},{64,128},{80,144},{96,160},{112,17... | collective-permute-start | bytes 294920 | tf_op jit(solution)/shard_map/ppermute | solution.py:169
  139.8 9.7 %collective-permute-done.7.refs_3_ = bf16[64,768]{1,0:T(8,128)(2,1)S(1)} collective-permute-done((bf16[64,768]{1,0:T(8,128)(2,1)S(1)}, bf16[64,768]{1,0:T(8,128)(2,1)S(1)}, u32[]{:S(2)}, u32[]{:S(2)}) %collective-permute-start.7) | collective-permute-done | bytes 98336 | tf_op jit(solution)/shard_map/ppermute | solution.py:169
  150.1 2.9 %collective-permute-start.8 = (bf16[256,768]{1,0:T(8,128)(2,1)S(1)}, bf16[256,768]{1,0:T(8,128)(2,1)S(1)}, u32[]{:S(2)}, u32[]{:S(2)}) collective-permute-start(bf16[256,768]{1,0:T(8,128)(2,1)S(1)} %shard_map.100.refs_0_), channel_id=1, source_target_pairs={{0,16},{16,0},{32,48},{48,32},{64,80},{80,64},{96,112},{112,96},{1... | collective-permute-start | bytes 1179656 | tf_op jit(solution)/shard_map/ppermute | solution.py:132
  153.0 1.3 collective-permute-done.8.refs_1_
  154.3 1.4 shard_map.101
  (42 shorter events, 7.2 us)
Async XLA Ops:
  1.4 29.7 %copy-start.4 = (s32[3,6]{1,0:T(4,128)S(1)}, s32[3,6]{1,0:T(4,128)}, u32[]{:S(2)}) copy-start(s32[3,6]{1,0:T(4,128)} %param.13) | copy-start | bytes 220
  2.0 29.2 %copy-start.3 = (bf16[384,768]{1,0:T(8,128)(2,1)S(1)}, bf16[384,768]{1,0:T(8,128)(2,1)}, u32[]{:S(2)}) copy-start(bf16[384,768]{1,0:T(8,128)(2,1)} %param.11) | copy-start | bytes 1769476
  2.1 56.5 %all-to-all-start = ((bf16[8,8,1536]{2,1,0:T(8,128)(2,1)}), bf16[8,8,1536]{2,1,0:T(8,128)(2,1)S(1)}, u32[]{:S(2)}, u32[]{:S(2)}) async-start(bf16[8,8,1536]{2,1,0:T(8,128)(2,1)} %broadcast_in_dim.8), calls=%async_computation | async-start | bytes 393216 | tf_op jit(solution)/shard_map/all_to_all | solution.py:39
  31.3 3.0 %copy-start.5 = (s32[6,3]{0,1:T(4,128)S(1)}, s32[6,3]{0,1:T(4,128)}, u32[]{:S(2)}) copy-start(s32[6,3]{0,1:T(4,128)} %param.12) | copy-start | bytes 220
  31.4 11.9 %collective-permute-start = (bf16[384,768]{1,0:T(8,128)(2,1)S(1)}, bf16[384,768]{1,0:T(8,128)(2,1)S(1)}, u32[]{:S(2)}, u32[]{:S(2)}) collective-permute-start(bf16[384,768]{1,0:T(8,128)(2,1)S(1)} %get-tuple-element.14.own_ref), channel_id=1, source_target_pairs={{0,16},{16,0},{32,48},{48,32},{64,80},{80,64},{96,112},{112,96},{1... | collective-permute-start | bytes 1769480 | tf_op jit(solution)/shard_map/ppermute | solution.py:132
  36.1 8.1 %collective-permute-start.1 = (bf16[768,384]{1,0:T(8,128)(2,1)S(1)}, bf16[768,384]{1,0:T(8,128)(2,1)}, u32[]{:S(2)}, u32[]{:S(2)}) collective-permute-start(bf16[768,384]{1,0:T(8,128)(2,1)S(1)} %mul.62.own_ref), channel_id=1, source_target_pairs={{0,16},{16,0},{32,48},{48,32},{64,80},{80,64},{96,112},{112,96},{1... | collective-permute-start | bytes 1769480 | tf_op jit(solution)/shard_map/ppermute | solution.py:132
  38.8 4.5 %collective-permute-start.2 = (bf16[16,384]{1,0:T(8,128)(2,1)S(1)}, bf16[16,384]{1,0:T(8,128)(2,1)S(1)}, u32[]{:S(2)}, u32[]{:S(2)}) collective-permute-start(bf16[16,384]{1,0:T(8,128)(2,1)S(1)} %get-tuple-element.30), channel_id=1, source_target_pairs={{0,16},{16,0},{32,48},{48,32},{64,80},{80,64},{96,112},{112,96},{1... | collective-permute-start | bytes 36872 | tf_op jit(solution)/shard_map/ppermute | solution.py:132
  43.3 0.8 copy-start
  58.5 20.6 %copy-start.1 = (bf16[384,768]{1,0:T(8,128)(2,1)S(1)}, bf16[384,768]{1,0:T(8,128)(2,1)}, u32[]{:S(2)}) copy-start(bf16[384,768]{1,0:T(8,128)(2,1)} %copy-done) | copy-start | bytes 1769476
  108.2 13.7 %all-to-all-start.4 = ((bf16[4,64,768]{2,1,0:T(8,128)(2,1)}), bf16[4,64,768]{2,1,0:T(8,128)(2,1)S(1)}, u32[]{:S(2)}, u32[]{:S(2)}) async-start(bf16[4,64,768]{2,1,0:T(8,128)(2,1)} %bitcast.10), calls=%async_computation.4 | async-start | bytes 786432 | tf_op jit(solution)/shard_map/all_to_all | solution.py:39
  111.7 8.8 %copy-start.2 = (bf16[2,4,8,8,384]{4,3,2,1,0:T(8,128)(2,1)S(1)}, bf16[2,4,8,8,384]{4,3,2,1,0:T(8,128)(2,1)}, u32[]{:S(2)}) copy-start(bf16[2,4,8,8,384]{4,3,2,1,0:T(8,128)(2,1)} %copy.17) | copy-start | bytes 1179652
  111.7 8.9 %collective-permute-start.4 = (bf16[256,768]{1,0:T(8,128)(2,1)S(1)}, bf16[256,768]{1,0:T(8,128)(2,1)S(1)}, u32[]{:S(2)}, u32[]{:S(2)}) collective-permute-start(bf16[256,768]{1,0:T(8,128)(2,1)S(1)} %bitcast.40), channel_id=1, source_target_pairs={{0,16},{16,0},{32,48},{48,32},{64,80},{80,64},{96,112},{112,96},{1... | collective-permute-start | bytes 1179656 | tf_op jit(solution)/shard_map/ppermute | solution.py:132
  118.6 3.3 %collective-permute-start.3 = (bf16[256,384]{1,0:T(8,128)(2,1)S(1)}, bf16[256,384]{1,0:T(8,128)(2,1)S(1)}, u32[]{:S(2)}, u32[]{:S(2)}) collective-permute-start(bf16[256,384]{1,0:T(8,128)(2,1)S(1)} %get-tuple-element.26), channel_id=1, source_target_pairs={{0,16},{16,0},{32,48},{48,32},{64,80},{80,64},{96,112},{112,96},{1... | collective-permute-start | bytes 589832 | tf_op jit(solution)/shard_map/ppermute | solution.py:132
  122.7 33.1 %all-to-all-start.5 = ((bf16[8,8,768]{2,1,0:T(8,128)(2,1)}), bf16[8,8,768]{2,1,0:T(8,128)(2,1)S(1)}, u32[]{:S(2)}, u32[]{:S(2)}) async-start(bf16[8,8,768]{2,1,0:T(8,128)(2,1)} %bitcast.13), calls=%async_computation.5 | async-start | bytes 196608 | tf_op jit(solution)/shard_map/all_to_all | solution.py:39
  127.5 11.7 %collective-permute-start.5 = (bf16[64,768]{1,0:T(8,128)(2,1)S(1)}, bf16[64,768]{1,0:T(8,128)(2,1)S(1)}, u32[]{:S(2)}, u32[]{:S(2)}) collective-permute-start(bf16[64,768]{1,0:T(8,128)(2,1)S(1)} %get-tuple-element.31.refs_0_), channel_id=1, source_target_pairs={{0,32},{16,48},{32,64},{48,80},{64,96},{80,112},{96,128},{112,144}... | collective-permute-start | bytes 294920 | tf_op jit(solution)/shard_map/ppermute | solution.py:169
  131.0 8.8 %collective-permute-start.6 = (bf16[64,768]{1,0:T(8,128)(2,1)S(1)}, bf16[64,768]{1,0:T(8,128)(2,1)S(1)}, u32[]{:S(2)}, u32[]{:S(2)}) collective-permute-start(bf16[64,768]{1,0:T(8,128)(2,1)S(1)} %get-tuple-element.31.refs_0_), channel_id=1, source_target_pairs={{0,992},{16,1008},{32,0},{48,16},{64,32},{80,48},{96,64},{112,80},... | collective-permute-start | bytes 294920 | tf_op jit(solution)/shard_map/ppermute | solution.py:169
  137.2 12.3 %collective-permute-start.7 = (bf16[64,768]{1,0:T(8,128)(2,1)S(1)}, bf16[64,768]{1,0:T(8,128)(2,1)S(1)}, u32[]{:S(2)}, u32[]{:S(2)}) collective-permute-start(bf16[64,768]{1,0:T(8,128)(2,1)S(1)} %get-tuple-element.31.refs_0_), channel_id=1, source_target_pairs={{0,64},{16,80},{32,96},{48,112},{64,128},{80,144},{96,160},{112,17... | collective-permute-start | bytes 294920 | tf_op jit(solution)/shard_map/ppermute | solution.py:169
  150.1 4.3 %collective-permute-start.8 = (bf16[256,768]{1,0:T(8,128)(2,1)S(1)}, bf16[256,768]{1,0:T(8,128)(2,1)S(1)}, u32[]{:S(2)}, u32[]{:S(2)}) collective-permute-start(bf16[256,768]{1,0:T(8,128)(2,1)S(1)} %shard_map.100.refs_0_), channel_id=1, source_target_pairs={{0,16},{16,0},{32,48},{48,32},{64,80},{80,64},{96,112},{112,96},{1... | collective-permute-start | bytes 1179656 | tf_op jit(solution)/shard_map/ppermute | solution.py:132
